TPU v7x, 512 devices: a whole 4x4x16 slice. The times are simulated.
512 devices in a mesh: dp: 32 (over y, z_lo), head: 16 (over z_hi, x, core).
Axes of the slice: x: 4, y: 4, z: 16 (z_hi: 2, z_lo: 8; z = z_hi * 8 + z_lo), core: 2. Of those that a mesh axis runs over, the one named last changes fastest.
Arguments:
- task_embed: bfloat16 [240, 1024], replicated, may hold values from -6 to 6
- task_ids: int32 [64], P('dp'), may hold values from 0 to 239
- seq_lengths: int32 [64], P('dp'), may hold values from 1 to 320, 12800 in all
- w_in: bfloat16 [1024, 256], replicated, may hold values from -0.1875 to 0.1875
- module_embed: float32 [2, 256], replicated, may hold values from -4 to 4
- wa_q: bfloat16 [256, 8, 4096], P('dp', None, 'head'), may hold values from -0.005859375 to 0.005859375
- wb_q: bfloat16 [256, 8, 4096], P('dp', None, 'head'), may hold values from -0.125 to 0.125
- wa_v: bfloat16 [256, 8, 4096], P('dp', None, 'head'), may hold values from -0.005859375 to 0.005859375
- wb_v: bfloat16 [256, 8, 1024], P('dp', None, 'head'), may hold values from -0.125 to 0.125
- base_q: bfloat16 [4096, 4096], P(None, 'head'), may hold values from -0.09375 to 0.09375
- base_v: bfloat16 [4096, 1024], P(None, 'head'), may hold values from -0.09375 to 0.09375
- hidden_in: bfloat16 [64, 320, 4096], P('dp', None, 'head'), may hold values from -6 to 6
- grad_q: bfloat16 [64, 320, 4096], P('dp', None, 'head'), may hold values from -6 to 6
- grad_v: bfloat16 [64, 320, 1024], P('dp', None, 'head'), may hold values from -6 to 6
Outputs:
- q_out: bfloat16 [64, 320, 4096], P('dp', None, 'head')
- v_out: bfloat16 [64, 320, 1024], P('dp', None, 'head')
- grad_wa_q: float32 [256, 8, 4096], P('dp', None, 'head')
- grad_wb_q: float32 [256, 8, 4096], P('dp', None, 'head')
- grad_wa_v: float32 [256, 8, 4096], P('dp', None, 'head')
- grad_wb_v: float32 [256, 8, 1024], P('dp', None, 'head')
- grad_w_in: float32 [1024, 256], P(None, 'dp')
- grad_module: float32 [2, 256], P(None, 'dp')
Inputs may be any that keep to these rules, and one draw needn't show every extreme that they name: `seq_lengths`: each task batch holds 1 to 320 real tokens followed by padding; some batch is full.
All inputs are finite; a program needn't handle non-finite values. No bound on the sum of `seq_lengths` on one device may be relied on, other than what follows from the above.
Results may differ from a plain program's by a relative error of at most 0.02.
Values may be sent and summed in bfloat16 or wider, within the bound.
No kernel may reach another device: no remote copies, remote signals or barrier semaphores. Data moves between devices by JAX's collectives and lax.ppermute only.
A program may use at most 64 MiB of HBM per device.

v0:
```python
import jax
import jax.numpy as jnp
from jax import lax
from jax.sharding import PartitionSpec as P

adapter_scale_factor = 2.0


def silu_grad(pre):
    sig = jax.nn.sigmoid(pre)
    return sig * (1.0 + pre * (1.0 - sig))


def contract(latent, weights, split):
    first = jnp.einsum(
        "sh,hrc->src", latent[:, 0], weights[:, :, :split], preferred_element_type=jnp.float32
    )
    second = jnp.einsum(
        "sh,hrc->src", latent[:, 1], weights[:, :, split:], preferred_element_type=jnp.float32
    )
    return jnp.concatenate([first, second], axis=2)


def on_device(
    task_embed,
    task_ids,
    seq_lengths,
    w_in,
    module_embed,
    wa_q,
    wb_q,
    wa_v,
    wb_v,
    base_q,
    base_v,
    hidden_in,
    grad_q,
    grad_v,
):
    highest = lax.Precision.HIGHEST
    tasks_all = task_embed.shape[0]
    onehot = (task_ids[:, None] == jnp.arange(tasks_all, dtype=jnp.int32)[None, :]).astype(
        jnp.bfloat16
    )
    embeds = jnp.dot(onehot, task_embed, preferred_element_type=jnp.float32)
    pre = (
        jnp.dot(embeds.astype(jnp.bfloat16), w_in, preferred_element_type=jnp.float32)[:, None, :]
        + module_embed[None, :, :]
    )
    latent = jax.nn.silu(pre).astype(jnp.bfloat16)
    width_q = wa_q.shape[2]
    split = 2 * width_q
    rank = wa_q.shape[1]
    rows_dev = wa_q.shape[0]
    packed = jnp.concatenate([wa_q, wb_q, wa_v, wb_v], axis=2)
    own_start = lax.axis_index("dp") * rows_dev
    adapters = contract(latent, lax.all_gather(packed, "dp", axis=0, tiled=True), split)
    adapters = adapters.astype(jnp.bfloat16)
    a_q = adapters[:, :, :width_q]
    query_up_factor = adapters[:, :, width_q:split]
    a_v = adapters[:, :, split : split + width_q]
    value_up_factor = adapters[:, :, split + width_q :]
    low_part = jnp.concatenate(
        [
            jnp.einsum("std,srd->str", hidden_in, a_q, preferred_element_type=jnp.float32),
            jnp.einsum("std,srd->str", hidden_in, a_v, preferred_element_type=jnp.float32),
        ],
        axis=2,
    )
    low = lax.psum(low_part, "head").astype(jnp.bfloat16)
    query_down_product = low[:, :, :rank]
    value_down_product = low[:, :, rank:]
    seq_len = hidden_in.shape[1]
    piece = lax.all_gather(hidden_in, "head", axis=2, tiled=True)
    base_out_q = jnp.einsum("std,dc->stc", piece, base_q, preferred_element_type=jnp.float32)
    base_out_v = jnp.einsum("std,dc->stc", piece, base_v, preferred_element_type=jnp.float32)
    q_out = (
        base_out_q
        + adapter_scale_factor
        * jnp.einsum(
            "ewn,enm->ewm", query_down_product, query_up_factor, preferred_element_type=jnp.float32
        )
    ).astype(jnp.bfloat16)
    v_out = (
        base_out_v
        + adapter_scale_factor
        * jnp.einsum(
            "ewn,enm->ewm", value_down_product, value_up_factor, preferred_element_type=jnp.float32
        )
    ).astype(jnp.bfloat16)
    positions = jnp.arange(seq_len, dtype=jnp.int32)
    weight = (positions[None, :] < seq_lengths[:, None]).astype(jnp.float32) / seq_lengths.astype(
        jnp.float32
    )[:, None]
    query_output_gradient = (grad_q.astype(jnp.float32) * weight[:, :, None]).astype(jnp.bfloat16)
    value_output_gradient = (grad_v.astype(jnp.float32) * weight[:, :, None]).astype(jnp.bfloat16)
    query_up_gradient = adapter_scale_factor * jnp.einsum(
        "qzy,qzf->qyf",
        query_down_product,
        query_output_gradient,
        preferred_element_type=jnp.float32,
    )
    value_up_gradient = adapter_scale_factor * jnp.einsum(
        "qzy,qzf->qyf",
        value_down_product,
        value_output_gradient,
        preferred_element_type=jnp.float32,
    )
    back_part = jnp.concatenate(
        [
            adapter_scale_factor
            * jnp.einsum(
                "zag,zkg->zak",
                query_output_gradient,
                query_up_factor,
                preferred_element_type=jnp.float32,
            ),
            adapter_scale_factor
            * jnp.einsum(
                "zag,zkg->zak",
                value_output_gradient,
                value_up_factor,
                preferred_element_type=jnp.float32,
            ),
        ],
        axis=2,
    )
    back = lax.psum(back_part, "head").astype(jnp.bfloat16)
    d_aq = jnp.einsum(
        "str,std->srd", back[:, :, :rank], hidden_in, preferred_element_type=jnp.float32
    )
    d_av = jnp.einsum(
        "str,std->srd", back[:, :, rank:], hidden_in, preferred_element_type=jnp.float32
    )
    d_adapters = jnp.concatenate([d_aq, query_up_gradient, d_av, value_up_gradient], axis=2)
    weights32 = packed.astype(jnp.float32)
    d_piece = lax.all_gather(d_adapters, "dp", axis=0, tiled=True)
    pre_piece = lax.all_gather(pre, "dp", axis=0, tiled=True)
    emb_piece = lax.all_gather(embeds, "dp", axis=0, tiled=True)
    pre_own = lax.dynamic_slice_in_dim(pre_piece, own_start, rows_dev, 2)
    lat_own = lax.optimization_barrier(jax.nn.silu(pre_own).astype(jnp.bfloat16)).astype(
        jnp.float32
    )
    grads = jnp.concatenate(
        [
            jnp.einsum("sh,src->hrc", lat_own[:, 0], d_piece[:, :, :split], precision=highest),
            jnp.einsum("sh,src->hrc", lat_own[:, 1], d_piece[:, :, split:], precision=highest),
        ],
        axis=2,
    )
    d_latent = jnp.stack(
        [
            jnp.einsum(
                "src,hrc->sh", d_piece[:, :, :split], weights32[:, :, :split], precision=highest
            ),
            jnp.einsum(
                "src,hrc->sh", d_piece[:, :, split:], weights32[:, :, split:], precision=highest
            ),
        ],
        axis=1,
    )
    d_pre = d_latent * silu_grad(pre_own)
    grad_in = jnp.dot(emb_piece.T, d_pre[:, 0] + d_pre[:, 1], precision=highest)
    grad_mod = jnp.sum(d_pre, axis=0)
    grads, grad_in, grad_mod = (grads, grad_in, grad_mod)
    grad_in, grad_mod = (
        lax.psum(grad_in.astype(jnp.bfloat16), "head").astype(jnp.float32),
        lax.psum(grad_mod.astype(jnp.bfloat16), "head").astype(jnp.float32),
    )
    grad_wa_q = grads[:, :, :width_q]
    grad_wb_q = grads[:, :, width_q:split]
    grad_wa_v = grads[:, :, split : split + width_q]
    grad_wb_v = grads[:, :, split + width_q :]
    return (q_out, v_out, grad_wa_q, grad_wb_q, grad_wa_v, grad_wb_v, grad_in, grad_mod)


def solution(mesh):
    placed = (
        P(),
        P("dp"),
        P("dp"),
        P(),
        P(),
        P("dp", None, "head"),
        P("dp", None, "head"),
        P("dp", None, "head"),
        P("dp", None, "head"),
        P(None, "head"),
        P(None, "head"),
        P("dp", None, "head"),
        P("dp", None, "head"),
        P("dp", None, "head"),
    )
    return jax.shard_map(
        on_device,
        mesh=mesh,
        in_specs=placed,
        out_specs=(
            P("dp", None, "head"),
            P("dp", None, "head"),
            P("dp", None, "head"),
            P("dp", None, "head"),
            P("dp", None, "head"),
            P("dp", None, "head"),
            P(None, "dp"),
            P(None, "dp"),
        ),
        check_vma=False,
    )
```

profile of v0, /device:TPU:1, one launch (start us, length us, event | category | flops | bytes accessed | tf_op | source)
XLA Modules:
  0.0 777.2 jit_solution(7045139113011843579)
XLA Ops:
  7.3 0.9 copy.49
  8.2 0.8 copy.50
  8.9 0.8 copy.51
  9.7 0.7 copy.52
  10.4 0.7 pad_maximum_fusion
  11.2 0.7 all-gather.5.cloned.1.call-update
  11.9 0.7 convert_element_type.67
  12.6 0.7 fusion.50
  13.3 1.3 fusion.46
  14.6 1.2 fusion.43
  15.8 0.7 broadcast_add_fusion
  16.5 215.3 %all-gather.7.cloned.1.call-done = bf16[256,8,832]{2,0,1:T(8,128)(2,1)} async-done(((bf16[8,8,832]{2,0,1:T(8,128)(2,1)}), bf16[256,8,832]{2,0,1:T(8,128)(2,1)}) %all-gather.7.cloned.1.call-update) | async-done | bytes 3407888 | tf_op jit(solution)/shard_map/all_gather | solution.py:57
  231.8 1.7 fusion.12
  233.6 2.0 fusion.9
  236.4 164.5 %all-reduce = (bf16[2,320,16]{1,2,0:T(8,128)(2,1)S(1)}, bf16[2,320,16]{1,2,0:T(8,128)(2,1)S(1)}) all-reduce(f32[2,320,16]{1,2,0:T(8,128)S(1)} %pad_maximum_fusion.2, f32[2,320,16]{1,2,0:T(8,128)S(1)} %pad_maximum_fusion.3), channel_id=1, replica_groups=mesh['dp'=32,'head'=16] {'head'}, use_global_device_ids=true, to_apply=%region_0.1 | all-reduce | flops 20480 | bytes 122880 | tf_op jit(solution)/shard_map/psum | solution.py:70
  401.6 0.6 pad_maximum_fusion.1
  402.3 99.7 %all_gather.17 = f32[64,2,256]{2,1,0:T(2,128)S(1)} all-gather(f32[2,2,256]{2,1,0:T(2,128)S(1)} %copy.58), channel_id=1, replica_groups=mesh['dp'=32,'head'=16] {'dp'}, dimensions={0}, use_global_device_ids=true | all-gather | bytes 135168 | tf_op jit(solution)/shard_map/all_gather | solution.py:138
  502.1 102.7 %all-gather = f32[32,2,1024]{2,1,0:T(2,128)S(1)} all-gather(f32[1,2,1024]{2,1,0:T(2,128)S(1)} %bitcast.45), channel_id=1, replica_groups=mesh['dp'=32,'head'=16] {'dp'}, dimensions={0}, use_global_device_ids=true | all-gather | bytes 270336 | tf_op jit(solution)/shard_map/all_gather | solution.py:139
  605.3 4.2 fusion.2
  609.5 1.0 fusion.7
  610.5 2.5 fusion.8
  613.0 3.1 all-gather.9.cloned.1.call-done
  616.1 1.3 slice.111
  617.4 1.2 convolution_bitcast_fusion.3
  618.6 1.2 slice.115
  620.9 1.0 fusion.16
  622.2 144.8 %all-reduce.1 = (bf16[1024,8]{0,1:T(8,128)(2,1)S(1)}, bf16[2,8]{1,0:T(2,128)(2,1)S(1)}) all-reduce(bf16[1024,8]{0,1:T(8,128)(2,1)S(1)} %convolution_convert_fusion, bf16[2,8]{1,0:T(2,128)(2,1)S(1)} %get-tuple-element.28), channel_id=1, replica_groups=mesh['dp'=32,'head'=16] {'head'}, use_global_device_ids=true, to_apply=%region_2.3 | all-reduce | flops 8208 | bytes 32832 | tf_op jit(solution)/shard_map/psum | solution.py:167
  766.9 0.6 convert_element_type.73
  768.1 0.7 copy.70
  768.8 0.6 copy.71
  769.4 0.7 copy.68
  770.1 0.7 copy.69
  (44 shorter events, 4.3 us)
Async XLA Ops:
  7.2 598.1 %copy-start = (bf16[4096,256]{1,0:T(8,128)(2,1)S(1)}, bf16[4096,256]{1,0:T(8,128)(2,1)}, u32[]{:S(2)}) copy-start(bf16[4096,256]{1,0:T(8,128)(2,1)} %param.23) | copy-start | bytes 6291460
  7.2 228.8 %copy-start.2 = (bf16[2,320,256]{2,1,0:T(8,128)(2,1)S(1)}, bf16[2,320,256]{2,1,0:T(8,128)(2,1)}, u32[]{:S(2)}) copy-start(bf16[2,320,256]{2,1,0:T(8,128)(2,1)} %param.25) | copy-start | bytes 983044
  7.2 228.4 %copy-start.4 = (bf16[2,320,64]{1,2,0:T(8,128)(2,1)S(1)}, bf16[2,320,64]{1,2,0:T(8,128)(2,1)}, u32[]{:S(2)}) copy-start(bf16[2,320,64]{1,2,0:T(8,128)(2,1)} %param.27) | copy-start | bytes 245764
  7.2 228.5 %copy-start.5 = (bf16[2,320,256]{2,1,0:T(8,128)(2,1)S(1)}, bf16[2,320,256]{2,1,0:T(8,128)(2,1)}, u32[]{:S(2)}) copy-start(bf16[2,320,256]{2,1,0:T(8,128)(2,1)} %param.26) | copy-start | bytes 983044
  7.2 224.6 %all-gather.7.cloned.1.call-start = ((), (), s32[]{:S(2)}) async-start(), calls=%async_computation.1 | async-start | bytes 3784704 | tf_op jit(solution)/shard_map/all_gather | solution.py:57
  11.1 594.2 %all-gather.5.cloned.1.call-start = ((), (), s32[]{:S(2)}) async-start(), calls=%async_computation | async-start | bytes 5570560 | tf_op jit(solution)/shard_map/all_gather | solution.py:74
  11.9 604.2 %all-gather.9.cloned.1.call-start = ((), (), s32[]{:S(2)}) async-start(), calls=%async_computation.2 | async-start | bytes 1892352 | tf_op jit(solution)/shard_map/all_gather | solution.py:137
  605.3 5.2 copy-start.3
  605.3 5.2 copy-start.1
Sparse Core Ops, SparseCore 0:
  11.2 220.5 all-gather.6
  234.9 155.6 all-gather.4
  402.4 213.7 all-gather.8
where the time goes:
time: 790 us; the launch traced here: 777 us
  blocking collectives  512 us (65%)
  waiting for transfers between devices  219 us (28%)
  matrix products  18.9 us (2%)
  between operations  13.9 us (2%)
  local copies, waits for them, and re-layouts  8.72 us (1%)
    all_gather x1, waiting for transfers between devices, on_device(): lax.all_gather(packed, 'dp', axis=0, tiled=True)  215 us
    psum x1, blocking collectives, on_device(): low = lax.psum(low_part, 'head').astype(jnp.bfloat16)  164 us
    psum x1, blocking collectives, on_device(): lax.psum(grad_in.astype(jnp.bfloat16), 'head').astype(jnp.float32)  145 us
    all_gather x1, blocking collectives, on_device(): emb_piece = lax.all_gather(embeds, 'dp', axis=0, tiled=True)  103 us
    all_gather x1, blocking collectives, on_device(): pre_piece = lax.all_gather(pre, 'dp', axis=0, tiled=True)  99.7 us
  transfers between devices with their start and end apart: 3, of which 2 were waited for; matrix products, arithmetic and copies ran while one was open for 2% of the time, Pallas kernels for 0%

commit v1 on v0

v1 whole, which is shorter than its diff:
```python
import jax
import jax.numpy as jnp
from jax import lax
from jax.sharding import Mesh, PartitionSpec as P

bf16, f32 = jnp.bfloat16, jnp.float32
scale = 2.0


def silu_grad(pre):
    sig = jax.nn.sigmoid(pre)
    return sig * (1.0 + pre * (1.0 - sig))


def swap(blocks, axes):
    return lax.all_to_all(blocks, axes, 0, 0, tiled=True)


def spread(block, axes, n):
    return swap(jnp.broadcast_to(block[None], (n,) + block.shape), axes)


def dot(eq, a, b):
    return jnp.einsum(eq, a, b, preferred_element_type=f32)


def on_device(
    task_embed,
    task_ids,
    seq_lengths,
    w_in,
    module_embed,
    wa_q,
    wb_q,
    wa_v,
    wb_v,
    base_q,
    base_v,
    hidden_in,
    grad_q,
    grad_v,
):
    ny, nz, nh, nx, nc = (lax.axis_size(a) for a in ("y", "zl", "zh", "x", "c"))
    y, zl, zh = (lax.axis_index(a) for a in ("y", "zl", "zh"))
    xc = ("x", "c")
    head = ("zh", "x", "c")
    seqs, length, wq = hidden_in.shape
    rows, rank, _ = wa_q.shape
    wv = wb_v.shape[2]
    tasks = task_embed.shape[0]
    split, width = 2 * wq, 3 * wq + wv

    other = lax.ppermute(hidden_in, "zh", [(0, 1), (1, 0)])
    near = lax.all_gather(hidden_in, xc, axis=0, tiled=False)
    far = lax.all_gather(other, xc, axis=0, tiled=False)

    ids_near = spread(jnp.broadcast_to(task_ids[:, None], (seqs, 128)), "zl", nz)[:, :, 0].reshape(-1)
    packed = jnp.concatenate([wa_q, wb_q, wa_v, wb_v], axis=2)
    w_y = spread(packed, "y", ny)

    pre_t = lax.dot_general(w_in, task_embed, (((0,), (1,)), ((), ())), preferred_element_type=f32)
    pre_t = pre_t[None] + module_embed[:, :, None]
    pre_z = lax.dynamic_slice_in_dim(pre_t.reshape(2, ny, nz, rows, tasks), zl, 1, 2)[:, :, 0]
    lat_z = jax.nn.silu(pre_z).astype(bf16).reshape(2, ny * rows, tasks)
    pre_own = lax.dynamic_slice_in_dim(pre_z, y, 1, 1)[:, 0]
    lat_own = jax.nn.silu(pre_own).astype(bf16)
    sg_own = silu_grad(pre_own)

    def picked(ids):
        return (jnp.arange(tasks, dtype=jnp.int32)[:, None] == ids[None, :]).astype(bf16)

    lat_near = dot("mht,ts->mhs", lat_z, picked(ids_near)).astype(bf16)
    w_all = w_y.reshape(ny * rows, rank, width)
    part = jnp.concatenate(
        [
            dot("hs,hrc->src", lat_near[0], w_all[:, :, :split]),
            dot("hs,hrc->src", lat_near[1], w_all[:, :, split:]),
        ],
        axis=2,
    ).astype(bf16)
    got = swap(part.reshape(nz, seqs * rank, width), "zl")
    adapters = jnp.sum(got.astype(f32), axis=0).astype(bf16).reshape(seqs, rank, width)
    a_q, b_q = adapters[:, :, :wq], adapters[:, :, wq:split]
    a_v, b_v = adapters[:, :, split : split + wq], adapters[:, :, split + wq :]

    positions = jnp.arange(length, dtype=jnp.int32)
    weight = (positions[None, :] < seq_lengths[:, None]).astype(f32) / seq_lengths.astype(f32)[:, None]
    w2 = scale * weight[:, None, :]
    u_q = dot("srd,std->srt", a_q, hidden_in)
    u_v = dot("srd,std->srt", a_v, hidden_in)
    du_q = dot("src,stc->srt", b_q, grad_q) * w2
    du_v = dot("src,stc->srt", b_v, grad_v) * w2
    low = jnp.stack([u_q, u_v, du_q, du_v], axis=1).astype(bf16)
    low = swap(low.reshape(nx * nc, rank, length), xc)
    low = jnp.sum(low.astype(f32), axis=0).astype(bf16)
    low = spread(low, head, nh * nx * nc)
    low = jnp.sum(low.reshape(nh, seqs, 4, rank, length).astype(f32), axis=0)
    u32 = low[:, :2]
    u = u32.astype(bf16)
    ug = (u32 * w2[:, None]).astype(bf16)
    du = low[:, 2:].astype(bf16)
    d_a = dot("smrt,std->smrd", du, hidden_in)
    d_bq = dot("srt,stc->src", ug[:, 0], grad_q)
    d_bv = dot("srt,stc->src", ug[:, 1], grad_v)
    ids_col = jnp.broadcast_to(task_ids.astype(f32)[:, None, None], (seqs, rank, 64))
    d_own = jnp.concatenate([d_a[:, 0], d_bq, d_a[:, 1], d_bv, ids_col], axis=2).astype(bf16)
    d_z = spread(d_own.reshape(seqs * rank, width + 64), "zl", nz)
    d_all = spread(d_z.reshape(nz * seqs * rank, width + 64), "y", ny)
    d_all = d_all.reshape(ny * nz * seqs, rank, width + 64)

    ids_all = d_all[:, 0, width].astype(jnp.int32)
    pick_all = picked(ids_all)
    lat_all = dot("mht,ts->mhs", lat_own, pick_all).astype(bf16)
    d_q, d_v = d_all[:, :, :split], d_all[:, :, split:width]
    grads_q = dot("hs,src->hrc", lat_all[0], d_q)
    grads_v = dot("hs,src->hrc", lat_all[1], d_v)
    d_lat = jnp.stack(
        [dot("src,hrc->hs", d_q, packed[:, :, :split]), dot("src,hrc->hs", d_v, packed[:, :, split:])]
    )
    d_lat = spread(d_lat.reshape(2 * rows, -1), head, nh * nx * nc)
    d_lat = jnp.sum(d_lat, axis=0).reshape(2, rows, -1)
    sg_all = jnp.einsum("mht,ts->mhs", sg_own, pick_all.astype(f32), precision=lax.Precision.HIGHEST)
    d_pre = d_lat * sg_all
    embeds = dot("ts,te->se", pick_all, task_embed).astype(bf16)
    both = d_pre[0] + d_pre[1]
    hi = both.astype(bf16)
    lo = (both - hi.astype(f32)).astype(bf16)
    grad_in = dot("se,hs->eh", embeds, hi) + dot("se,hs->eh", embeds, lo)
    grad_mod = jnp.sum(d_pre, axis=2)

    cols = nx * nc
    base_q = base_q.reshape(nh, cols, wq, -1)
    base_v = base_v.reshape(nh, cols, wq, -1)
    full = jnp.stack([jnp.where(zh == 0, near, far), jnp.where(zh == 0, far, near)])
    q_out = dot("gjstd,gjdc->stc", full, base_q) + scale * dot("srt,src->stc", u[:, 0], b_q)
    v_out = dot("gjstd,gjdc->stc", full, base_v) + scale * dot("srt,src->stc", u[:, 1], b_v)

    return (
        q_out.astype(bf16),
        v_out.astype(bf16),
        grads_q[:, :, :wq],
        grads_q[:, :, wq:],
        grads_v[:, :, :wq],
        grads_v[:, :, wq:],
        grad_in,
        grad_mod,
    )


def solution(mesh):
    fine = Mesh(mesh.devices.reshape(4, 8, 2, 4, 2), ("y", "zl", "zh", "x", "c"))
    dp, head = ("y", "zl"), ("zh", "x", "c")
    rows_cols = P(dp, None, head)
    return jax.shard_map(
        on_device,
        mesh=fine,
        in_specs=(P(), P(dp), P(dp), P(), P())
        + (rows_cols,) * 4
        + (P(None, head),) * 2
        + (rows_cols,) * 3,
        out_specs=(rows_cols,) * 6 + (P(None, dp),) * 2,
        check_vma=False,
    )
```

time: 790 us -> 202 us (0.26); the launches traced: 777 us -> 201 us
  blocking collectives: 512 us -> 20.6 us
  waiting for transfers between devices: 219 us -> 54.9 us
  starting transfers between devices: 0.12 us -> 65.5 us
  local copies, waits for them, and re-layouts: 8.72 us -> 17.7 us
    psum x2 -> x0, blocking collectives: 309 us -> none  [the longest x1 164 us: on_device(): low = lax.psum(low_part, 'head').astype(jnp.bfloat16)]
    all_gather x3 -> x2, waiting for transfers between devices: 218 us -> 0.01 us  [the longest x1 0.01 us: on_device(): near = lax.all_gather(hidden_in, xc, axis=0, tiled=False)]
    all_gather x2 -> x0, blocking collectives: 202 us -> none  [the longest x1 103 us: on_device(): emb_piece = lax.all_gather(embeds, 'dp', axis=0, tiled=True)]
    all_to_all x0 -> x7, starting transfers between devices: none -> 57.5 us  [swap(): return lax.all_to_all(blocks, axes, 0, 0, tiled=True)]
    all_to_all x0 -> x7, waiting for transfers between devices: none -> 34.3 us  [swap(): return lax.all_to_all(blocks, axes, 0, 0, tiled=True)]
    all_to_all x0 -> x1, blocking collectives: none -> 20.6 us  [swap(): return lax.all_to_all(blocks, axes, 0, 0, tiled=True)]
    ppermute x0 -> x1, waiting for transfers between devices: none -> 19.9 us  [on_device(): other = lax.ppermute(hidden_in, 'zh', [(0, 1), (1, 0)])]
    ppermute x0 -> x1, starting transfers between devices: none -> 7.93 us  [on_device(): other = lax.ppermute(hidden_in, 'zh', [(0, 1), (1, 0)])]
  transfers between devices with their start and end apart: 3 -> 10, of which waited for: 2 -> 7; matrix products, arithmetic and copies ran while one was open for 2% -> 18% of each run, Pallas kernels for 0% -> 0%
where the time goes in v1:
time: 202 us; the launch traced here: 201 us
  starting transfers between devices  65.5 us (32%)
  waiting for transfers between devices  54.9 us (27%)
  blocking collectives  20.6 us (10%)
  matrix products  19 us (9%)
  local copies, waits for them, and re-layouts  17.7 us (9%)
  between operations  14.4 us (7%)
  other arithmetic  8.58 us (4%)
    all_to_all x7, starting transfers between devices, swap(): return lax.all_to_all(blocks, axes, 0, 0, tiled=True)  57.5 us
    all_to_all x7, waiting for transfers between devices, swap(): return lax.all_to_all(blocks, axes, 0, 0, tiled=True)  34.3 us
    all_to_all x1, blocking collectives, swap(): return lax.all_to_all(blocks, axes, 0, 0, tiled=True)  20.6 us
    ppermute x1, waiting for transfers between devices, on_device(): other = lax.ppermute(hidden_in, 'zh', [(0, 1), (1, 0)])  19.9 us
    dot_general x22, matrix products, dot(): return jnp.einsum(eq, a, b, preferred_element_type=f32)  15.9 us
    unnamed x43, local copies, waits for them, and re-layouts  10.3 us
    ppermute x1, starting transfers between devices, on_device(): other = lax.ppermute(hidden_in, 'zh', [(0, 1), (1, 0)])  7.93 us
  transfers between devices with their start and end apart: 10, of which 7 were waited for; matrix products, arithmetic and copies ran while one was open for 18% of the time, Pallas kernels for 0%

profile of v1, /device:TPU:1, one launch (start us, length us, event | category | flops | bytes accessed | tf_op | source)
XLA Modules:
  0.0 200.8 jit_solution(6600982491535220821)
XLA Ops:
  7.9 1.3 broadcast_in_dim_broadcast_in_dim_broadcast_in_dim.2
  9.2 13.1 %all-to-all-start = ((s32[8,2,128]{2,1,0:T(2,128)}), s32[8,2,128]{2,1,0:T(2,128)S(1)}, u32[]{:S(2)}, u32[]{:S(2)}) async-start(s32[8,2,128]{2,1,0:T(2,128)} %broadcast_in_dim_broadcast_in_dim_broadcast_in_dim.2), calls=%async_computation | async-start | bytes 16384 | tf_op jit(solution)/shard_map/all_to_all | solution.py:16
  23.1 1.5 fusion.83
  26.5 5.1 %all-to-all-done = s32[8,2,128]{2,1,0:T(2,128)S(1)} async-done(((s32[8,2,128]{2,1,0:T(2,128)}), s32[8,2,128]{2,1,0:T(2,128)S(1)}, u32[]{:S(2)}, u32[]{:S(2)}) %all-to-all-start) | async-done | bytes 8224 | tf_op jit(solution)/shard_map/all_to_all | solution.py:16
  32.4 4.3 %all-to-all-start.1 = ((bf16[4,8,8,832]{3,1,2,0:T(8,128)(2,1)}), bf16[4,8,8,832]{3,1,2,0:T(8,128)(2,1)S(1)}, u32[]{:S(2)}, u32[]{:S(2)}) async-start(bf16[4,8,8,832]{3,1,2,0:T(8,128)(2,1)} %broadcast_in_dim.18), calls=%async_computation.1 | async-start | bytes 917504 | tf_op jit(solution)/shard_map/all_to_all | solution.py:16
  37.0 1.0 convolution_convert_fusion.7
  38.1 5.3 %all-to-all-done.1 = bf16[4,8,8,832]{3,1,2,0:T(8,128)(2,1)S(1)} async-done(((bf16[4,8,8,832]{3,1,2,0:T(8,128)(2,1)}), bf16[4,8,8,832]{3,1,2,0:T(8,128)(2,1)S(1)}, u32[]{:S(2)}, u32[]{:S(2)}) %all-to-all-start.1) | async-done | bytes 426016 | tf_op jit(solution)/shard_map/all_to_all | solution.py:16
  44.6 4.6 %all-to-all-start.2 = ((bf16[8,16,832]{2,1,0:T(8,128)(2,1)}), bf16[8,16,832]{2,1,0:T(8,128)(2,1)S(1)}, u32[]{:S(2)}, u32[]{:S(2)}) async-start(bf16[8,16,832]{2,1,0:T(8,128)(2,1)} %pad_maximum_fusion.15), calls=%async_computation.2 | async-start | bytes 458752 | tf_op jit(solution)/shard_map/all_to_all | solution.py:16
  49.3 11.2 %all-to-all-done.2 = bf16[8,16,832]{2,1,0:T(8,128)(2,1)S(1)} async-done(((bf16[8,16,832]{2,1,0:T(8,128)(2,1)}), bf16[8,16,832]{2,1,0:T(8,128)(2,1)S(1)}, u32[]{:S(2)}, u32[]{:S(2)}) %all-to-all-start.2) | async-done | bytes 213024 | tf_op jit(solution)/shard_map/all_to_all | solution.py:16
  61.9 8.8 %all-to-all-start.3 = ((bf16[8,8,320]{2,1,0:T(8,128)(2,1)}), bf16[8,8,320]{2,1,0:T(8,128)(2,1)S(1)}, u32[]{:S(2)}, u32[]{:S(2)}) async-start(bf16[8,8,320]{2,1,0:T(8,128)(2,1)} %bitcast.22), calls=%async_computation.3 | async-start | bytes 98304 | tf_op jit(solution)/shard_map/all_to_all | solution.py:16
  70.7 7.9 %collective-permute-start = (bf16[2,320,256]{2,1,0:T(8,128)(2,1)S(1)}, bf16[2,320,256]{2,1,0:T(8,128)(2,1)S(1)}, u32[]{:S(2)}, u32[]{:S(2)}) collective-permute-start(bf16[2,320,256]{2,1,0:T(8,128)(2,1)S(1)} %copy-done.1), channel_id=1, source_target_pairs={{0,8},{8,0},{1,9},{9,1},{2,10},{10,2},{3,11},{11,3},{4,12},{12,4},... | collective-permute-start | bytes 983048 | tf_op jit(solution)/shard_map/ppermute | solution.py:53
  79.3 9.0 %all-to-all-start.4 = ((bf16[16,8,320]{2,1,0:T(8,128)(2,1)}), bf16[16,8,320]{2,1,0:T(8,128)(2,1)S(1)}, u32[]{:S(2)}, u32[]{:S(2)}) async-start(bf16[16,8,320]{2,1,0:T(8,128)(2,1)} %broadcast_in_dim.19), calls=%async_computation.4 | async-start | bytes 196608 | tf_op jit(solution)/shard_map/all_to_all | solution.py:16
  88.5 19.9 %collective-permute-done = bf16[2,320,256]{2,1,0:T(8,128)(2,1)S(1)} collective-permute-done((bf16[2,320,256]{2,1,0:T(8,128)(2,1)S(1)}, bf16[2,320,256]{2,1,0:T(8,128)(2,1)S(1)}, u32[]{:S(2)}, u32[]{:S(2)}) %collective-permute-start) | collective-permute-done | bytes 327712 | tf_op jit(solution)/shard_map/ppermute | solution.py:53
  109.2 2.9 %all-to-all-done.4 = bf16[16,8,320]{2,1,0:T(8,128)(2,1)S(1)} async-done(((bf16[16,8,320]{2,1,0:T(8,128)(2,1)}), bf16[16,8,320]{2,1,0:T(8,128)(2,1)S(1)}, u32[]{:S(2)}, u32[]{:S(2)}) %all-to-all-start.4) | async-done | bytes 81952 | tf_op jit(solution)/shard_map/all_to_all | solution.py:16
  112.8 20.6 %all_to_all.40 = bf16[8,16,896]{2,1,0:T(8,128)(2,1)S(1)} all-to-all(bf16[8,16,896]{2,1,0:T(8,128)(2,1)S(1)} %broadcast_in_dim.22), channel_id=1, replica_groups=mesh['y'=4,'zl'=8,'zh'=2,'x'=4,'c'=2] {'zl'}, dimensions={0} | all-to-all | bytes 458752 | tf_op jit(solution)/shard_map/all_to_all | solution.py:16
  133.5 1.0 broadcast_in_dim.24
  134.5 3.5 %all-to-all-start.6 = ((bf16[4,128,896]{2,1,0:T(8,128)(2,1)}), bf16[4,128,896]{2,1,0:T(8,128)(2,1)S(1)}, u32[]{:S(2)}, u32[]{:S(2)}) async-start(bf16[4,128,896]{2,1,0:T(8,128)(2,1)} %broadcast_in_dim.24), calls=%async_computation.6 | async-start | bytes 1835008 | tf_op jit(solution)/shard_map/all_to_all | solution.py:16
  140.5 2.0 copy.113
  143.4 1.1 convolution_multiply_fusion
  144.5 2.7 %all-to-all-done.6 = bf16[4,128,896]{2,1,0:T(8,128)(2,1)S(1)} async-done(((bf16[4,128,896]{2,1,0:T(8,128)(2,1)}), bf16[4,128,896]{2,1,0:T(8,128)(2,1)S(1)}, u32[]{:S(2)}, u32[]{:S(2)}) %all-to-all-start.6) | async-done | bytes 917536 | tf_op jit(solution)/shard_map/all_to_all | solution.py:16
  149.1 1.2 convolution_bitcast_fusion.1
  150.9 1.7 reshape.195
  152.6 14.2 %all-to-all-start.7 = ((f32[16,1,1024]{2,1,0:T(1,128)}), f32[16,1,1024]{2,1,0:T(1,128)}, u32[]{:S(2)}, u32[]{:S(2)}) async-start(f32[16,1,1024]{2,1,0:T(1,128)} %reshape.195), calls=%async_computation.7 | async-start | bytes 131072 | tf_op jit(solution)/shard_map/all_to_all | solution.py:16
  166.8 1.3 fusion.41
  169.0 1.2 fusion.22
  173.1 1.3 convolution_convert_fusion
  174.4 7.1 %all-to-all-done.7 = f32[16,1,1024]{2,1,0:T(1,128)} async-done(((f32[16,1,1024]{2,1,0:T(1,128)}), f32[16,1,1024]{2,1,0:T(1,128)}, u32[]{:S(2)}, u32[]{:S(2)}) %all-to-all-start.7) | async-done | bytes 65568 | tf_op jit(solution)/shard_map/all_to_all | solution.py:16
  182.0 1.6 reduce.6
  183.7 1.6 fusion.82
  186.2 2.9 %broadcast_select_fusion.1 = (bf16[16,320,256]{2,1,0:T(8,128)(2,1)S(1)}, bf16[16,320,256]{2,1,0:T(8,128)(2,1)S(1)}) fusion(bf16[16,320,256]{2,1,0:T(8,128)(2,1)} %all-gather.5.cloned.1.call-done, bf16[16,320,256]{2,1,0:T(8,128)(2,1)} %all-gather.7.cloned.1.call-done, pred[]{:T(512)S(6)} %eq.32), kind=kLoop, calls=%fused_computation.4 | loop fusion | flops 2621440 | bytes 10485761 | tf_op jit(solution)/shard_map/jit(_where)/select_n | solution.py:134
  189.2 2.5 %fusion.7 = bf16[2,320,64]{1,2,0:T(8,128)(2,1)} fusion(f32[2,320,64]{1,2,0:T(8,128)S(1)} %copy-done.8, bf16[1,8,2,320,256]{4,3,2,1,0:T(8,128)(2,1)S(1)} %bitcast.184, bf16[1,8,2,320,256]{4,3,2,1,0:T(8,128)(2,1)S(1)} %bitcast.182, bf16[2,8,256,64,1]{2,1,0,3,4:T(8,128)(2,1)S(1)} %bitcast.192), kind=kOutput, calls=%fused_computation.14 | convolution fusion | flops 338247680 | bytes 6012928 | tf_op jit(solution)/shard_map/gjstd,gjdc->stc/dot_general | solution.py:24
  191.7 2.3 %fusion.4 = bf16[2,320,256]{2,1,0:T(8,128)(2,1)} fusion(f32[2,320,256]{2,1,0:T(8,128)S(1)} %copy-done.4, bf16[2,8,256,256,1]{3,2,4,1,0:T(8,128)(2,1)S(1)} %bitcast.178, bf16[1,8,2,320,256]{4,3,2,1,0:T(8,128)(2,1)S(1)} %bitcast.185, bf16[1,8,2,320,256]{4,3,2,1,0:T(8,128)(2,1)S(1)} %bitcast.183), kind=kOutput, calls=%fused_computation.8 | convolution fusion | flops 1345126400 | bytes 8323072 | tf_op jit(solution)/shard_map/gjstd,gjdc->stc/dot_general | solution.py:24
  (101 shorter events, 20.5 us)
Async XLA Ops:
  7.2 184.5 %copy-start = (bf16[4096,256]{1,0:T(8,128)(2,1)S(1)}, bf16[4096,256]{1,0:T(8,128)(2,1)}, u32[]{:S(2)}) copy-start(bf16[4096,256]{1,0:T(8,128)(2,1)} %param.23) | copy-start | bytes 6291460
  7.2 179.0 %all-gather.5.cloned.1.call-start = ((), (), s32[]{:S(2)}) async-start(), calls=%async_computation.8 | async-start | bytes 2949120 | tf_op jit(solution)/shard_map/all_gather | solution.py:54
  9.2 22.4 %all-to-all-start = ((s32[8,2,128]{2,1,0:T(2,128)}), s32[8,2,128]{2,1,0:T(2,128)S(1)}, u32[]{:S(2)}, u32[]{:S(2)}) async-start(s32[8,2,128]{2,1,0:T(2,128)} %broadcast_in_dim_broadcast_in_dim_broadcast_in_dim.2), calls=%async_computation | async-start | bytes 16384 | tf_op jit(solution)/shard_map/all_to_all | solution.py:16
  25.6 23.6 %copy-start.15 = (s32[2]{0:T(128)S(1)}, s32[2]{0:T(128)}, u32[]{:S(2)}) copy-start(s32[2]{0:T(128)} %param.16) | copy-start | bytes 28
  26.4 34.1 %copy-start.6 = (bf16[2,320,64]{1,2,0:T(8,128)(2,1)S(1)}, bf16[2,320,64]{1,2,0:T(8,128)(2,1)}, u32[]{:S(2)}) copy-start(bf16[2,320,64]{1,2,0:T(8,128)(2,1)} %param.27) | copy-start | bytes 245764
  26.5 34.2 %copy-start.1 = (bf16[2,320,256]{2,1,0:T(8,128)(2,1)S(1)}, bf16[2,320,256]{2,1,0:T(8,128)(2,1)}, u32[]{:S(2)}) copy-start(bf16[2,320,256]{2,1,0:T(8,128)(2,1)} %param.25) | copy-start | bytes 983044
  32.4 28.6 %copy-start.3 = (bf16[2,320,256]{2,1,0:T(8,128)(2,1)S(1)}, bf16[2,320,256]{2,1,0:T(8,128)(2,1)}, u32[]{:S(2)}) copy-start(bf16[2,320,256]{2,1,0:T(8,128)(2,1)} %param.26) | copy-start | bytes 983044
  32.4 10.9 %all-to-all-start.1 = ((bf16[4,8,8,832]{3,1,2,0:T(8,128)(2,1)}), bf16[4,8,8,832]{3,1,2,0:T(8,128)(2,1)S(1)}, u32[]{:S(2)}, u32[]{:S(2)}) async-start(bf16[4,8,8,832]{3,1,2,0:T(8,128)(2,1)} %broadcast_in_dim.18), calls=%async_computation.1 | async-start | bytes 917504 | tf_op jit(solution)/shard_map/all_to_all | solution.py:16
  38.1 50.3 %copy-start.14 = (s32[2]{0:T(128)S(1)}, s32[2]{0:T(128)}, u32[]{:S(2)}) copy-start(s32[2]{0:T(128)} %param.15) | copy-start | bytes 28
  44.6 15.9 %all-to-all-start.2 = ((bf16[8,16,832]{2,1,0:T(8,128)(2,1)}), bf16[8,16,832]{2,1,0:T(8,128)(2,1)S(1)}, u32[]{:S(2)}, u32[]{:S(2)}) async-start(bf16[8,16,832]{2,1,0:T(8,128)(2,1)} %pad_maximum_fusion.15), calls=%async_computation.2 | async-start | bytes 458752 | tf_op jit(solution)/shard_map/all_to_all | solution.py:16
  61.9 16.8 %all-to-all-start.3 = ((bf16[8,8,320]{2,1,0:T(8,128)(2,1)}), bf16[8,8,320]{2,1,0:T(8,128)(2,1)S(1)}, u32[]{:S(2)}, u32[]{:S(2)}) async-start(bf16[8,8,320]{2,1,0:T(8,128)(2,1)} %bitcast.22), calls=%async_computation.3 | async-start | bytes 98304 | tf_op jit(solution)/shard_map/all_to_all | solution.py:16
  70.7 37.7 %collective-permute-start = (bf16[2,320,256]{2,1,0:T(8,128)(2,1)S(1)}, bf16[2,320,256]{2,1,0:T(8,128)(2,1)S(1)}, u32[]{:S(2)}, u32[]{:S(2)}) collective-permute-start(bf16[2,320,256]{2,1,0:T(8,128)(2,1)S(1)} %copy-done.1), channel_id=1, source_target_pairs={{0,8},{8,0},{1,9},{9,1},{2,10},{10,2},{3,11},{11,3},{4,12},{12,4},... | collective-permute-start | bytes 983048 | tf_op jit(solution)/shard_map/ppermute | solution.py:53
  79.3 32.8 %all-to-all-start.4 = ((bf16[16,8,320]{2,1,0:T(8,128)(2,1)}), bf16[16,8,320]{2,1,0:T(8,128)(2,1)S(1)}, u32[]{:S(2)}, u32[]{:S(2)}) async-start(bf16[16,8,320]{2,1,0:T(8,128)(2,1)} %broadcast_in_dim.19), calls=%async_computation.4 | async-start | bytes 196608 | tf_op jit(solution)/shard_map/all_to_all | solution.py:16
  88.3 97.9 %all-gather.7.cloned.1.call-start = ((), (), s32[]{:S(2)}) async-start(), calls=%async_computation.9 | async-start | bytes 2949120 | tf_op jit(solution)/shard_map/all_gather | solution.py:55
  108.4 0.7 copy-start.7
  108.4 29.5 %copy-start.9 = (bf16[8,8,256]{2,1,0:T(8,128)(2,1)S(1)}, bf16[8,8,256]{2,1,0:T(8,128)(2,1)}, u32[]{:S(2)}) copy-start(bf16[8,8,256]{2,1,0:T(8,128)(2,1)} %param.19) | copy-start | bytes 98308
  108.4 30.2 %copy-start.10 = (bf16[8,8,256]{2,1,0:T(8,128)(2,1)S(1)}, bf16[8,8,256]{2,1,0:T(8,128)(2,1)}, u32[]{:S(2)}) copy-start(bf16[8,8,256]{2,1,0:T(8,128)(2,1)} %param.20) | copy-start | bytes 98308
  109.2 30.1 %copy-start.11 = (bf16[8,8,256]{2,1,0:T(8,128)(2,1)S(1)}, bf16[8,8,256]{2,1,0:T(8,128)(2,1)}, u32[]{:S(2)}) copy-start(bf16[8,8,256]{2,1,0:T(8,128)(2,1)} %param.21) | copy-start | bytes 98308
  109.2 30.7 %copy-start.12 = (bf16[8,8,64]{2,1,0:T(8,128)(2,1)S(1)}, bf16[8,8,64]{2,1,0:T(8,128)(2,1)}, u32[]{:S(2)}) copy-start(bf16[8,8,64]{2,1,0:T(8,128)(2,1)} %param.22) | copy-start | bytes 24580
  134.5 12.8 %all-to-all-start.6 = ((bf16[4,128,896]{2,1,0:T(8,128)(2,1)}), bf16[4,128,896]{2,1,0:T(8,128)(2,1)S(1)}, u32[]{:S(2)}, u32[]{:S(2)}) async-start(bf16[4,128,896]{2,1,0:T(8,128)(2,1)} %broadcast_in_dim.24), calls=%async_computation.6 | async-start | bytes 1835008 | tf_op jit(solution)/shard_map/all_to_all | solution.py:16
  140.5 7.6 %copy-start.13 = (bf16[8,8,64]{2,0,1:T(8,128)(2,1)S(1)}, bf16[8,8,64]{2,0,1:T(8,128)(2,1)}, u32[]{:S(2)}) copy-start(bf16[8,8,64]{2,0,1:T(8,128)(2,1)} %copy.96) | copy-start | bytes 24580
  147.3 0.8 copy-start.2
  152.6 28.8 %all-to-all-start.7 = ((f32[16,1,1024]{2,1,0:T(1,128)}), f32[16,1,1024]{2,1,0:T(1,128)}, u32[]{:S(2)}, u32[]{:S(2)}) async-start(f32[16,1,1024]{2,1,0:T(1,128)} %reshape.195), calls=%async_computation.7 | async-start | bytes 131072 | tf_op jit(solution)/shard_map/all_to_all | solution.py:16
  186.2 3.0 %copy-start.5 = (bf16[8,8,16,256]{3,2,1,0:T(8,128)(2,1)S(1)}, bf16[8,8,16,256]{3,2,1,0:T(8,128)(2,1)}, u32[]{:S(2)}) copy-start(bf16[8,8,16,256]{3,2,1,0:T(8,128)(2,1)} %copy.113) | copy-start | bytes 1572868
  186.2 3.0 %copy-start.8 = (f32[2,320,64]{1,2,0:T(8,128)S(1)}, f32[2,320,64]{1,2,0:T(8,128)}, u32[]{:S(2)}) copy-start(f32[2,320,64]{1,2,0:T(8,128)} %convolution_multiply_fusion.1) | copy-start | bytes 491524
  189.2 2.5 %copy-start.4 = (f32[2,320,256]{2,1,0:T(8,128)S(1)}, f32[2,320,256]{2,1,0:T(8,128)}, u32[]{:S(2)}) copy-start(f32[2,320,256]{2,1,0:T(8,128)} %convolution_multiply_fusion) | copy-start | bytes 1966084
Sparse Core Ops, SparseCore 0:
  10.1 39.4 all-gather.4
  109.3 36.0 all-gather.6

commit v2 on v1

--- a/solution.py
+++ b/solution.py
@@ -1,6 +1,8 @@
 import jax
 import jax.numpy as jnp
 from jax import lax
+from jax.experimental import pallas as pl
+from jax.experimental.pallas import tpu as pltpu
 from jax.sharding import Mesh, PartitionSpec as P
 
 bf16, f32 = jnp.bfloat16, jnp.float32
@@ -22,6 +24,50 @@
 
 def dot(eq, a, b):
     return jnp.einsum(eq, a, b, preferred_element_type=f32)
+
+
+def base_kernel(order, *refs):
+    near = refs[:8]
+    base_q, base_vt, u, ad, q_out, vt_out, acc_q, acc_v = refs[8:]
+    seqs, length, wq = q_out.shape
+    wv = vt_out.shape[1]
+    for n, block in enumerate(near):
+        for half in range(2):
+            h = block[half].reshape(seqs * length, wq)
+            at = pl.ds(pl.multiple_of(order[2 * n + half] * wq, wq), wq)
+            add_q = jnp.dot(h, base_q[at, :], preferred_element_type=f32)
+            add_v = lax.dot_general(h, base_vt[:, at], (((1,), (1,)), ((), ())), preferred_element_type=f32)
+            if n + half == 0:
+                acc_q[...], acc_v[...] = add_q, add_v
+            else:
+                acc_q[...] += add_q
+                acc_v[...] += add_v
+    first = (((0,), (0,)), ((), ()))
+    for s in range(seqs):
+        own = slice(s * length, (s + 1) * length)
+        b_q, b_v = ad[s, :, wq : 2 * wq], ad[s, :, 3 * wq : 3 * wq + wv]
+        low_q = lax.dot_general(u[s, 0], b_q, first, preferred_element_type=f32)
+        low_v = lax.dot_general(b_v, u[s, 1], first, preferred_element_type=f32)
+        q_out[s] = (acc_q[own, :] + scale * low_q).astype(bf16)
+        vt_out[s] = (acc_v[own, :].T + scale * low_v).astype(bf16)
+
+
+def base_product(order, blocks, base_q, base_vt, u, adapters, wv):
+    _, seqs, length, wq = blocks[0].shape
+    in_vmem = pl.BlockSpec(memory_space=pltpu.VMEM)
+    return pl.pallas_call(
+        base_kernel,
+        out_shape=(
+            jax.ShapeDtypeStruct((seqs, length, wq), bf16),
+            jax.ShapeDtypeStruct((seqs, wv, length), bf16),
+        ),
+        in_specs=[pl.BlockSpec(memory_space=pltpu.SMEM)] + [in_vmem] * (len(blocks) + 4),
+        out_specs=(in_vmem, in_vmem),
+        scratch_shapes=[pltpu.VMEM((seqs * length, wq), f32), pltpu.VMEM((seqs * length, wv), f32)],
+        compiler_params=pltpu.CompilerParams(vmem_limit_bytes=32 * 2**20),
+        cost_estimate=pl.CostEstimate(flops=2_000_000_000, bytes_accessed=9_000_000, transcendentals=0),
+        name="base_product",
+    )(order, *blocks, base_q, base_vt, u, adapters)
 
 
 def on_device(
@@ -51,12 +97,10 @@
     split, width = 2 * wq, 3 * wq + wv
 
     other = lax.ppermute(hidden_in, "zh", [(0, 1), (1, 0)])
-    near = lax.all_gather(hidden_in, xc, axis=0, tiled=False)
-    far = lax.all_gather(other, xc, axis=0, tiled=False)
 
     ids_near = spread(jnp.broadcast_to(task_ids[:, None], (seqs, 128)), "zl", nz)[:, :, 0].reshape(-1)
     packed = jnp.concatenate([wa_q, wb_q, wa_v, wb_v], axis=2)
-    w_y = spread(packed, "y", ny)
+    w_y = lax.all_gather(packed, "y", axis=0, tiled=False)
 
     pre_t = lax.dot_general(w_in, task_embed, (((0,), (1,)), ((), ())), preferred_element_type=f32)
     pre_t = pre_t[None] + module_embed[:, :, None]
@@ -79,6 +123,9 @@
         axis=2,
     ).astype(bf16)
     got = swap(part.reshape(nz, seqs * rank, width), "zl")
+    got, other = lax.optimization_barrier((got, other))
+    both_z = jnp.stack([hidden_in, other])
+    turned = [both_z] + [lax.ppermute(both_z, "x", [(i, (i + k) % nx) for i in range(nx)]) for k in range(1, nx)]
     adapters = jnp.sum(got.astype(f32), axis=0).astype(bf16).reshape(seqs, rank, width)
     a_q, b_q = adapters[:, :, :wq], adapters[:, :, wq:split]
     a_v, b_v = adapters[:, :, split : split + wq], adapters[:, :, split + wq :]
@@ -102,6 +149,7 @@
     d_a = dot("smrt,std->smrd", du, hidden_in)
     d_bq = dot("srt,stc->src", ug[:, 0], grad_q)
     d_bv = dot("srt,stc->src", ug[:, 1], grad_v)
+    turned = turned + [lax.ppermute(t, "c", [(0, 1), (1, 0)]) for t in turned]
     ids_col = jnp.broadcast_to(task_ids.astype(f32)[:, None, None], (seqs, rank, 64))
     d_own = jnp.concatenate([d_a[:, 0], d_bq, d_a[:, 1], d_bv, ids_col], axis=2).astype(bf16)
     d_z = spread(d_own.reshape(seqs * rank, width + 64), "zl", nz)
@@ -117,27 +165,36 @@
     d_lat = jnp.stack(
         [dot("src,hrc->hs", d_q, packed[:, :, :split]), dot("src,hrc->hs", d_v, packed[:, :, split:])]
     )
-    d_lat = spread(d_lat.reshape(2 * rows, -1), head, nh * nx * nc)
-    d_lat = jnp.sum(d_lat, axis=0).reshape(2, rows, -1)
+    batches = d_lat.shape[2]
+    d_lat = jnp.pad(d_lat.reshape(2 * rows, batches), ((0, 0), (0, 128 - batches)))
+    d_lat = spread(d_lat, head, nh * nx * nc)
     sg_all = jnp.einsum("mht,ts->mhs", sg_own, pick_all.astype(f32), precision=lax.Precision.HIGHEST)
+    embeds = dot("ts,te->se", pick_all, task_embed).astype(bf16)
+
+    x, c = lax.axis_index("x"), lax.axis_index("c")
+    order = jnp.stack(
+        [
+            (zh ^ half) * (nx * nc) + lax.rem(x - k + nx, nx) * nc + (c ^ core)
+            for core in range(nc)
+            for k in range(nx)
+            for half in range(nh)
+        ]
+    ).astype(jnp.int32)
+    q_out, vt_out = base_product(order, turned, base_q, base_v.T, u, adapters, wv)
+    d_lat, sg_all, embeds, q_out, vt_out, grads_q, grads_v = lax.optimization_barrier(
+        (d_lat, sg_all, embeds, q_out, vt_out, grads_q, grads_v)
+    )
+    d_lat = jnp.sum(d_lat, axis=0)[:, :batches].reshape(2, rows, batches)
     d_pre = d_lat * sg_all
-    embeds = dot("ts,te->se", pick_all, task_embed).astype(bf16)
     both = d_pre[0] + d_pre[1]
     hi = both.astype(bf16)
     lo = (both - hi.astype(f32)).astype(bf16)
     grad_in = dot("se,hs->eh", embeds, hi) + dot("se,hs->eh", embeds, lo)
     grad_mod = jnp.sum(d_pre, axis=2)
 
-    cols = nx * nc
-    base_q = base_q.reshape(nh, cols, wq, -1)
-    base_v = base_v.reshape(nh, cols, wq, -1)
-    full = jnp.stack([jnp.where(zh == 0, near, far), jnp.where(zh == 0, far, near)])
-    q_out = dot("gjstd,gjdc->stc", full, base_q) + scale * dot("srt,src->stc", u[:, 0], b_q)
-    v_out = dot("gjstd,gjdc->stc", full, base_v) + scale * dot("srt,src->stc", u[:, 1], b_v)
-
     return (
-        q_out.astype(bf16),
-        v_out.astype(bf16),
+        q_out,
+        vt_out.swapaxes(1, 2),
         grads_q[:, :, :wq],
         grads_q[:, :, wq:],
         grads_v[:, :, :wq],

time: 202 us -> 206 us (1.020)
  the two profiles are of different devices: /device:TPU:1 before, /device:TPU:97 now
where the time goes in v2:
time: 206 us; the launch traced here: 205 us
  starting transfers between devices  81.5 us (40%)
  waiting for transfers between devices  67.6 us (33%)
  blocking collectives  21.5 us (10%)
  local copies, waits for them, and re-layouts  16.1 us (8%)
  matrix products  7.05 us (3%)
  Pallas kernels  6.11 us (3%)
  other arithmetic  4 us (2%)
    all_to_all x6, starting transfers between devices, swap(): return lax.all_to_all(blocks, axes, 0, 0, tiled=True)  53 us
    ppermute x1, waiting for transfers between devices, on_device(): other = lax.ppermute(hidden_in, 'zh', [(0, 1), (1, 0)])  37.8 us
    all_to_all x6, waiting for transfers between devices, swap(): return lax.all_to_all(blocks, axes, 0, 0, tiled=True)  22.2 us
    all_gather x1, blocking collectives, on_device(): w_y = lax.all_gather(packed, 'y', axis=0, tiled=False)  11.6 us
    ppermute x3, starting transfers between devices, on_device(): lax.ppermute(both_z, 'x', [(i, (i + k) % nx) for i in range(nx)])  10.7 us
    ppermute x4, starting transfers between devices, on_device(): turned = turned + [lax.ppermute(t, 'c', [(0, 1), (1, 0)]) for t in turned]  9.94 us
    all_to_all x1, blocking collectives, swap(): return lax.all_to_all(blocks, axes, 0, 0, tiled=True)  9.9 us
    ppermute x1, starting transfers between devices, on_device(): other = lax.ppermute(hidden_in, 'zh', [(0, 1), (1, 0)])  7.93 us
  transfers between devices with their start and end apart: 14, of which 5 were waited for; matrix products, arithmetic and copies ran while one was open for 5% of the time, Pallas kernels for 3%

profile of v2, /device:TPU:97, one launch (start us, length us, event | category | flops | bytes accessed | tf_op | source)
XLA Modules:
  0.0 204.9 jit_solution(1355464302304159535)
XLA Ops:
  0.6 1.4 broadcast_in_dim_broadcast_in_dim_broadcast_in_dim.2
  2.0 11.2 %all-to-all-start = ((s32[8,2,128]{2,1,0:T(2,128)}), s32[8,2,128]{2,1,0:T(2,128)S(1)}, u32[]{:S(2)}, u32[]{:S(2)}) async-start(s32[8,2,128]{2,1,0:T(2,128)} %broadcast_in_dim_broadcast_in_dim_broadcast_in_dim.2), calls=%async_computation | async-start | bytes 16384 | tf_op jit(solution)/shard_map/all_to_all | solution.py:18
  17.1 1.4 fusion.72
  18.7 11.6 %all-gather = bf16[32,8,832]{2,0,1:T(8,128)(2,1)S(1)} all-gather(bf16[8,8,832]{2,0,1:T(8,128)(2,1)S(1)} %pad_maximum_fusion.2), channel_id=2, replica_groups=mesh['y'=4,'zl'=8,'zh'=2,'x'=4,'c'=2] {'y'}, dimensions={0}, use_global_device_ids=true | all-gather | bytes 532480 | tf_op jit(solution)/shard_map/all_gather | solution.py:103
  31.9 9.4 %all-to-all-start.1 = ((bf16[8,16,832]{2,1,0:T(8,128)(2,1)}), bf16[8,16,832]{2,1,0:T(8,128)(2,1)S(1)}, u32[]{:S(2)}, u32[]{:S(2)}) async-start(bf16[8,16,832]{2,1,0:T(8,128)(2,1)} %pad_maximum_fusion.1), calls=%async_computation.1 | async-start | bytes 458752 | tf_op jit(solution)/shard_map/all_to_all | solution.py:18
  41.3 7.9 %collective-permute-start = (bf16[2,320,256]{2,1,0:T(8,128)(2,1)S(1)}, bf16[2,320,256]{2,1,0:T(8,128)(2,1)S(1)}, u32[]{:S(2)}, u32[]{:S(2)}) collective-permute-start(bf16[2,320,256]{2,1,0:T(8,128)(2,1)S(1)} %copy-done.3), channel_id=1, source_target_pairs={{0,8},{8,0},{1,9},{9,1},{2,10},{10,2},{3,11},{11,3},{4,12},{12,4},... | collective-permute-start | bytes 983048 | tf_op jit(solution)/shard_map/ppermute | solution.py:99
  49.3 37.8 %collective-permute-done = bf16[2,320,256]{2,1,0:T(8,128)(2,1)S(1)} collective-permute-done((bf16[2,320,256]{2,1,0:T(8,128)(2,1)S(1)}, bf16[2,320,256]{2,1,0:T(8,128)(2,1)S(1)}, u32[]{:S(2)}, u32[]{:S(2)}) %collective-permute-start) | collective-permute-done | bytes 327712 | tf_op jit(solution)/shard_map/ppermute | solution.py:99
  87.9 9.9 %all_to_all.35 = bf16[8,8,320]{2,1,0:T(8,128)(2,1)S(1)} all-to-all(bf16[8,8,320]{2,1,0:T(8,128)(2,1)S(1)} %bitcast.161), channel_id=1, replica_groups=mesh['y'=4,'zl'=8,'zh'=2,'x'=4,'c'=2] {'x','c'}, dimensions={0} | all-to-all | bytes 81920 | tf_op jit(solution)/shard_map/all_to_all | solution.py:18
  98.5 7.5 %all-to-all-start.3 = ((bf16[16,8,320]{2,1,0:T(8,128)(2,1)}), bf16[16,8,320]{2,1,0:T(8,128)(2,1)S(1)}, u32[]{:S(2)}, u32[]{:S(2)}) async-start(bf16[16,8,320]{2,1,0:T(8,128)(2,1)} %broadcast_in_dim.14), calls=%async_computation.3 | async-start | bytes 196608 | tf_op jit(solution)/shard_map/all_to_all | solution.py:18
  106.3 3.3 %collective-permute-start.1 = (bf16[2,2,320,256]{3,2,1,0:T(8,128)(2,1)S(1)}, bf16[2,2,320,256]{3,2,1,0:T(8,128)(2,1)}, u32[]{:S(2)}, u32[]{:S(2)}) collective-permute-start(bf16[2,2,320,256]{3,2,1,0:T(8,128)(2,1)S(1)} %pad_maximum_fusion.refs_0_), channel_id=1, source_target_pairs={{0,2},{2,4},{4,6},{6,0},{1,3},{3,5},{5,7},{7,1},{8,10},{10,12},{12... | collective-permute-start | bytes 1966088 | tf_op jit(solution)/shard_map/ppermute | solution.py:128
  109.6 4.3 %collective-permute-start.2 = (bf16[2,2,320,256]{3,2,1,0:T(8,128)(2,1)S(1)}, bf16[2,2,320,256]{3,2,1,0:T(8,128)(2,1)}, u32[]{:S(2)}, u32[]{:S(2)}) collective-permute-start(bf16[2,2,320,256]{3,2,1,0:T(8,128)(2,1)S(1)} %pad_maximum_fusion.refs_0_), channel_id=1, source_target_pairs={{0,4},{2,6},{4,0},{6,2},{1,5},{3,7},{5,1},{7,3},{8,12},{10,14},{12... | collective-permute-start | bytes 1966088 | tf_op jit(solution)/shard_map/ppermute | solution.py:128
  113.9 3.1 %collective-permute-start.3 = (bf16[2,2,320,256]{3,2,1,0:T(8,128)(2,1)S(1)}, bf16[2,2,320,256]{3,2,1,0:T(8,128)(2,1)}, u32[]{:S(2)}, u32[]{:S(2)}) collective-permute-start(bf16[2,2,320,256]{3,2,1,0:T(8,128)(2,1)S(1)} %pad_maximum_fusion.refs_0_), channel_id=1, source_target_pairs={{0,6},{2,0},{4,2},{6,4},{1,7},{3,1},{5,3},{7,5},{8,14},{10,8},{12,... | collective-permute-start | bytes 1966088 | tf_op jit(solution)/shard_map/ppermute | solution.py:128
  117.0 3.6 %all-to-all-done.3 = bf16[16,8,320]{2,1,0:T(8,128)(2,1)S(1)} async-done(((bf16[16,8,320]{2,1,0:T(8,128)(2,1)}), bf16[16,8,320]{2,1,0:T(8,128)(2,1)S(1)}, u32[]{:S(2)}, u32[]{:S(2)}) %all-to-all-start.3) | async-done | bytes 81952 | tf_op jit(solution)/shard_map/all_to_all | solution.py:18
  122.3 6.3 %all-to-all-start.4 = ((bf16[8,16,896]{2,1,0:T(8,128)(2,1)}), bf16[8,16,896]{2,1,0:T(8,128)(2,1)S(1)}, u32[]{:S(2)}, u32[]{:S(2)}) async-start(bf16[8,16,896]{2,1,0:T(8,128)(2,1)} %broadcast_in_dim.17), calls=%async_computation.4 | async-start | bytes 458752 | tf_op jit(solution)/shard_map/all_to_all | solution.py:18
  128.6 3.0 %collective-permute-start.4 = (bf16[2,2,320,256]{3,2,1,0:T(8,128)(2,1)S(1)}, bf16[2,2,320,256]{3,2,1,0:T(8,128)(2,1)}, u32[]{:S(2)}, u32[]{:S(2)}) collective-permute-start(bf16[2,2,320,256]{3,2,1,0:T(8,128)(2,1)S(1)} %pad_maximum_fusion.refs_0_), channel_id=1, source_target_pairs={{0,1},{1,0},{2,3},{3,2},{4,5},{5,4},{6,7},{7,6},{8,9},{9,8},{10,11... | collective-permute-start | bytes 1966088 | tf_op jit(solution)/shard_map/ppermute | solution.py:152
  131.6 1.9 collective-permute-start.5
  133.5 7.6 %collective-permute-done.2.refs_2_ = bf16[2,2,320,256]{3,2,1,0:T(8,128)(2,1)} collective-permute-done((bf16[2,2,320,256]{3,2,1,0:T(8,128)(2,1)S(1)}, bf16[2,2,320,256]{3,2,1,0:T(8,128)(2,1)}, u32[]{:S(2)}, u32[]{:S(2)}) %collective-permute-start.2) | collective-permute-done | bytes 655392 | tf_op jit(solution)/shard_map/ppermute | solution.py:128
  141.1 3.1 %collective-permute-start.6 = (bf16[2,2,320,256]{3,2,1,0:T(8,128)(2,1)}, bf16[2,2,320,256]{3,2,1,0:T(8,128)(2,1)}, u32[]{:S(2)}, u32[]{:S(2)}) collective-permute-start(bf16[2,2,320,256]{3,2,1,0:T(8,128)(2,1)} %collective-permute-done.2.refs_2_), channel_id=1, source_target_pairs={{0,1},{1,0},{2,3},{3,2},{4,5},{5,4},{6,7},{7,6},{8,9},{9,8},{10,11... | collective-permute-start | bytes 1966088 | tf_op jit(solution)/shard_map/ppermute | solution.py:152
  144.2 1.9 collective-permute-start.7
  146.1 1.0 broadcast_in_dim.19
  147.2 4.2 %all-to-all-start.5 = ((bf16[4,128,896]{2,1,0:T(8,128)(2,1)}), bf16[4,128,896]{2,1,0:T(8,128)(2,1)}, u32[]{:S(2)}, u32[]{:S(2)}) async-start(bf16[4,128,896]{2,1,0:T(8,128)(2,1)} %broadcast_in_dim.19), calls=%async_computation.5 | async-start | bytes 1835008 | tf_op jit(solution)/shard_map/all_to_all | solution.py:18
  151.5 0.8 slice.186.refs_10_
  152.4 1.0 copy-done.2
  153.4 6.1 %base_product.1 = (bf16[2,320,256]{2,1,0:T(8,128)(2,1)}, bf16[2,64,320]{2,1,0:T(8,128)(2,1)}) custom-call(s32[16]{0:T(128)S(1)} %stack.113.order, bf16[2,2,320,256]{3,2,1,0:T(8,128)(2,1)S(1)} %pad_maximum_fusion.refs_0_, bf16[2,2,320,256]{3,2,1,0:T(8,128)(2,1)} %collective-permute-done.1.refs_1_, bf16[2,2,320,256]{3,2,1,0:T(8,128)(2,1)} %collective-permute-done.2.refs_2_, ...), custom_call_target="tpu_custom_call" | custom-call | flops 2000000000 | bytes 9000000 | tf_op jit(solution)/shard_map/base_product/pallas_call | solution.py:58
  159.5 5.2 %all-to-all-done.5 = bf16[4,128,896]{2,1,0:T(8,128)(2,1)} async-done(((bf16[4,128,896]{2,1,0:T(8,128)(2,1)}), bf16[4,128,896]{2,1,0:T(8,128)(2,1)}, u32[]{:S(2)}, u32[]{:S(2)}) %all-to-all-start.5) | async-done | bytes 917536 | tf_op jit(solution)/shard_map/all_to_all | solution.py:18
  164.8 2.2 %fusion.32 = s32[64]{0:T(128)S(1)} fusion(bf16[64,8,896]{2,1,0:T(8,128)(2,1)} %bitcast.25), kind=kLoop, calls=%fused_computation.57 | loop fusion | flops 64 | bytes 384 | tf_op jit(solution)/shard_map/convert_element_type | solution.py:159
  167.0 1.1 slice.129
  168.1 1.0 slice.130
  169.3 0.9 convolution_convert_fusion.8
  171.5 14.4 %all-to-all-start.6 = ((f32[16,16,128]{2,1,0:T(8,128)}), f32[16,16,128]{2,1,0:T(8,128)S(1)}, u32[]{:S(2)}, u32[]{:S(2)}) async-start(f32[16,16,128]{2,1,0:T(8,128)} %broadcast_in_dim.20), calls=%async_computation.6 | async-start | bytes 262144 | tf_op jit(solution)/shard_map/all_to_all | solution.py:18
  185.9 0.9 fusion.25
  187.3 13.4 %all-to-all-done.6 = f32[16,16,128]{2,1,0:T(8,128)S(1)} async-done(((f32[16,16,128]{2,1,0:T(8,128)}), f32[16,16,128]{2,1,0:T(8,128)S(1)}, u32[]{:S(2)}, u32[]{:S(2)}) %all-to-all-start.6) | async-done | bytes 131104 | tf_op jit(solution)/shard_map/all_to_all | solution.py:18
  (103 shorter events, 15.4 us)
Async XLA Ops:
  0.6 16.5 %copy-start = (bf16[1024,256]{1,0:T(8,128)(2,1)S(1)}, bf16[1024,256]{1,0:T(8,128)(2,1)}, u32[]{:S(2)}) copy-start(bf16[1024,256]{1,0:T(8,128)(2,1)} %param.17) | copy-start | bytes 1572868
  2.0 28.2 %all-to-all-start = ((s32[8,2,128]{2,1,0:T(2,128)}), s32[8,2,128]{2,1,0:T(2,128)S(1)}, u32[]{:S(2)}, u32[]{:S(2)}) async-start(s32[8,2,128]{2,1,0:T(2,128)} %broadcast_in_dim_broadcast_in_dim_broadcast_in_dim.2), calls=%async_computation | async-start | bytes 16384 | tf_op jit(solution)/shard_map/all_to_all | solution.py:18
  14.8 15.8 %copy-start.9 = (bf16[8,8,256]{2,0,1:T(8,128)(2,1)}, bf16[8,8,256]{2,0,1:T(8,128)(2,1)S(1)}, u32[]{:S(2)}) copy-start(bf16[8,8,256]{2,0,1:T(8,128)(2,1)S(1)} %copy.77) | copy-start | bytes 98308
  15.6 15.6 %copy-start.11 = (bf16[8,8,256]{2,0,1:T(8,128)(2,1)}, bf16[8,8,256]{2,0,1:T(8,128)(2,1)S(1)}, u32[]{:S(2)}) copy-start(bf16[8,8,256]{2,0,1:T(8,128)(2,1)S(1)} %copy.78) | copy-start | bytes 98308
  16.3 14.8 %copy-start.13 = (bf16[8,8,256]{2,0,1:T(8,128)(2,1)}, bf16[8,8,256]{2,0,1:T(8,128)(2,1)S(1)}, u32[]{:S(2)}) copy-start(bf16[8,8,256]{2,0,1:T(8,128)(2,1)S(1)} %copy.84) | copy-start | bytes 98308
  18.5 22.8 %copy-start.3 = (bf16[2,320,256]{2,1,0:T(8,128)(2,1)S(1)}, bf16[2,320,256]{2,1,0:T(8,128)(2,1)}, u32[]{:S(2)}) copy-start(bf16[2,320,256]{2,1,0:T(8,128)(2,1)} %param.25) | copy-start | bytes 983044
  18.5 30.7 %copy-start.16 = (s32[2]{0:T(128)S(1)}, s32[2]{0:T(128)}, u32[]{:S(2)}) copy-start(s32[2]{0:T(128)} %param.16) | copy-start | bytes 28
  18.6 68.9 %copy-start.7 = (f32[2,4,8,8,240]{4,3,0,2,1:T(8,128)}, f32[2,4,8,8,240]{4,3,0,2,1:T(8,128)S(1)}, u32[]{:S(2)}) copy-start(f32[2,4,8,8,240]{4,3,0,2,1:T(8,128)S(1)} %broadcast_add_fusion) | copy-start | bytes 1474564
  18.6 68.9 %copy-start.5 = (bf16[2,320,256]{2,1,0:T(8,128)(2,1)S(1)}, bf16[2,320,256]{2,1,0:T(8,128)(2,1)}, u32[]{:S(2)}) copy-start(bf16[2,320,256]{2,1,0:T(8,128)(2,1)} %param.26) | copy-start | bytes 983044
  18.7 69.0 %copy-start.8 = (bf16[2,320,64]{1,2,0:T(8,128)(2,1)S(1)}, bf16[2,320,64]{1,2,0:T(8,128)(2,1)}, u32[]{:S(2)}) copy-start(bf16[2,320,64]{1,2,0:T(8,128)(2,1)} %param.27) | copy-start | bytes 245764
  30.7 75.3 %copy-start.15 = (s32[2]{0:T(128)S(1)}, s32[2]{0:T(128)}, u32[]{:S(2)}) copy-start(s32[2]{0:T(128)} %param.15) | copy-start | bytes 28
  31.9 55.2 %all-to-all-start.1 = ((bf16[8,16,832]{2,1,0:T(8,128)(2,1)}), bf16[8,16,832]{2,1,0:T(8,128)(2,1)S(1)}, u32[]{:S(2)}, u32[]{:S(2)}) async-start(bf16[8,16,832]{2,1,0:T(8,128)(2,1)} %pad_maximum_fusion.1), calls=%async_computation.1 | async-start | bytes 458752 | tf_op jit(solution)/shard_map/all_to_all | solution.py:18
  41.3 45.8 %collective-permute-start = (bf16[2,320,256]{2,1,0:T(8,128)(2,1)S(1)}, bf16[2,320,256]{2,1,0:T(8,128)(2,1)S(1)}, u32[]{:S(2)}, u32[]{:S(2)}) collective-permute-start(bf16[2,320,256]{2,1,0:T(8,128)(2,1)S(1)} %copy-done.3), channel_id=1, source_target_pairs={{0,8},{8,0},{1,9},{9,1},{2,10},{10,2},{3,11},{11,3},{4,12},{12,4},... | collective-permute-start | bytes 983048 | tf_op jit(solution)/shard_map/ppermute | solution.py:99
  98.5 22.1 %all-to-all-start.3 = ((bf16[16,8,320]{2,1,0:T(8,128)(2,1)}), bf16[16,8,320]{2,1,0:T(8,128)(2,1)S(1)}, u32[]{:S(2)}, u32[]{:S(2)}) async-start(bf16[16,8,320]{2,1,0:T(8,128)(2,1)} %broadcast_in_dim.14), calls=%async_computation.3 | async-start | bytes 196608 | tf_op jit(solution)/shard_map/all_to_all | solution.py:18
  106.3 25.3 %collective-permute-start.1 = (bf16[2,2,320,256]{3,2,1,0:T(8,128)(2,1)S(1)}, bf16[2,2,320,256]{3,2,1,0:T(8,128)(2,1)}, u32[]{:S(2)}, u32[]{:S(2)}) collective-permute-start(bf16[2,2,320,256]{3,2,1,0:T(8,128)(2,1)S(1)} %pad_maximum_fusion.refs_0_), channel_id=1, source_target_pairs={{0,2},{2,4},{4,6},{6,0},{1,3},{3,5},{5,7},{7,1},{8,10},{10,12},{12... | collective-permute-start | bytes 1966088 | tf_op jit(solution)/shard_map/ppermute | solution.py:128
  109.6 31.5 %collective-permute-start.2 = (bf16[2,2,320,256]{3,2,1,0:T(8,128)(2,1)S(1)}, bf16[2,2,320,256]{3,2,1,0:T(8,128)(2,1)}, u32[]{:S(2)}, u32[]{:S(2)}) collective-permute-start(bf16[2,2,320,256]{3,2,1,0:T(8,128)(2,1)S(1)} %pad_maximum_fusion.refs_0_), channel_id=1, source_target_pairs={{0,4},{2,6},{4,0},{6,2},{1,5},{3,7},{5,1},{7,3},{8,12},{10,14},{12... | collective-permute-start | bytes 1966088 | tf_op jit(solution)/shard_map/ppermute | solution.py:128
  113.9 30.3 %collective-permute-start.3 = (bf16[2,2,320,256]{3,2,1,0:T(8,128)(2,1)S(1)}, bf16[2,2,320,256]{3,2,1,0:T(8,128)(2,1)}, u32[]{:S(2)}, u32[]{:S(2)}) collective-permute-start(bf16[2,2,320,256]{3,2,1,0:T(8,128)(2,1)S(1)} %pad_maximum_fusion.refs_0_), channel_id=1, source_target_pairs={{0,6},{2,0},{4,2},{6,4},{1,7},{3,1},{5,3},{7,5},{8,14},{10,8},{12,... | collective-permute-start | bytes 1966088 | tf_op jit(solution)/shard_map/ppermute | solution.py:128
  120.6 0.6 copy-start.6
  121.2 31.1 %copy-start.1 = (bf16[4096,256]{1,0:T(8,128)(2,1)S(1)}, bf16[4096,256]{1,0:T(8,128)(2,1)}, u32[]{:S(2)}) copy-start(bf16[4096,256]{1,0:T(8,128)(2,1)} %refs_8_.1) | copy-start | bytes 6291460
  122.3 23.9 %all-to-all-start.4 = ((bf16[8,16,896]{2,1,0:T(8,128)(2,1)}), bf16[8,16,896]{2,1,0:T(8,128)(2,1)S(1)}, u32[]{:S(2)}, u32[]{:S(2)}) async-start(bf16[8,16,896]{2,1,0:T(8,128)(2,1)} %broadcast_in_dim.17), calls=%async_computation.4 | async-start | bytes 458752 | tf_op jit(solution)/shard_map/all_to_all | solution.py:18
  128.6 23.8 %collective-permute-start.4 = (bf16[2,2,320,256]{3,2,1,0:T(8,128)(2,1)S(1)}, bf16[2,2,320,256]{3,2,1,0:T(8,128)(2,1)}, u32[]{:S(2)}, u32[]{:S(2)}) collective-permute-start(bf16[2,2,320,256]{3,2,1,0:T(8,128)(2,1)S(1)} %pad_maximum_fusion.refs_0_), channel_id=1, source_target_pairs={{0,1},{1,0},{2,3},{3,2},{4,5},{5,4},{6,7},{7,6},{8,9},{9,8},{10,11... | collective-permute-start | bytes 1966088 | tf_op jit(solution)/shard_map/ppermute | solution.py:152
  131.6 20.7 %collective-permute-start.5 = (bf16[2,2,320,256]{3,2,1,0:T(8,128)(2,1)}, bf16[2,2,320,256]{3,2,1,0:T(8,128)(2,1)}, u32[]{:S(2)}, u32[]{:S(2)}) collective-permute-start(bf16[2,2,320,256]{3,2,1,0:T(8,128)(2,1)} %collective-permute-done.1.refs_1_), channel_id=1, source_target_pairs={{0,1},{1,0},{2,3},{3,2},{4,5},{5,4},{6,7},{7,6},{8,9},{9,8},{10,11... | collective-permute-start | bytes 1966088 | tf_op jit(solution)/shard_map/ppermute | solution.py:152
  141.1 11.3 %collective-permute-start.6 = (bf16[2,2,320,256]{3,2,1,0:T(8,128)(2,1)}, bf16[2,2,320,256]{3,2,1,0:T(8,128)(2,1)}, u32[]{:S(2)}, u32[]{:S(2)}) collective-permute-start(bf16[2,2,320,256]{3,2,1,0:T(8,128)(2,1)} %collective-permute-done.2.refs_2_), channel_id=1, source_target_pairs={{0,1},{1,0},{2,3},{3,2},{4,5},{5,4},{6,7},{7,6},{8,9},{9,8},{10,11... | collective-permute-start | bytes 1966088 | tf_op jit(solution)/shard_map/ppermute | solution.py:152
  144.2 8.2 %collective-permute-start.7 = (bf16[2,2,320,256]{3,2,1,0:T(8,128)(2,1)}, bf16[2,2,320,256]{3,2,1,0:T(8,128)(2,1)}, u32[]{:S(2)}, u32[]{:S(2)}) collective-permute-start(bf16[2,2,320,256]{3,2,1,0:T(8,128)(2,1)} %collective-permute-done.3.refs_3_), channel_id=1, source_target_pairs={{0,1},{1,0},{2,3},{3,2},{4,5},{5,4},{6,7},{7,6},{8,9},{9,8},{10,11... | collective-permute-start | bytes 1966088 | tf_op jit(solution)/shard_map/ppermute | solution.py:152
  147.2 17.6 %all-to-all-start.5 = ((bf16[4,128,896]{2,1,0:T(8,128)(2,1)}), bf16[4,128,896]{2,1,0:T(8,128)(2,1)}, u32[]{:S(2)}, u32[]{:S(2)}) async-start(bf16[4,128,896]{2,1,0:T(8,128)(2,1)} %broadcast_in_dim.19), calls=%async_computation.5 | async-start | bytes 1835008 | tf_op jit(solution)/shard_map/all_to_all | solution.py:18
  152.4 1.0 copy-start.2
  153.4 15.7 %copy-start.14 = (bf16[8,8,256]{2,0,1:T(8,128)(2,1)S(1)}, bf16[8,8,256]{2,0,1:T(8,128)(2,1)}, u32[]{:S(2)}) copy-start(bf16[8,8,256]{2,0,1:T(8,128)(2,1)} %copy-done.13) | copy-start | bytes 98308
  159.5 10.9 %copy-start.10 = (bf16[8,8,256]{2,0,1:T(8,128)(2,1)S(1)}, bf16[8,8,256]{2,0,1:T(8,128)(2,1)}, u32[]{:S(2)}) copy-start(bf16[8,8,256]{2,0,1:T(8,128)(2,1)} %copy-done.9) | copy-start | bytes 98308
  159.5 10.9 %copy-start.12 = (bf16[8,8,256]{2,0,1:T(8,128)(2,1)S(1)}, bf16[8,8,256]{2,0,1:T(8,128)(2,1)}, u32[]{:S(2)}) copy-start(bf16[8,8,256]{2,0,1:T(8,128)(2,1)} %copy-done.11) | copy-start | bytes 98308
  159.5 27.3 %copy-start.4 = (bf16[240,1024]{1,0:T(8,128)(2,1)S(1)}, bf16[240,1024]{1,0:T(8,128)(2,1)}, u32[]{:S(2)}) copy-start(bf16[240,1024]{1,0:T(8,128)(2,1)} %param.14) | copy-start | bytes 1474564
  171.5 29.2 %all-to-all-start.6 = ((f32[16,16,128]{2,1,0:T(8,128)}), f32[16,16,128]{2,1,0:T(8,128)S(1)}, u32[]{:S(2)}, u32[]{:S(2)}) async-start(f32[16,16,128]{2,1,0:T(8,128)} %broadcast_in_dim.20), calls=%async_computation.6 | async-start | bytes 262144 | tf_op jit(solution)/shard_map/all_to_all | solution.py:18

commit v3 on v1

v3 whole, which is shorter than its diff:
```python
import functools

import jax
import jax.numpy as jnp
from jax import lax
from jax.experimental import pallas as pl
from jax.experimental.pallas import tpu as pltpu
from jax.sharding import Mesh, PartitionSpec as P

bf16, f32 = jnp.bfloat16, jnp.float32
exact = lax.Precision.HIGHEST
scale = 2.0


def mm(a, b, dims=((1,), (0,)), precision=None):
    return lax.dot_general(a, b, (dims, ((), ())), precision=precision, preferred_element_type=f32)


def mm_nt(a, b, precision=None):
    return mm(a, b, ((1,), (1,)), precision)


def iota(shape, dim):
    return lax.broadcasted_iota(jnp.int32, shape, dim)


def silu_grad(pre):
    sig = jax.nn.sigmoid(pre)
    return sig * (1.0 + pre * (1.0 - sig))


def swap(blocks, axes):
    return lax.all_to_all(blocks, axes, 0, 0, tiled=True)


def spread(block, axes, n):
    return swap(jnp.broadcast_to(block[None], (n,) + block.shape), axes)


def local(body, outs, args, scalars=0, scratch=(), flops=1_000_000, name=None):
    in_vmem = pl.BlockSpec(memory_space=pltpu.VMEM)
    in_smem = pl.BlockSpec(memory_space=pltpu.SMEM)
    return pl.pallas_call(
        body,
        out_shape=tuple(jax.ShapeDtypeStruct(s, d) for s, d in outs),
        in_specs=[in_smem] * scalars + [in_vmem] * (len(args) - scalars),
        out_specs=tuple(in_vmem for _ in outs),
        scratch_shapes=list(scratch),
        compiler_params=pltpu.CompilerParams(vmem_limit_bytes=32 * 2**20),
        cost_estimate=pl.CostEstimate(flops=flops, bytes_accessed=100_000, transcendentals=0),
        name=name,
    )(*args)


def tables_kernel(ny, nz, place, task_embed, w_in, module, lat_line, lat_own, sg_own):
    latents = w_in.shape[1]
    rows = latents // (ny * nz)
    rank = lat_own.shape[2] // rows
    y, z = place[0], place[1]
    pre = mm(task_embed[...], w_in[...])
    q = iota((latents, lat_line.shape[2]), 1)
    line = iota((latents, lat_line.shape[2]), 0) == (
        (q // (rows * rank)) * (nz * rows) + z * rows + (q // rank) % rows
    )
    line = line.astype(f32).astype(bf16)
    first = (y * nz + z) * rows
    q = iota((latents, lat_own.shape[2]), 1)
    own = (iota((latents, lat_own.shape[2]), 0) == first + q // rank).astype(f32).astype(bf16)
    mine = (iota((rows, latents), 1) == first + iota((rows, latents), 0)).astype(f32)
    for m in range(2):
        p = pre + module[m : m + 1, :]
        lat = (p * jax.nn.sigmoid(p)).astype(bf16)
        lat_line[m] = mm(lat, line).astype(bf16)
        lat_own[m] = mm(lat, own).astype(bf16)
        sg_own[m * rows : (m + 1) * rows, :] = mm_nt(mine, silu_grad(p), exact)


def part_kernel(split, rank, ids, lat_line, w_line, part):
    n, k = part.shape[0], w_line.shape[0]
    tasks = lat_line.shape[1]
    at = ids[...].reshape(n, ids.shape[2])[:, :1]
    pick = (iota((n, tasks), 1) == at).astype(f32).astype(bf16)
    same = iota((n, k), 0) % rank == iota((n, k), 1) % rank
    for m, cols in enumerate((slice(0, split), slice(split, None))):
        spread_lat = jnp.where(same, mm(pick, lat_line[m]), 0.0).astype(bf16)
        part[:, cols] = mm(spread_lat, w_line[:, cols]).astype(bf16)


def row_weight(lengths, s, length):
    n = jnp.full((1, length), lengths[s], jnp.int32)
    return jnp.where(iota((1, length), 1) < n, scale / n.astype(f32), 0.0)


def low_kernel(wq, wv, rank, lengths, got, hidden, grad_q, grad_vt, adapters, low):
    total = got[0].astype(f32)
    for i in range(1, got.shape[0]):
        total += got[i].astype(f32)
    adapters[...] = total.astype(bf16)
    total = total.astype(bf16).astype(f32)
    for s in range(hidden.shape[0]):
        own = total[s * rank : (s + 1) * rank, :]
        a = jnp.concatenate([own[:, :wq], own[:, 2 * wq : 3 * wq]], axis=0).astype(bf16)
        b_q, b_v = own[:, wq : 2 * wq].astype(bf16), own[:, 3 * wq :].astype(bf16)
        low[s, 0] = mm_nt(a, hidden[s])
        back = jnp.concatenate([mm_nt(b_q, grad_q[s]), mm(b_v, grad_vt[s])], axis=0)
        low[s, 1] = back * row_weight(lengths, s, hidden.shape[1])


def adapter_grad_kernel(wq, wv, rank, lengths, ids, low, hidden, grad_q, grad_vt, out, rows):
    for s in range(hidden.shape[0]):
        at = slice(s * rank, (s + 1) * rank)
        weight = row_weight(lengths, s, hidden.shape[1])
        du = jnp.concatenate([low[4 * s + 2], low[4 * s + 3]], axis=0).astype(bf16)
        d_a = mm(du, hidden[s])
        rows[at, :wq] = d_a[:rank]
        rows[at, wq : 2 * wq] = mm((low[4 * s] * weight).astype(bf16), grad_q[s])
        rows[at, 2 * wq : 3 * wq] = d_a[rank:]
        rows[at, 3 * wq : 3 * wq + wv] = mm_nt((low[4 * s + 1] * weight).astype(bf16), grad_vt[s])
        rest = rows.shape[1] - 3 * wq - wv
        rows[at, 3 * wq + wv :] = jnp.full((rank, rest), ids[s], jnp.int32).astype(f32)
    done = rows[...].astype(bf16)
    for i in range(out.shape[0]):
        out[i] = done


def latent_grad_kernel(split, width, rank, d_all, weights, out):
    n, k = d_all.shape[0], weights.shape[0]
    same = iota((n, k), 0) % rank == iota((n, k), 1) % rank
    fold = (iota((k // rank, k), 0) == iota((k // rank, k), 1) // rank).astype(f32)
    parts = []
    for cols in (slice(0, split), slice(split, width)):
        full = jnp.where(same, mm_nt(d_all[:, cols], weights[:, cols]), 0.0)
        by_batch = jnp.sum(full.reshape(n // rank, rank, k), axis=1)
        parts.append(mm_nt(fold, by_batch, exact))
    both = jnp.concatenate(parts, axis=0)
    pad = out.shape[2] - both.shape[1]
    both = jnp.concatenate([both, jnp.zeros((both.shape[0], pad), f32)], axis=1)
    for i in range(out.shape[0]):
        out[i] = both


def head_grad_kernel(wq, wv, rank, d_all, lat_own, sg_own, task_embed, g_aq, g_bq, g_av, g_bv, sg_all, embeds):
    n, k = d_all.shape[0], lat_own.shape[2]
    tasks = lat_own.shape[1]
    width = 3 * wq + wv
    tail = d_all[:, 3 * wq :].astype(f32)
    pick = (iota((n, tasks), 1).astype(f32) == tail[:, wv : wv + 1]).astype(f32)
    same = iota((n, k), 0) % rank == iota((n, k), 1) % rank
    lat = [jnp.where(same, mm(pick.astype(bf16), lat_own[m]), 0.0).astype(bf16) for m in range(2)]
    g_q = mm(lat[0], d_all[:, : 2 * wq], ((0,), (0,)))
    g_aq[...], g_bq[...] = g_q[:, :wq], g_q[:, wq:]
    g_v = mm(lat[1], d_all[:, 2 * wq : width], ((0,), (0,)))
    g_av[...], g_bv[...] = g_v[:, :wq], g_v[:, wq:]
    one = jnp.where(iota((n, tasks), 0) % rank == 0, pick, 0.0)
    one = jnp.sum(one.reshape(n // rank, rank, tasks), axis=1)
    sg_all[...] = mm_nt(sg_own[...], one, exact)
    embeds[...] = mm(one.astype(bf16), task_embed[...]).astype(bf16)


def trunk_kernel(got, sg_all, embeds, g_in, g_mod):
    total = got[0]
    for i in range(1, got.shape[0]):
        total += got[i]
    rows, batches = sg_all.shape
    d_pre = total[:, :batches] * sg_all[...]
    both = d_pre[: rows // 2] + d_pre[rows // 2 :]
    hi = both.astype(bf16)
    lo = (both - hi.astype(f32)).astype(bf16)
    g_in[...] = mm(hi, embeds[...]) + mm(lo, embeds[...])
    g_mod[...] = jnp.sum(d_pre, axis=1, keepdims=True)


def base_kernel(order, *refs):
    near = refs[:8]
    base_q, base_vt, part_q, part_vt, acc_q, acc_v, out = refs[8:]
    seqs, length, wq = near[0].shape
    for n, block in enumerate(near):
        h = block[...].reshape(seqs * length, wq)
        at = pl.ds(pl.multiple_of(order[2 * n] * wq, wq), wq)
        far = pl.ds(pl.multiple_of(order[2 * n + 1] * wq, wq), wq)
        adds = mm(h, base_q[at, :]), mm_nt(h, base_vt[:, at])
        partner = jnp.concatenate([mm(h, part_q[far, :]), mm_nt(h, part_vt[:, far])], axis=1)
        if n == 0:
            acc_q[...], acc_v[...] = adds
            both = partner
        else:
            acc_q[...] += adds[0]
            acc_v[...] += adds[1]
            both += partner
    out[...] = both.astype(bf16)


def out_kernel(rank, acc_q, acc_v, got, low, ad, q_out, vt_out):
    seqs, length, wq = q_out.shape
    both = ad[...].astype(f32)
    first = ((0,), (0,))
    for s in range(seqs):
        own = slice(s * length, (s + 1) * length)
        b = both[s * rank : (s + 1) * rank, :].astype(bf16)
        low_q = mm(low[4 * s].astype(bf16), b[:, wq : 2 * wq], first)
        low_v = mm(b[:, 3 * wq :], low[4 * s + 1].astype(bf16), first)
        got_q, got_v = got[own, :wq].astype(f32), got[own, wq:].astype(f32)
        q_out[s] = (acc_q[own, :] + got_q + scale * low_q).astype(bf16)
        vt_out[s] = ((acc_v[own, :] + got_v).T + scale * low_v).astype(bf16)


def on_device(
    task_embed,
    task_ids,
    seq_lengths,
    w_in,
    module_embed,
    wa_q,
    wb_q,
    wa_v,
    wb_v,
    base_q,
    base_v,
    hidden_in,
    grad_q,
    grad_v,
):
    ny, nz, nh, nx, nc = (lax.axis_size(a) for a in ("y", "zl", "zh", "x", "c"))
    y, zl, zh, x, c = (lax.axis_index(a) for a in ("y", "zl", "zh", "x", "c"))
    xc, head = ("x", "c"), ("zh", "x", "c")
    seqs, length, wq = hidden_in.shape
    rows, rank, _ = wa_q.shape
    wv = wb_v.shape[2]
    tasks, emb = task_embed.shape
    split, width = 2 * wq, 3 * wq + wv
    batches = seqs * ny * nz
    grad_vt = grad_v.swapaxes(1, 2)

    ids_rows = jnp.broadcast_to(task_ids[:, None, None], (seqs, rank, 128)).reshape(seqs * rank, 128)
    ids_line = spread(ids_rows, "zl", nz)
    other = lax.ppermute(hidden_in, "zh", [(0, 1), (1, 0)])
    packed = jnp.concatenate([wa_q, wb_q, wa_v, wb_v], axis=2).reshape(rows * rank, width)
    w_line = lax.all_gather(packed, "y", axis=0, tiled=True)
    lat_line, lat_own, sg_own = local(
        functools.partial(tables_kernel, ny, nz),
        [((2, tasks, ny * rows * rank), bf16), ((2, tasks, rows * rank), bf16), ((2 * rows, tasks), f32)],
        (jnp.stack([y, zl]).astype(jnp.int32), task_embed, w_in, module_embed),
        scalars=1,
        name="tables",
    )
    turns = [[(i, (i + k) % nx) for i in range(nx)] for k in range(1, nx)]
    near = [lax.ppermute(hidden_in, "x", t) for t in turns]
    ids_line, w_line, other, *near = lax.optimization_barrier((ids_line, w_line, other, *near))
    far = [lax.ppermute(other, "x", t) for t in turns]

    (part,) = local(
        functools.partial(part_kernel, split, rank),
        [((nz * seqs * rank, width), bf16)],
        (ids_line, lat_line, w_line),
        name="adapter_parts",
    )
    got = swap(part.reshape(nz, seqs * rank, width), "zl")
    adapters, low = local(
        functools.partial(low_kernel, wq, wv, rank),
        [((seqs * rank, width), bf16), ((seqs, 2, 2 * rank, length), f32)],
        (seq_lengths, got, hidden_in, grad_q, grad_vt),
        scalars=1,
        flops=30_000_000_000,
        name="low_rank",
    )

    low = swap(low.reshape(nx * nc, seqs * 4 * rank // (nx * nc), length), xc)
    low, *far = lax.optimization_barrier((low, *far))
    low = jnp.sum(low, axis=0).astype(bf16)
    low = spread(low, head, nh * nx * nc)
    low = jnp.sum(low.reshape(nh, 4 * seqs, rank, length).astype(f32), axis=0)
    (d_own,) = local(
        functools.partial(adapter_grad_kernel, wq, wv, rank),
        [((nz, seqs * rank, width + 64), bf16)],
        (seq_lengths, task_ids, low, hidden_in, grad_q, grad_vt),
        scalars=2,
        scratch=[pltpu.VMEM((seqs * rank, width + 64), f32)],
        name="adapter_grads",
    )
    d_line = swap(d_own, "zl").reshape(nz * seqs * rank, width + 64)
    d_all = spread(d_line, "y", ny).reshape(batches * rank, width + 64)

    (d_lat,) = local(
        functools.partial(latent_grad_kernel, split, width, rank),
        [((nh * nx * nc, 2 * rows, 128), f32)],
        (d_all, packed),
        name="latent_grads",
    )
    d_lat = swap(d_lat, head)
    g_aq, g_bq, g_av, g_bv, sg_all, embeds = local(
        functools.partial(head_grad_kernel, wq, wv, rank),
        [((rows * rank, wq), f32)] * 3
        + [((rows * rank, wv), f32), ((2 * rows, batches), f32), ((batches, emb), bf16)],
        (d_all, lat_own, sg_own, task_embed),
        name="head_grads",
    )

    blocks = nh * nx
    pair = [(0, 1), (1, 0)]
    base_vt = base_v.T
    part_q = lax.dynamic_index_in_dim(base_q.reshape(blocks, nc, wq, wq), 1 - c, 1, keepdims=False)
    part_vt = lax.dynamic_index_in_dim(base_vt.reshape(wv, blocks, nc, wq), 1 - c, 2, keepdims=False)
    part_q = lax.ppermute(part_q.reshape(blocks * wq, wq), "c", pair)
    part_vt = lax.ppermute(part_vt.reshape(wv, blocks * wq), "c", pair)
    order = []
    for half in range(nh):
        for k in range(nx):
            block = (zh ^ half) * nx + lax.rem(x - k + nx, nx)
            order += [block * nc + c, block]
    acc_q, acc_v, given = local(
        base_kernel,
        [((seqs * length, wq), f32), ((seqs * length, wv), f32), ((seqs * length, wq + wv), bf16)],
        (
            jnp.stack(order).astype(jnp.int32),
            hidden_in,
            *near,
            other,
            *far,
            base_q,
            base_vt,
            part_q,
            part_vt,
        ),
        scalars=1,
        name="base_product",
    )
    q_out, vt_out = local(
        functools.partial(out_kernel, rank),
        [((seqs, length, wq), bf16), ((seqs, wv, length), bf16)],
        (acc_q, acc_v, lax.ppermute(given, "c", pair), low, adapters),
        name="outputs",
    )
    d_lat, sg_all, embeds, g_aq, q_out = lax.optimization_barrier((d_lat, sg_all, embeds, g_aq, q_out))
    g_in, g_mod = local(
        trunk_kernel, [((rows, emb), f32), ((2 * rows, 1), f32)], (d_lat, sg_all, embeds), name="trunk_grads"
    )

    def cube(g):
        return g.reshape(rows, rank, -1)

    return (
        q_out,
        vt_out.swapaxes(1, 2),
        cube(g_aq),
        cube(g_bq),
        cube(g_av),
        cube(g_bv),
        g_in.T,
        g_mod.reshape(2, rows),
    )


def solution(mesh):
    fine = Mesh(mesh.devices.reshape(4, 8, 2, 4, 2), ("y", "zl", "zh", "x", "c"))
    dp, head = ("y", "zl"), ("zh", "x", "c")
    rows_cols = P(dp, None, head)
    return jax.shard_map(
        on_device,
        mesh=fine,
        in_specs=(P(), P(dp), P(dp), P(), P())
        + (rows_cols,) * 4
        + (P(None, head),) * 2
        + (rows_cols,) * 3,
        out_specs=(rows_cols,) * 6 + (P(None, dp),) * 2,
        check_vma=False,
    )
```

time: 202 us -> 181 us (0.90)
  waiting for transfers between devices: 54.9 us -> 17.3 us
  starting transfers between devices: 65.5 us -> 91.4 us
  matrix products: 19 us -> 0 us
  Pallas kernels: 0 us -> 15.3 us
  between operations: 14.4 us -> 1.01 us
  blocking collectives: 20.6 us -> 32.3 us
  other arithmetic: 8.58 us -> 1.12 us
  local copies, waits for them, and re-layouts: 17.7 us -> 21.4 us
    ppermute x0 -> x9, starting transfers between devices: none -> 30.4 us  [the longest x3 10.5 us: on_device(): near = [lax.ppermute(hidden_in, 'x', t) for t in turns]]
    ppermute x1, waiting for transfers between devices: 19.9 us -> 0.01 us  [on_device(): other = lax.ppermute(hidden_in, 'zh', [(0, 1), (1, 0)])]
    dot_general x24 -> x0, matrix products: 19 us -> none  [the longest x22 15.9 us: dot(): return jnp.einsum(eq, a, b, preferred_element_type=f32)]
    all_to_all x7 -> x6, waiting for transfers between devices: 34.3 us -> 15.7 us  [swap(): return lax.all_to_all(blocks, axes, 0, 0, tiled=True)]
    pallas_call x0 -> x9, Pallas kernels: none -> 15.3 us  [local(): pl.pallas_call(body, out_shape=tuple((jax.ShapeDtypeStruct(s, d) for s, d...]
    all_to_all x7 -> x6, starting transfers between devices: 57.5 us -> 44.6 us  [swap(): return lax.all_to_all(blocks, axes, 0, 0, tiled=True)]
    all_gather x0 -> x1, blocking collectives: none -> 10.9 us  [on_device(): w_line = lax.all_gather(packed, 'y', axis=0, tiled=True)]
    ppermute x1, starting transfers between devices: 7.93 us -> 16.4 us  [on_device(): other = lax.ppermute(hidden_in, 'zh', [(0, 1), (1, 0)])]
  transfers between devices with their start and end apart: 10 -> 16, of which waited for: 7 -> 4; matrix products, arithmetic and copies ran while one was open for 18% -> 5% of each run, Pallas kernels for 0% -> 6%
where the time goes in v3:
time: 181 us; the launch traced here: 180 us
  starting transfers between devices  91.4 us (50%)
  blocking collectives  32.3 us (18%)
  local copies, waits for them, and re-layouts  21.4 us (12%)
  waiting for transfers between devices  17.3 us (10%)
  Pallas kernels  15.3 us (8%)
    all_to_all x6, starting transfers between devices, swap(): return lax.all_to_all(blocks, axes, 0, 0, tiled=True)  44.6 us
    all_to_all x1, blocking collectives, swap(): return lax.all_to_all(blocks, axes, 0, 0, tiled=True)  21.5 us
    ppermute x1, starting transfers between devices, on_device(): other = lax.ppermute(hidden_in, 'zh', [(0, 1), (1, 0)])  16.4 us
    all_to_all x6, waiting for transfers between devices, swap(): return lax.all_to_all(blocks, axes, 0, 0, tiled=True)  15.7 us
    pallas_call x9, Pallas kernels, local(): pl.pallas_call(body, out_shape=tuple((jax.ShapeDtypeStruct(s, d) for s, d...  15.3 us
    unnamed x67, local copies, waits for them, and re-layouts  12.7 us
    all_gather x1, blocking collectives, on_device(): w_line = lax.all_gather(packed, 'y', axis=0, tiled=True)  10.9 us
    ppermute x3, starting transfers between devices, on_device(): near = [lax.ppermute(hidden_in, 'x', t) for t in turns]  10.5 us
  transfers between devices with their start and end apart: 16, of which 4 were waited for; matrix products, arithmetic and copies ran while one was open for 5% of the time, Pallas kernels for 6%

profile of v3, /device:TPU:1, one launch (start us, length us, event | category | flops | bytes accessed | tf_op | source)
XLA Modules:
  0.0 179.8 jit_solution(11104881285547612848)
XLA Ops:
  0.7 16.4 %collective-permute-start = (bf16[2,320,256]{2,1,0:T(8,128)(2,1)}, bf16[2,320,256]{2,1,0:T(8,128)(2,1)}, u32[]{:S(2)}, u32[]{:S(2)}) collective-permute-start(bf16[2,320,256]{2,1,0:T(8,128)(2,1)} %refs_0_.1), channel_id=1, source_target_pairs={{0,8},{8,0},{1,9},{9,1},{2,10},{10,2},{3,11},{11,3},{4,12},{12,4},... | collective-permute-start | bytes 983048 | tf_op jit(solution)/shard_map/ppermute | solution.py:236
  17.1 3.1 %collective-permute-start.1 = (bf16[2,320,256]{2,1,0:T(8,128)(2,1)}, bf16[2,320,256]{2,1,0:T(8,128)(2,1)S(1)}, u32[]{:S(2)}, u32[]{:S(2)}) collective-permute-start(bf16[2,320,256]{2,1,0:T(8,128)(2,1)} %refs_0_.1), channel_id=1, source_target_pairs={{0,2},{2,4},{4,6},{6,0},{1,3},{3,5},{5,7},{7,1},{8,10},{10,12},{12... | collective-permute-start | bytes 983048 | tf_op jit(solution)/shard_map/ppermute | solution.py:247
  20.2 4.4 %collective-permute-start.2 = (bf16[2,320,256]{2,1,0:T(8,128)(2,1)}, bf16[2,320,256]{2,1,0:T(8,128)(2,1)S(1)}, u32[]{:S(2)}, u32[]{:S(2)}) collective-permute-start(bf16[2,320,256]{2,1,0:T(8,128)(2,1)} %refs_0_.1), channel_id=1, source_target_pairs={{0,4},{2,6},{4,0},{6,2},{1,5},{3,7},{5,1},{7,3},{8,12},{10,14},{12... | collective-permute-start | bytes 983048 | tf_op jit(solution)/shard_map/ppermute | solution.py:247
  24.6 3.1 %collective-permute-start.3 = (bf16[2,320,256]{2,1,0:T(8,128)(2,1)}, bf16[2,320,256]{2,1,0:T(8,128)(2,1)S(1)}, u32[]{:S(2)}, u32[]{:S(2)}) collective-permute-start(bf16[2,320,256]{2,1,0:T(8,128)(2,1)} %refs_0_.1), channel_id=1, source_target_pairs={{0,6},{2,0},{4,2},{6,4},{1,7},{3,1},{5,3},{7,5},{8,14},{10,8},{12,... | collective-permute-start | bytes 983048 | tf_op jit(solution)/shard_map/ppermute | solution.py:247
  29.2 4.7 %all-to-all-start = ((s32[8,16,128]{2,1,0:T(8,128)}), s32[8,16,128]{2,1,0:T(8,128)S(1)}, u32[]{:S(2)}, u32[]{:S(2)}) async-start(s32[8,16,128]{2,1,0:T(8,128)} %broadcast_in_dim.28), calls=%async_computation | async-start | bytes 131072 | tf_op jit(solution)/shard_map/all_to_all | solution.py:33
  36.7 1.5 tables.1
  39.1 10.9 %all_gather.3.w_line = bf16[256,832]{1,0:T(8,128)(2,1)S(1)} all-gather(bf16[64,832]{1,0:T(8,128)(2,1)S(1)} %maximum_bitcast_fusion.weights), channel_id=1, replica_groups=mesh['y'=4,'zl'=8,'zh'=2,'x'=4,'c'=2] {'y'}, dimensions={0}, use_global_device_ids=true | all-gather | bytes 532480 | tf_op jit(solution)/shard_map/all_gather | solution.py:238
  50.7 1.2 adapter_parts.1
  51.9 9.4 %all-to-all-start.1 = ((bf16[8,16,832]{2,1,0:T(8,128)(2,1)}), bf16[8,16,832]{2,1,0:T(8,128)(2,1)S(1)}, u32[]{:S(2)}, u32[]{:S(2)}) async-start(bf16[8,16,832]{2,1,0:T(8,128)(2,1)} %bitcast.3), calls=%async_computation.1 | async-start | bytes 458752 | tf_op jit(solution)/shard_map/all_to_all | solution.py:33
  61.3 1.9 %collective-permute-start.4 = (bf16[2,320,256]{2,1,0:T(8,128)(2,1)}, bf16[2,320,256]{2,1,0:T(8,128)(2,1)S(1)}, u32[]{:S(2)}, u32[]{:S(2)}) collective-permute-start(bf16[2,320,256]{2,1,0:T(8,128)(2,1)} %collective-permute-done.refs_4_), channel_id=1, source_target_pairs={{0,2},{2,4},{4,6},{6,0},{1,3},{3,5},{5,7},{7,1},{8,10},{10,12},{12... | collective-permute-start | bytes 983048 | tf_op jit(solution)/shard_map/ppermute | solution.py:249
  63.2 2.8 %collective-permute-start.5 = (bf16[2,320,256]{2,1,0:T(8,128)(2,1)}, bf16[2,320,256]{2,1,0:T(8,128)(2,1)}, u32[]{:S(2)}, u32[]{:S(2)}) collective-permute-start(bf16[2,320,256]{2,1,0:T(8,128)(2,1)} %collective-permute-done.refs_4_), channel_id=1, source_target_pairs={{0,4},{2,6},{4,0},{6,2},{1,5},{3,7},{5,1},{7,3},{8,12},{10,14},{12... | collective-permute-start | bytes 983048 | tf_op jit(solution)/shard_map/ppermute | solution.py:249
  66.0 3.7 %collective-permute-start.6 = (bf16[2,320,256]{2,1,0:T(8,128)(2,1)}, bf16[2,320,256]{2,1,0:T(8,128)(2,1)}, u32[]{:S(2)}, u32[]{:S(2)}) collective-permute-start(bf16[2,320,256]{2,1,0:T(8,128)(2,1)} %collective-permute-done.refs_4_), channel_id=1, source_target_pairs={{0,6},{2,0},{4,2},{6,4},{1,7},{3,1},{5,3},{7,5},{8,14},{10,8},{12,... | collective-permute-start | bytes 983048 | tf_op jit(solution)/shard_map/ppermute | solution.py:249
  69.7 2.8 %all-to-all-done.1.got = bf16[8,16,832]{2,1,0:T(8,128)(2,1)S(1)} async-done(((bf16[8,16,832]{2,1,0:T(8,128)(2,1)}), bf16[8,16,832]{2,1,0:T(8,128)(2,1)S(1)}, u32[]{:S(2)}, u32[]{:S(2)}) %all-to-all-start.1) | async-done | bytes 213024 | tf_op jit(solution)/shard_map/all_to_all | solution.py:33
  72.6 1.5 low_rank.1
  74.1 10.1 %all-to-all-start.2 = ((f32[8,8,320]{2,1,0:T(8,128)}), f32[8,8,320]{2,1,0:T(8,128)S(1)}, u32[]{:S(2)}, u32[]{:S(2)}) async-start(f32[8,8,320]{2,1,0:T(8,128)} %bitcast.5), calls=%async_computation.2 | async-start | bytes 196608 | tf_op jit(solution)/shard_map/all_to_all | solution.py:33
  84.2 5.0 %all-to-all-done.2 = f32[8,8,320]{2,1,0:T(8,128)S(1)} async-done(((f32[8,8,320]{2,1,0:T(8,128)}), f32[8,8,320]{2,1,0:T(8,128)S(1)}, u32[]{:S(2)}, u32[]{:S(2)}) %all-to-all-start.2) | async-done | bytes 81952 | tf_op jit(solution)/shard_map/all_to_all | solution.py:33
  89.2 21.5 %all_to_all.35 = bf16[16,8,320]{2,1,0:T(8,128)(2,1)S(1)} all-to-all(bf16[16,8,320]{2,1,0:T(8,128)(2,1)S(1)} %broadcast_in_dim.29), channel_id=1, replica_groups=mesh['y'=4,'zl'=8,'zh'=2,'x'=4,'c'=2] {'zh','x','c'}, dimensions={0} | all-to-all | bytes 163840 | tf_op jit(solution)/shard_map/all_to_all | solution.py:33
  111.4 1.5 adapter_grads.1
  113.5 9.3 %all-to-all-start.4 = ((bf16[8,16,896]{2,1,0:T(8,128)(2,1)}), bf16[8,16,896]{2,1,0:T(8,128)(2,1)S(1)}, u32[]{:S(2)}, u32[]{:S(2)}) async-start(bf16[8,16,896]{2,1,0:T(8,128)(2,1)} %adapter_grads.1), calls=%async_computation.4 | async-start | bytes 458752 | tf_op jit(solution)/shard_map/all_to_all | solution.py:33
  122.8 1.1 constant_dynamic-slice_fusion
  123.9 2.7 %collective-permute-start.7 = (bf16[2048,256]{1,0:T(8,128)(2,1)}, bf16[2048,256]{1,0:T(8,128)(2,1)}, u32[]{:S(2)}, u32[]{:S(2)}) collective-permute-start(bf16[2048,256]{1,0:T(8,128)(2,1)} %bitcast.27), channel_id=1, source_target_pairs={{0,1},{1,0},{2,3},{3,2},{4,5},{5,4},{6,7},{7,6},{8,9},{9,8},{10,11... | collective-permute-start | bytes 3145736 | tf_op jit(solution)/shard_map/ppermute | solution.py:303
  126.5 7.9 %all-to-all-done.4 = bf16[8,16,896]{2,1,0:T(8,128)(2,1)S(1)} async-done(((bf16[8,16,896]{2,1,0:T(8,128)(2,1)}), bf16[8,16,896]{2,1,0:T(8,128)(2,1)S(1)}, u32[]{:S(2)}, u32[]{:S(2)}) %all-to-all-start.4) | async-done | bytes 229408 | tf_op jit(solution)/shard_map/all_to_all | solution.py:33
  135.5 3.5 %all-to-all-start.5 = ((bf16[4,128,896]{2,1,0:T(8,128)(2,1)}), bf16[4,128,896]{2,1,0:T(8,128)(2,1)S(1)}, u32[]{:S(2)}, u32[]{:S(2)}) async-start(bf16[4,128,896]{2,1,0:T(8,128)(2,1)} %broadcast_in_dim.31), calls=%async_computation.5 | async-start | bytes 1835008 | tf_op jit(solution)/shard_map/all_to_all | solution.py:33
  139.0 1.2 reshape.72
  140.1 2.6 %dynamic-slice_reduce_fusion = bf16[64,8,256]{2,1,0:T(8,128)(2,1)S(1)} fusion(bf16[64,8,2,256]{3,2,1,0:T(2,128)(2,1)} %reshape.72, s32[]{:T(128)S(6)} %select_n.6), kind=kLoop, calls=%fused_computation | loop fusion | bytes 524292 | tf_op jit(solution)/shard_map/jit(dynamic_index_in_dim)/dynamic_slice | solution.py:302
  143.5 6.6 %collective-permute-start.8 = (bf16[64,2048]{1,0:T(8,128)(2,1)}, bf16[64,2048]{1,0:T(8,128)(2,1)}, u32[]{:S(2)}, u32[]{:S(2)}) collective-permute-start(bf16[64,2048]{1,0:T(8,128)(2,1)} %bitcast.38), channel_id=1, source_target_pairs={{0,1},{1,0},{2,3},{3,2},{4,5},{5,4},{6,7},{7,6},{8,9},{9,8},{10,11... | collective-permute-start | bytes 786440 | tf_op jit(solution)/shard_map/ppermute | solution.py:304
  152.7 7.6 %all-to-all-start.6 = ((f32[16,16,128]{2,1,0:T(8,128)}), f32[16,16,128]{2,1,0:T(8,128)}, u32[]{:S(2)}, u32[]{:S(2)}) async-start(f32[16,16,128]{2,1,0:T(8,128)} %copy-done.11), calls=%async_computation.6 | async-start | bytes 262144 | tf_op jit(solution)/shard_map/all_to_all | solution.py:33
  166.7 4.5 %base_product.1 = (f32[640,256]{1,0:T(8,128)S(1)}, f32[640,64]{1,0:T(8,128)S(1)}, bf16[640,320]{1,0:T(8,128)(2,1)S(1)}) custom-call(s32[16]{0:T(128)S(1)} %copy-done.29, bf16[2,320,256]{2,1,0:T(8,128)(2,1)S(1)} %copy-done.5, bf16[2,320,256]{2,1,0:T(8,128)(2,1)S(1)} %copy-done.15, bf16[2,320,256]{2,1,0:T(8,128)(2,1)S(1)} %copy-done.17, ...), custom_call_target="tpu_custom_call" | custom-call | flops 1000000 | bytes 100000 | tf_op jit(solution)/shard_map/base_product/pallas_call | solution.py:43
  171.2 2.2 %collective-permute-start.9 = (bf16[640,320]{1,0:T(8,128)(2,1)S(1)}, bf16[640,320]{1,0:T(8,128)(2,1)S(1)}, u32[]{:S(2)}, u32[]{:S(2)}) collective-permute-start(bf16[640,320]{1,0:T(8,128)(2,1)S(1)} %get-tuple-element.60), channel_id=1, source_target_pairs={{0,1},{1,0},{2,3},{3,2},{4,5},{5,4},{6,7},{7,6},{8,9},{9,8},{10,11... | collective-permute-start | bytes 1228808 | tf_op jit(solution)/shard_map/ppermute | solution.py:330
  173.4 1.5 collective-permute-done.9.got
  176.0 1.3 head_grads.1
  177.3 1.7 trunk_grads.1
  (93 shorter events, 19.8 us)
Async XLA Ops:
  0.6 71.9 %copy-start.24 = (bf16[2,320,64]{1,2,0:T(8,128)(2,1)S(1)}, bf16[2,320,64]{1,2,0:T(8,128)(2,1)}, u32[]{:S(2)}) copy-start(bf16[2,320,64]{1,2,0:T(8,128)(2,1)} %param.27) | copy-start | bytes 245764
  0.6 71.9 %copy-start.30 = (s32[2]{0:T(128)S(1)}, s32[2]{0:T(128)}, u32[]{:S(2)}) copy-start(s32[2]{0:T(128)} %lengths.3) | copy-start | bytes 28
  0.7 50.0 %collective-permute-start = (bf16[2,320,256]{2,1,0:T(8,128)(2,1)}, bf16[2,320,256]{2,1,0:T(8,128)(2,1)}, u32[]{:S(2)}, u32[]{:S(2)}) collective-permute-start(bf16[2,320,256]{2,1,0:T(8,128)(2,1)} %refs_0_.1), channel_id=1, source_target_pairs={{0,8},{8,0},{1,9},{9,1},{2,10},{10,2},{3,11},{11,3},{4,12},{12,4},... | collective-permute-start | bytes 983048 | tf_op jit(solution)/shard_map/ppermute | solution.py:236
  17.1 33.6 %collective-permute-start.1 = (bf16[2,320,256]{2,1,0:T(8,128)(2,1)}, bf16[2,320,256]{2,1,0:T(8,128)(2,1)S(1)}, u32[]{:S(2)}, u32[]{:S(2)}) collective-permute-start(bf16[2,320,256]{2,1,0:T(8,128)(2,1)} %refs_0_.1), channel_id=1, source_target_pairs={{0,2},{2,4},{4,6},{6,0},{1,3},{3,5},{5,7},{7,1},{8,10},{10,12},{12... | collective-permute-start | bytes 983048 | tf_op jit(solution)/shard_map/ppermute | solution.py:247
  20.2 30.4 %collective-permute-start.2 = (bf16[2,320,256]{2,1,0:T(8,128)(2,1)}, bf16[2,320,256]{2,1,0:T(8,128)(2,1)S(1)}, u32[]{:S(2)}, u32[]{:S(2)}) collective-permute-start(bf16[2,320,256]{2,1,0:T(8,128)(2,1)} %refs_0_.1), channel_id=1, source_target_pairs={{0,4},{2,6},{4,0},{6,2},{1,5},{3,7},{5,1},{7,3},{8,12},{10,14},{12... | collective-permute-start | bytes 983048 | tf_op jit(solution)/shard_map/ppermute | solution.py:247
  24.6 26.1 %collective-permute-start.3 = (bf16[2,320,256]{2,1,0:T(8,128)(2,1)}, bf16[2,320,256]{2,1,0:T(8,128)(2,1)S(1)}, u32[]{:S(2)}, u32[]{:S(2)}) collective-permute-start(bf16[2,320,256]{2,1,0:T(8,128)(2,1)} %refs_0_.1), channel_id=1, source_target_pairs={{0,6},{2,0},{4,2},{6,4},{1,7},{3,1},{5,3},{7,5},{8,14},{10,8},{12,... | collective-permute-start | bytes 983048 | tf_op jit(solution)/shard_map/ppermute | solution.py:247
  29.2 21.5 %all-to-all-start = ((s32[8,16,128]{2,1,0:T(8,128)}), s32[8,16,128]{2,1,0:T(8,128)S(1)}, u32[]{:S(2)}, u32[]{:S(2)}) async-start(s32[8,16,128]{2,1,0:T(8,128)} %broadcast_in_dim.28), calls=%async_computation | async-start | bytes 131072 | tf_op jit(solution)/shard_map/all_to_all | solution.py:33
  36.7 35.8 %copy-start.4 = (bf16[2,320,256]{2,1,0:T(8,128)(2,1)S(1)}, bf16[2,320,256]{2,1,0:T(8,128)(2,1)}, u32[]{:S(2)}) copy-start(bf16[2,320,256]{2,1,0:T(8,128)(2,1)} %refs_0_.1) | copy-start | bytes 983044
  36.7 35.8 %copy-start.12 = (bf16[2,320,256]{2,1,0:T(8,128)(2,1)S(1)}, bf16[2,320,256]{2,1,0:T(8,128)(2,1)}, u32[]{:S(2)}) copy-start(bf16[2,320,256]{2,1,0:T(8,128)(2,1)} %grad_q.3) | copy-start | bytes 983044
  38.2 34.3 %copy-start.22 = (bf16[2,240,64]{2,1,0:T(8,128)(2,1)}, bf16[2,240,64]{2,1,0:T(8,128)(2,1)S(1)}, u32[]{:S(2)}) copy-start(bf16[2,240,64]{2,1,0:T(8,128)(2,1)S(1)} %get-tuple-element.47.lat_own) | copy-start | bytes 184324
  50.6 21.8 %copy-start.14 = (bf16[2,320,256]{2,1,0:T(8,128)(2,1)}, bf16[2,320,256]{2,1,0:T(8,128)(2,1)S(1)}, u32[]{:S(2)}) copy-start(bf16[2,320,256]{2,1,0:T(8,128)(2,1)S(1)} %collective-permute-done.1.refs_1_) | copy-start | bytes 983044
  50.7 21.8 %copy-start.16 = (bf16[2,320,256]{2,1,0:T(8,128)(2,1)}, bf16[2,320,256]{2,1,0:T(8,128)(2,1)S(1)}, u32[]{:S(2)}) copy-start(bf16[2,320,256]{2,1,0:T(8,128)(2,1)S(1)} %collective-permute-done.2.refs_2_) | copy-start | bytes 983044
  50.7 21.8 %copy-start.18 = (bf16[2,320,256]{2,1,0:T(8,128)(2,1)}, bf16[2,320,256]{2,1,0:T(8,128)(2,1)S(1)}, u32[]{:S(2)}) copy-start(bf16[2,320,256]{2,1,0:T(8,128)(2,1)S(1)} %collective-permute-done.3.refs_3_) | copy-start | bytes 983044
  51.9 20.6 %all-to-all-start.1 = ((bf16[8,16,832]{2,1,0:T(8,128)(2,1)}), bf16[8,16,832]{2,1,0:T(8,128)(2,1)S(1)}, u32[]{:S(2)}, u32[]{:S(2)}) async-start(bf16[8,16,832]{2,1,0:T(8,128)(2,1)} %bitcast.3), calls=%async_computation.1 | async-start | bytes 458752 | tf_op jit(solution)/shard_map/all_to_all | solution.py:33
  61.3 22.9 %collective-permute-start.4 = (bf16[2,320,256]{2,1,0:T(8,128)(2,1)}, bf16[2,320,256]{2,1,0:T(8,128)(2,1)S(1)}, u32[]{:S(2)}, u32[]{:S(2)}) collective-permute-start(bf16[2,320,256]{2,1,0:T(8,128)(2,1)} %collective-permute-done.refs_4_), channel_id=1, source_target_pairs={{0,2},{2,4},{4,6},{6,0},{1,3},{3,5},{5,7},{7,1},{8,10},{10,12},{12... | collective-permute-start | bytes 983048 | tf_op jit(solution)/shard_map/ppermute | solution.py:249
  63.2 21.0 %collective-permute-start.5 = (bf16[2,320,256]{2,1,0:T(8,128)(2,1)}, bf16[2,320,256]{2,1,0:T(8,128)(2,1)}, u32[]{:S(2)}, u32[]{:S(2)}) collective-permute-start(bf16[2,320,256]{2,1,0:T(8,128)(2,1)} %collective-permute-done.refs_4_), channel_id=1, source_target_pairs={{0,4},{2,6},{4,0},{6,2},{1,5},{3,7},{5,1},{7,3},{8,12},{10,14},{12... | collective-permute-start | bytes 983048 | tf_op jit(solution)/shard_map/ppermute | solution.py:249
  66.0 18.2 %collective-permute-start.6 = (bf16[2,320,256]{2,1,0:T(8,128)(2,1)}, bf16[2,320,256]{2,1,0:T(8,128)(2,1)}, u32[]{:S(2)}, u32[]{:S(2)}) collective-permute-start(bf16[2,320,256]{2,1,0:T(8,128)(2,1)} %collective-permute-done.refs_4_), channel_id=1, source_target_pairs={{0,6},{2,0},{4,2},{6,4},{1,7},{3,1},{5,3},{7,5},{8,14},{10,8},{12,... | collective-permute-start | bytes 983048 | tf_op jit(solution)/shard_map/ppermute | solution.py:249
  72.5 38.1 %copy-start.13 = (bf16[2,320,256]{2,1,0:T(8,128)(2,1)S(1)}, bf16[2,320,256]{2,1,0:T(8,128)(2,1)}, u32[]{:S(2)}) copy-start(bf16[2,320,256]{2,1,0:T(8,128)(2,1)} %grad_q.3) | copy-start | bytes 983044
  72.5 38.1 %copy-start.25 = (bf16[2,320,64]{1,2,0:T(8,128)(2,1)S(1)}, bf16[2,320,64]{1,2,0:T(8,128)(2,1)}, u32[]{:S(2)}) copy-start(bf16[2,320,64]{1,2,0:T(8,128)(2,1)} %param.27) | copy-start | bytes 245764
  72.6 38.1 %copy-start.31 = (s32[2]{0:T(128)S(1)}, s32[2]{0:T(128)}, u32[]{:S(2)}) copy-start(s32[2]{0:T(128)} %lengths.3) | copy-start | bytes 28
  74.1 36.6 %copy-start.26 = (bf16[16,832]{1,0:T(8,128)(2,1)}, bf16[16,832]{1,0:T(8,128)(2,1)S(1)}, u32[]{:S(2)}) copy-start(bf16[16,832]{1,0:T(8,128)(2,1)S(1)} %get-tuple-element.61.ad) | copy-start | bytes 79876
  74.1 48.7 %copy-start = (bf16[4096,256]{1,0:T(8,128)(2,1)S(1)}, bf16[4096,256]{1,0:T(8,128)(2,1)}, u32[]{:S(2)}) copy-start(bf16[4096,256]{1,0:T(8,128)(2,1)} %refs_8_.1) | copy-start | bytes 6291460
  74.1 15.1 %all-to-all-start.2 = ((f32[8,8,320]{2,1,0:T(8,128)}), f32[8,8,320]{2,1,0:T(8,128)S(1)}, u32[]{:S(2)}, u32[]{:S(2)}) async-start(f32[8,8,320]{2,1,0:T(8,128)} %bitcast.5), calls=%async_computation.2 | async-start | bytes 196608 | tf_op jit(solution)/shard_map/all_to_all | solution.py:33
  84.1 26.5 %copy-start.20 = (bf16[2,320,256]{2,1,0:T(8,128)(2,1)}, bf16[2,320,256]{2,1,0:T(8,128)(2,1)S(1)}, u32[]{:S(2)}) copy-start(bf16[2,320,256]{2,1,0:T(8,128)(2,1)S(1)} %collective-permute-done.4.refs_5_) | copy-start | bytes 983044
  113.5 21.0 %all-to-all-start.4 = ((bf16[8,16,896]{2,1,0:T(8,128)(2,1)}), bf16[8,16,896]{2,1,0:T(8,128)(2,1)S(1)}, u32[]{:S(2)}, u32[]{:S(2)}) async-start(bf16[8,16,896]{2,1,0:T(8,128)(2,1)} %adapter_grads.1), calls=%async_computation.4 | async-start | bytes 458752 | tf_op jit(solution)/shard_map/all_to_all | solution.py:33
  122.8 16.2 %copy-start.1 = (bf16[4096,64]{0,1:T(8,128)(2,1)S(1)}, bf16[4096,64]{0,1:T(8,128)(2,1)}, u32[]{:S(2)}) copy-start(bf16[4096,64]{0,1:T(8,128)(2,1)} %param.24) | copy-start | bytes 1572868
  123.9 37.2 %collective-permute-start.7 = (bf16[2048,256]{1,0:T(8,128)(2,1)}, bf16[2048,256]{1,0:T(8,128)(2,1)}, u32[]{:S(2)}, u32[]{:S(2)}) collective-permute-start(bf16[2048,256]{1,0:T(8,128)(2,1)} %bitcast.27), channel_id=1, source_target_pairs={{0,1},{1,0},{2,3},{3,2},{4,5},{5,4},{6,7},{7,6},{8,9},{9,8},{10,11... | collective-permute-start | bytes 3145736 | tf_op jit(solution)/shard_map/ppermute | solution.py:303
  135.5 14.6 %all-to-all-start.5 = ((bf16[4,128,896]{2,1,0:T(8,128)(2,1)}), bf16[4,128,896]{2,1,0:T(8,128)(2,1)S(1)}, u32[]{:S(2)}, u32[]{:S(2)}) async-start(bf16[4,128,896]{2,1,0:T(8,128)(2,1)} %broadcast_in_dim.31), calls=%async_computation.5 | async-start | bytes 1835008 | tf_op jit(solution)/shard_map/all_to_all | solution.py:33
  143.5 17.6 %collective-permute-start.8 = (bf16[64,2048]{1,0:T(8,128)(2,1)}, bf16[64,2048]{1,0:T(8,128)(2,1)}, u32[]{:S(2)}, u32[]{:S(2)}) collective-permute-start(bf16[64,2048]{1,0:T(8,128)(2,1)} %bitcast.38), channel_id=1, source_target_pairs={{0,1},{1,0},{2,3},{3,2},{4,5},{5,4},{6,7},{7,6},{8,9},{9,8},{10,11... | collective-permute-start | bytes 786440 | tf_op jit(solution)/shard_map/ppermute | solution.py:304
  152.7 24.6 %all-to-all-start.6 = ((f32[16,16,128]{2,1,0:T(8,128)}), f32[16,16,128]{2,1,0:T(8,128)}, u32[]{:S(2)}, u32[]{:S(2)}) async-start(f32[16,16,128]{2,1,0:T(8,128)} %copy-done.11), calls=%async_computation.6 | async-start | bytes 262144 | tf_op jit(solution)/shard_map/all_to_all | solution.py:33
  161.0 15.0 %copy-start.3 = (bf16[240,1024]{1,0:T(8,128)(2,1)S(1)}, bf16[240,1024]{1,0:T(8,128)(2,1)}, u32[]{:S(2)}) copy-start(bf16[240,1024]{1,0:T(8,128)(2,1)} %task_embed.3) | copy-start | bytes 1474564
  171.2 3.8 %collective-permute-start.9 = (bf16[640,320]{1,0:T(8,128)(2,1)S(1)}, bf16[640,320]{1,0:T(8,128)(2,1)S(1)}, u32[]{:S(2)}, u32[]{:S(2)}) collective-permute-start(bf16[640,320]{1,0:T(8,128)(2,1)S(1)} %get-tuple-element.60), channel_id=1, source_target_pairs={{0,1},{1,0},{2,3},{3,2},{4,5},{5,4},{6,7},{7,6},{8,9},{9,8},{10,11... | collective-permute-start | bytes 1228808 | tf_op jit(solution)/shard_map/ppermute | solution.py:330
  (17 other events, 37.8 us)

commit v4 on v3

--- a/solution.py
+++ b/solution.py
@@ -37,7 +37,7 @@
     return swap(jnp.broadcast_to(block[None], (n,) + block.shape), axes)
 
 
-def local(body, outs, args, scalars=0, scratch=(), flops=1_000_000, name=None):
+def local(body, outs, args, scalars=0, scratch=(), flops=1_000_000, mib=8, name=None):
     in_vmem = pl.BlockSpec(memory_space=pltpu.VMEM)
     in_smem = pl.BlockSpec(memory_space=pltpu.SMEM)
     return pl.pallas_call(
@@ -46,7 +46,7 @@
         in_specs=[in_smem] * scalars + [in_vmem] * (len(args) - scalars),
         out_specs=tuple(in_vmem for _ in outs),
         scratch_shapes=list(scratch),
-        compiler_params=pltpu.CompilerParams(vmem_limit_bytes=32 * 2**20),
+        compiler_params=pltpu.CompilerParams(vmem_limit_bytes=mib * 2**20),
         cost_estimate=pl.CostEstimate(flops=flops, bytes_accessed=100_000, transcendentals=0),
         name=name,
     )(*args)
@@ -132,9 +132,7 @@
         full = jnp.where(same, mm_nt(d_all[:, cols], weights[:, cols]), 0.0)
         by_batch = jnp.sum(full.reshape(n // rank, rank, k), axis=1)
         parts.append(mm_nt(fold, by_batch, exact))
-    both = jnp.concatenate(parts, axis=0)
-    pad = out.shape[2] - both.shape[1]
-    both = jnp.concatenate([both, jnp.zeros((both.shape[0], pad), f32)], axis=1)
+    both = jnp.concatenate(parts, axis=1)
     for i in range(out.shape[0]):
         out[i] = both
 
@@ -162,7 +160,8 @@
     for i in range(1, got.shape[0]):
         total += got[i]
     rows, batches = sg_all.shape
-    d_pre = total[:, :batches] * sg_all[...]
+    total = jnp.concatenate([total[:, :batches], total[:, batches:]], axis=0)
+    d_pre = total * sg_all[...]
     both = d_pre[: rows // 2] + d_pre[rows // 2 :]
     hi = both.astype(bf16)
     lo = (both - hi.astype(f32)).astype(bf16)
@@ -170,16 +169,26 @@
     g_mod[...] = jnp.sum(d_pre, axis=1, keepdims=True)
 
 
+def give_kernel(core, base_q, base_vt, out):
+    wq, wv = base_q.shape[1], base_vt.shape[0]
+    out[...] = jnp.zeros_like(out)
+    for n in range(out.shape[0] // wq):
+        at = pl.ds(pl.multiple_of((2 * n + core[0]) * wq, wq), wq)
+        to = slice(n * wq, (n + 1) * wq)
+        out[to, :wq] = base_q[at, :]
+        out[to, wq : wq + wv] = base_vt[:, at].astype(f32).T.astype(bf16)
+
+
 def base_kernel(order, *refs):
-    near = refs[:8]
-    base_q, base_vt, part_q, part_vt, acc_q, acc_v, out = refs[8:]
-    seqs, length, wq = near[0].shape
-    for n, block in enumerate(near):
-        h = block[...].reshape(seqs * length, wq)
+    near = refs[:4]
+    base_q, base_vt, theirs, acc_q, acc_v, out = refs[4:]
+    halves, seqs, length, wq = near[0].shape
+    for n in range(halves * len(near)):
+        h = near[n // halves][n % halves].reshape(seqs * length, wq)
         at = pl.ds(pl.multiple_of(order[2 * n] * wq, wq), wq)
         far = pl.ds(pl.multiple_of(order[2 * n + 1] * wq, wq), wq)
         adds = mm(h, base_q[at, :]), mm_nt(h, base_vt[:, at])
-        partner = jnp.concatenate([mm(h, part_q[far, :]), mm_nt(h, part_vt[:, far])], axis=1)
+        partner = mm(h, theirs[far, :])
         if n == 0:
             acc_q[...], acc_v[...] = adds
             both = partner
@@ -187,10 +196,10 @@
             acc_q[...] += adds[0]
             acc_v[...] += adds[1]
             both += partner
-    out[...] = both.astype(bf16)
-
-
-def out_kernel(rank, acc_q, acc_v, got, low, ad, q_out, vt_out):
+    out[...] = both[:, : out.shape[1]].astype(bf16)
+
+
+def out_kernel(rank, core, acc_q, acc_v, got, low, ad, q_out, vt_out):
     seqs, length, wq = q_out.shape
     both = ad[...].astype(f32)
     first = ((0,), (0,))
@@ -199,7 +208,8 @@
         b = both[s * rank : (s + 1) * rank, :].astype(bf16)
         low_q = mm(low[4 * s].astype(bf16), b[:, wq : 2 * wq], first)
         low_v = mm(b[:, 3 * wq :], low[4 * s + 1].astype(bf16), first)
-        got_q, got_v = got[own, :wq].astype(f32), got[own, wq:].astype(f32)
+        theirs = got[core[0], own, :].astype(f32)
+        got_q, got_v = theirs[:, :wq], theirs[:, wq:]
         q_out[s] = (acc_q[own, :] + got_q + scale * low_q).astype(bf16)
         vt_out[s] = ((acc_v[own, :] + got_v).T + scale * low_v).astype(bf16)
 
@@ -231,11 +241,11 @@
     batches = seqs * ny * nz
     grad_vt = grad_v.swapaxes(1, 2)
 
-    ids_rows = jnp.broadcast_to(task_ids[:, None, None], (seqs, rank, 128)).reshape(seqs * rank, 128)
-    ids_line = spread(ids_rows, "zl", nz)
-    other = lax.ppermute(hidden_in, "zh", [(0, 1), (1, 0)])
     packed = jnp.concatenate([wa_q, wb_q, wa_v, wb_v], axis=2).reshape(rows * rank, width)
     w_line = lax.all_gather(packed, "y", axis=0, tiled=True)
+    ids, w_line = lax.optimization_barrier((task_ids, w_line))
+    ids_rows = jnp.broadcast_to(ids[:, None, None], (seqs, rank, 128)).reshape(seqs * rank, 128)
+    ids_line = spread(ids_rows, "zl", nz)
     lat_line, lat_own, sg_own = local(
         functools.partial(tables_kernel, ny, nz),
         [((2, tasks, ny * rows * rank), bf16), ((2, tasks, rows * rank), bf16), ((2 * rows, tasks), f32)],
@@ -243,10 +253,8 @@
         scalars=1,
         name="tables",
     )
-    turns = [[(i, (i + k) % nx) for i in range(nx)] for k in range(1, nx)]
-    near = [lax.ppermute(hidden_in, "x", t) for t in turns]
-    ids_line, w_line, other, *near = lax.optimization_barrier((ids_line, w_line, other, *near))
-    far = [lax.ppermute(other, "x", t) for t in turns]
+    other = lax.ppermute(hidden_in, "zh", [(0, 1), (1, 0)])
+    ids_line, w_line, other = lax.optimization_barrier((ids_line, w_line, other))
 
     (part,) = local(
         functools.partial(part_kernel, split, rank),
@@ -260,14 +268,24 @@
         [((seqs * rank, width), bf16), ((seqs, 2, 2 * rank, length), f32)],
         (seq_lengths, got, hidden_in, grad_q, grad_vt),
         scalars=1,
-        flops=30_000_000_000,
         name="low_rank",
     )
 
     low = swap(low.reshape(nx * nc, seqs * 4 * rank // (nx * nc), length), xc)
-    low, *far = lax.optimization_barrier((low, *far))
     low = jnp.sum(low, axis=0).astype(bf16)
     low = spread(low, head, nh * nx * nc)
+
+    blocks = nh * nx
+    pair = [(0, 1), (1, 0)]
+    base_vt = base_v.T
+    (theirs,) = local(
+        give_kernel,
+        [((blocks * wq, wq + 128), bf16)],
+        (jnp.reshape(1 - c, (1,)).astype(jnp.int32), base_q, base_vt),
+        scalars=1,
+        name="partner_rows",
+    )
+    theirs = lax.ppermute(theirs, "c", pair)
     low = jnp.sum(low.reshape(nh, 4 * seqs, rank, length).astype(f32), axis=0)
     (d_own,) = local(
         functools.partial(adapter_grad_kernel, wq, wv, rank),
@@ -278,11 +296,34 @@
         name="adapter_grads",
     )
     d_line = swap(d_own, "zl").reshape(nz * seqs * rank, width + 64)
-    d_all = spread(d_line, "y", ny).reshape(batches * rank, width + 64)
-
+    d_all = lax.all_gather(d_line, "y", axis=0, tiled=True)
+
+    both_z = jnp.stack([hidden_in, other])
+    turned = [both_z] + [lax.ppermute(both_z, "x", [(i, (i + k) % nx) for i in range(nx)]) for k in range(1, nx)]
+    order = []
+    for k in range(nx):
+        for half in range(nh):
+            block = (zh ^ half) * nx + lax.rem(x - k + nx, nx)
+            order += [block * nc + c, block]
+    order = jnp.stack(order).astype(jnp.int32)
+    d_all, order = lax.optimization_barrier((d_all, order))
+    acc_q, acc_v, given = local(
+        base_kernel,
+        [((seqs * length, wq), f32), ((seqs * length, wv), f32), ((seqs * length, wq + wv), bf16)],
+        (
+            order,
+            *turned,
+            base_q,
+            base_vt,
+            theirs,
+        ),
+        scalars=1,
+        mib=20,
+        name="base_product",
+    )
     (d_lat,) = local(
         functools.partial(latent_grad_kernel, split, width, rank),
-        [((nh * nx * nc, 2 * rows, 128), f32)],
+        [((nh * nx * nc, rows, 2 * batches), f32)],
         (d_all, packed),
         name="latent_grads",
     )
@@ -295,39 +336,11 @@
         name="head_grads",
     )
 
-    blocks = nh * nx
-    pair = [(0, 1), (1, 0)]
-    base_vt = base_v.T
-    part_q = lax.dynamic_index_in_dim(base_q.reshape(blocks, nc, wq, wq), 1 - c, 1, keepdims=False)
-    part_vt = lax.dynamic_index_in_dim(base_vt.reshape(wv, blocks, nc, wq), 1 - c, 2, keepdims=False)
-    part_q = lax.ppermute(part_q.reshape(blocks * wq, wq), "c", pair)
-    part_vt = lax.ppermute(part_vt.reshape(wv, blocks * wq), "c", pair)
-    order = []
-    for half in range(nh):
-        for k in range(nx):
-            block = (zh ^ half) * nx + lax.rem(x - k + nx, nx)
-            order += [block * nc + c, block]
-    acc_q, acc_v, given = local(
-        base_kernel,
-        [((seqs * length, wq), f32), ((seqs * length, wv), f32), ((seqs * length, wq + wv), bf16)],
-        (
-            jnp.stack(order).astype(jnp.int32),
-            hidden_in,
-            *near,
-            other,
-            *far,
-            base_q,
-            base_vt,
-            part_q,
-            part_vt,
-        ),
-        scalars=1,
-        name="base_product",
-    )
     q_out, vt_out = local(
         functools.partial(out_kernel, rank),
         [((seqs, length, wq), bf16), ((seqs, wv, length), bf16)],
-        (acc_q, acc_v, lax.ppermute(given, "c", pair), low, adapters),
+        (jnp.reshape(1 - c, (1,)).astype(jnp.int32), acc_q, acc_v, lax.all_gather(given, "c"), low, adapters),
+        scalars=1,
         name="outputs",
     )
     d_lat, sg_all, embeds, g_aq, q_out = lax.optimization_barrier((d_lat, sg_all, embeds, g_aq, q_out))

time: 181 us -> 174 us (0.961)
  starting transfers between devices: 91.4 us -> 55.2 us
  blocking collectives: 32.3 us -> 59.5 us
  local copies, waits for them, and re-layouts: 21.4 us -> 16.4 us
  waiting for transfers between devices: 17.3 us -> 20.6 us
  other arithmetic: 1.12 us -> 3.81 us
    ppermute x9 -> x4, starting transfers between devices: 30.4 us -> 9.85 us  [the longest x3 7.8 us: on_device(): lax.ppermute(both_z, 'x', [(i, (i + k) % nx) for i in range(nx)])]
    all_gather x0 -> x2, blocking collectives: none -> 15.6 us  [the longest x1 13 us: on_device(): d_all = lax.all_gather(d_line, 'y', axis=0, tiled=True)]
    all_to_all x6 -> x4, starting transfers between devices: 44.6 us -> 29.1 us  [swap(): return lax.all_to_all(blocks, axes, 0, 0, tiled=True)]
    all_to_all x1 -> x2, blocking collectives: 21.5 us -> 32 us  [swap(): return lax.all_to_all(blocks, axes, 0, 0, tiled=True)]
    all_to_all x6 -> x4, waiting for transfers between devices: 15.7 us -> 20.6 us  [swap(): return lax.all_to_all(blocks, axes, 0, 0, tiled=True)]
    dynamic_slice x2 -> x0, local copies, waits for them, and re-layouts: 3.66 us -> none  [the longest x1 2.59 us: on_device(): lax.dynamic_index_in_dim(base_vt.reshape(wv, blocks, nc, wq), 1 - c, 2, k...]
    another operation x0 -> x1, other arithmetic: none -> 1.87 us  [on_device(): both_z = jnp.stack([hidden_in, other])]
    pallas_call x9 -> x10, Pallas kernels: 15.3 us -> 15.9 us  [local(): pl.pallas_call(body, out_shape=tuple((jax.ShapeDtypeStruct(s, d) for s, d...]
  transfers between devices with their start and end apart: 16 -> 9, of which waited for: 4 -> 4; matrix products, arithmetic and copies ran while one was open for 5% -> 3% of each run, Pallas kernels for 6% -> 7%
where the time goes in v4:
time: 174 us; the launch traced here: 172 us
  blocking collectives  59.5 us (34%)
  starting transfers between devices  55.2 us (32%)
  waiting for transfers between devices  20.6 us (12%)
  local copies, waits for them, and re-layouts  16.4 us (9%)
  Pallas kernels  15.9 us (9%)
  other arithmetic  3.81 us (2%)
    all_to_all x2, blocking collectives, swap(): return lax.all_to_all(blocks, axes, 0, 0, tiled=True)  32 us
    all_to_all x4, starting transfers between devices, swap(): return lax.all_to_all(blocks, axes, 0, 0, tiled=True)  29.1 us
    all_to_all x4, waiting for transfers between devices, swap(): return lax.all_to_all(blocks, axes, 0, 0, tiled=True)  20.6 us
    ppermute x1, starting transfers between devices, on_device(): other = lax.ppermute(hidden_in, 'zh', [(0, 1), (1, 0)])  16.3 us
    pallas_call x10, Pallas kernels, local(): pl.pallas_call(body, out_shape=tuple((jax.ShapeDtypeStruct(s, d) for s, d...  15.9 us
    unnamed x56, local copies, waits for them, and re-layouts  13 us
    all_gather x1, blocking collectives, on_device(): d_all = lax.all_gather(d_line, 'y', axis=0, tiled=True)  13 us
    all_gather x1, blocking collectives, on_device(): w_line = lax.all_gather(packed, 'y', axis=0, tiled=True)  11.9 us
  transfers between devices with their start and end apart: 9, of which 4 were waited for; matrix products, arithmetic and copies ran while one was open for 3% of the time, Pallas kernels for 7%

profile of v4, /device:TPU:1, one launch (start us, length us, event | category | flops | bytes accessed | tf_op | source)
XLA Modules:
  0.0 172.4 jit_solution(6158168917129287437)
XLA Ops:
  0.6 16.3 %collective-permute-start = (bf16[2,320,256]{2,1,0:T(8,128)(2,1)}, bf16[2,320,256]{2,1,0:T(8,128)(2,1)}, u32[]{:S(2)}, u32[]{:S(2)}) collective-permute-start(bf16[2,320,256]{2,1,0:T(8,128)(2,1)} %hidden.3), channel_id=1, source_target_pairs={{0,8},{8,0},{1,9},{9,1},{2,10},{10,2},{3,11},{11,3},{4,12},{12,4},... | collective-permute-start | bytes 983048 | tf_op jit(solution)/shard_map/ppermute | solution.py:256
  17.8 11.9 %all_gather.12.w_line = bf16[256,832]{1,0:T(8,128)(2,1)S(1)} all-gather(bf16[64,832]{1,0:T(8,128)(2,1)S(1)} %maximum_bitcast_fusion.weights), channel_id=1, replica_groups=mesh['y'=4,'zl'=8,'zh'=2,'x'=4,'c'=2] {'y'}, dimensions={0}, use_global_device_ids=true | all-gather | bytes 532480 | tf_op jit(solution)/shard_map/all_gather | solution.py:245
  31.8 4.7 %all-to-all-start = ((s32[8,16,128]{2,1,0:T(8,128)}), s32[8,16,128]{2,1,0:T(8,128)S(1)}, u32[]{:S(2)}, u32[]{:S(2)}) async-start(s32[8,16,128]{2,1,0:T(8,128)} %broadcast_in_dim.10), calls=%async_computation | async-start | bytes 131072 | tf_op jit(solution)/shard_map/all_to_all | solution.py:33
  36.6 1.0 copy-done.3
  37.6 1.0 copy-done.10
  39.3 1.5 tables.1
  42.2 7.2 %all-to-all-done.ids = s32[8,16,128]{2,1,0:T(8,128)S(1)} async-done(((s32[8,16,128]{2,1,0:T(8,128)}), s32[8,16,128]{2,1,0:T(8,128)S(1)}, u32[]{:S(2)}, u32[]{:S(2)}) %all-to-all-start) | async-done | bytes 65568 | tf_op jit(solution)/shard_map/all_to_all | solution.py:33
  49.4 0.9 copy-done.15
  50.8 18.6 %all_to_all.30.got = bf16[8,16,832]{2,1,0:T(8,128)(2,1)S(1)} all-to-all(bf16[8,16,832]{2,1,0:T(8,128)(2,1)S(1)} %bitcast.41), channel_id=1, replica_groups=mesh['y'=4,'zl'=8,'zh'=2,'x'=4,'c'=2] {'zl'}, dimensions={0} | all-to-all | bytes 425984 | tf_op jit(solution)/shard_map/all_to_all | solution.py:33
  69.5 1.0 copy-done.5
  72.2 13.4 %all_to_all.31 = f32[8,8,320]{2,1,0:T(8,128)S(1)} all-to-all(f32[8,8,320]{2,1,0:T(8,128)S(1)} %bitcast.44), channel_id=1, replica_groups=mesh['y'=4,'zl'=8,'zh'=2,'x'=4,'c'=2] {'x','c'}, dimensions={0} | all-to-all | bytes 163840 | tf_op jit(solution)/shard_map/all_to_all | solution.py:33
  86.2 9.1 %all-to-all-start.3 = ((bf16[16,8,320]{2,1,0:T(8,128)(2,1)}), bf16[16,8,320]{2,1,0:T(8,128)(2,1)}, u32[]{:S(2)}, u32[]{:S(2)}) async-start(bf16[16,8,320]{2,1,0:T(8,128)(2,1)} %broadcast_in_dim.22), calls=%async_computation.3 | async-start | bytes 196608 | tf_op jit(solution)/shard_map/all_to_all | solution.py:33
  95.4 1.4 partner_rows.1
  96.8 2.1 %collective-permute-start.4 = (bf16[2048,384]{1,0:T(8,128)(2,1)}, bf16[2048,384]{1,0:T(8,128)(2,1)}, u32[]{:S(2)}, u32[]{:S(2)}) collective-permute-start(bf16[2048,384]{1,0:T(8,128)(2,1)} %partner_rows.1), channel_id=1, source_target_pairs={{0,1},{1,0},{2,3},{3,2},{4,5},{5,4},{6,7},{7,6},{8,9},{9,8},{10,11... | collective-permute-start | bytes 4718600 | tf_op jit(solution)/shard_map/ppermute | solution.py:288
  98.8 11.2 %all-to-all-done.3 = bf16[16,8,320]{2,1,0:T(8,128)(2,1)} async-done(((bf16[16,8,320]{2,1,0:T(8,128)(2,1)}), bf16[16,8,320]{2,1,0:T(8,128)(2,1)}, u32[]{:S(2)}, u32[]{:S(2)}) %all-to-all-start.3) | async-done | bytes 81952 | tf_op jit(solution)/shard_map/all_to_all | solution.py:33
  110.0 0.9 convert_reduce_fusion.low
  111.0 1.5 adapter_grads.1
  112.5 5.1 %all-to-all-start.4 = ((bf16[8,16,896]{2,1,0:T(8,128)(2,1)}), bf16[8,16,896]{2,1,0:T(8,128)(2,1)}, u32[]{:S(2)}, u32[]{:S(2)}) async-start(bf16[8,16,896]{2,1,0:T(8,128)(2,1)} %adapter_grads.1), calls=%async_computation.4 | async-start | bytes 458752 | tf_op jit(solution)/shard_map/all_to_all | solution.py:33
  117.6 1.9 %pad_maximum_fusion.refs_0_ = bf16[2,2,320,256]{3,2,1,0:T(8,128)(2,1)} fusion(bf16[1,2,320,256]{3,2,1,0:T(8,128)(2,1)} %bitcast.26, bf16[1,2,320,256]{3,2,1,0:T(8,128)(2,1)S(1)} %bitcast.38), kind=kLoop, calls=%fused_computation | loop fusion | flops 327680 | bytes 1310720 | tf_op jit(solution)/shard_map/stack | solution.py:301
  119.5 3.0 %collective-permute-start.3 = (bf16[2,2,320,256]{3,2,1,0:T(8,128)(2,1)}, bf16[2,2,320,256]{3,2,1,0:T(8,128)(2,1)}, u32[]{:S(2)}, u32[]{:S(2)}) collective-permute-start(bf16[2,2,320,256]{3,2,1,0:T(8,128)(2,1)} %pad_maximum_fusion.refs_0_), channel_id=1, source_target_pairs={{0,6},{2,0},{4,2},{6,4},{1,7},{3,1},{5,3},{7,5},{8,14},{10,8},{12,... | collective-permute-start | bytes 1966088 | tf_op jit(solution)/shard_map/ppermute | solution.py:302
  122.5 2.9 %collective-permute-start.2 = (bf16[2,2,320,256]{3,2,1,0:T(8,128)(2,1)}, bf16[2,2,320,256]{3,2,1,0:T(8,128)(2,1)}, u32[]{:S(2)}, u32[]{:S(2)}) collective-permute-start(bf16[2,2,320,256]{3,2,1,0:T(8,128)(2,1)} %pad_maximum_fusion.refs_0_), channel_id=1, source_target_pairs={{0,4},{2,6},{4,0},{6,2},{1,5},{3,7},{5,1},{7,3},{8,12},{10,14},{12... | collective-permute-start | bytes 1966088 | tf_op jit(solution)/shard_map/ppermute | solution.py:302
  125.4 1.9 %collective-permute-start.1 = (bf16[2,2,320,256]{3,2,1,0:T(8,128)(2,1)}, bf16[2,2,320,256]{3,2,1,0:T(8,128)(2,1)}, u32[]{:S(2)}, u32[]{:S(2)}) collective-permute-start(bf16[2,2,320,256]{3,2,1,0:T(8,128)(2,1)} %pad_maximum_fusion.refs_0_), channel_id=1, source_target_pairs={{0,2},{2,4},{4,6},{6,0},{1,3},{3,5},{5,7},{7,1},{8,10},{10,12},{12... | collective-permute-start | bytes 1966088 | tf_op jit(solution)/shard_map/ppermute | solution.py:302
  128.0 1.5 all-to-all-done.4
  129.4 13.0 %all_gather.13.d_all = bf16[512,896]{1,0:T(8,128)(2,1)S(1)} all-gather(bf16[128,896]{1,0:T(8,128)(2,1)} %bitcast.7), channel_id=1, replica_groups=mesh['y'=4,'zl'=8,'zh'=2,'x'=4,'c'=2] {'y'}, dimensions={0}, use_global_device_ids=true | all-gather | bytes 1146880 | tf_op jit(solution)/shard_map/all_gather | solution.py:299
  143.3 1.1 latent_grads.1
  145.0 10.1 %all-to-all-start.5 = ((f32[16,8,128]{2,1,0:T(8,128)}), f32[16,8,128]{2,1,0:T(8,128)}, u32[]{:S(2)}, u32[]{:S(2)}) async-start(f32[16,8,128]{2,1,0:T(8,128)} %copy-done.13), calls=%async_computation.5 | async-start | bytes 131072 | tf_op jit(solution)/shard_map/all_to_all | solution.py:33
  155.2 1.0 copy-done.4
  157.1 1.3 head_grads.1
  160.3 5.1 %base_product.1 = (f32[640,256]{1,0:T(8,128)S(1)}, f32[640,64]{1,0:T(8,128)S(1)}, bf16[640,320]{1,0:T(8,128)(2,1)S(1)}) custom-call(s32[16]{0:T(128)S(1)} %copy-done.26, bf16[2,2,320,256]{3,2,1,0:T(8,128)(2,1)} %pad_maximum_fusion.refs_0_, bf16[2,2,320,256]{3,2,1,0:T(8,128)(2,1)} %collective-permute-done.1.refs_1_, ...), custom_call_target="tpu_custom_call" | custom-call | flops 1000000 | bytes 100000 | tf_op jit(solution)/shard_map/base_product/pallas_call | solution.py:43
  165.4 2.6 %all-gather = bf16[1280,320]{1,0:T(8,128)(2,1)S(1)} all-gather(bf16[640,320]{1,0:T(8,128)(2,1)S(1)} %get-tuple-element.54), channel_id=2, replica_groups=mesh['y'=4,'zl'=8,'zh'=2,'x'=4,'c'=2] {'c'}, dimensions={0}, use_global_device_ids=true | all-gather | bytes 1228800 | tf_op jit(solution)/shard_map/all_gather | solution.py:342
  168.1 1.1 outputs.1
  169.9 1.7 trunk_grads.1
  (69 shorter events, 14.5 us)
Async XLA Ops:
  0.6 48.7 %collective-permute-start = (bf16[2,320,256]{2,1,0:T(8,128)(2,1)}, bf16[2,320,256]{2,1,0:T(8,128)(2,1)}, u32[]{:S(2)}, u32[]{:S(2)}) collective-permute-start(bf16[2,320,256]{2,1,0:T(8,128)(2,1)} %hidden.3), channel_id=1, source_target_pairs={{0,8},{8,0},{1,9},{9,1},{2,10},{10,2},{3,11},{11,3},{4,12},{12,4},... | collective-permute-start | bytes 983048 | tf_op jit(solution)/shard_map/ppermute | solution.py:256
  17.7 51.7 %copy-start.1 = (bf16[2,320,256]{2,1,0:T(8,128)(2,1)S(1)}, bf16[2,320,256]{2,1,0:T(8,128)(2,1)}, u32[]{:S(2)}) copy-start(bf16[2,320,256]{2,1,0:T(8,128)(2,1)} %hidden.3) | copy-start | bytes 983044
  17.8 51.7 %copy-start.24 = (s32[2]{0:T(128)S(1)}, s32[2]{0:T(128)}, u32[]{:S(2)}) copy-start(s32[2]{0:T(128)} %lengths.3) | copy-start | bytes 28
  31.8 17.6 %all-to-all-start = ((s32[8,16,128]{2,1,0:T(8,128)}), s32[8,16,128]{2,1,0:T(8,128)S(1)}, u32[]{:S(2)}, u32[]{:S(2)}) async-start(s32[8,16,128]{2,1,0:T(8,128)} %broadcast_in_dim.10), calls=%async_computation | async-start | bytes 131072 | tf_op jit(solution)/shard_map/all_to_all | solution.py:33
  36.6 1.0 copy-start.3
  37.6 1.0 copy-start.10
  38.6 0.7 copy-start.25
  40.8 0.7 copy-start.14
  42.2 53.1 %copy-start = (bf16[4096,256]{1,0:T(8,128)(2,1)S(1)}, bf16[4096,256]{1,0:T(8,128)(2,1)}, u32[]{:S(2)}) copy-start(bf16[4096,256]{1,0:T(8,128)(2,1)} %refs_4_.1) | copy-start | bytes 6291460
  42.2 53.1 %copy-start.2 = (bf16[4096,64]{0,1:T(8,128)(2,1)S(1)}, bf16[4096,64]{0,1:T(8,128)(2,1)}, u32[]{:S(2)}) copy-start(bf16[4096,64]{0,1:T(8,128)(2,1)} %param.24) | copy-start | bytes 1572868
  49.4 0.9 copy-start.15
  69.5 1.0 copy-start.5
  70.5 0.9 copy-start.11
  72.2 24.6 %copy-start.20 = (bf16[16,832]{1,0:T(8,128)(2,1)}, bf16[16,832]{1,0:T(8,128)(2,1)S(1)}, u32[]{:S(2)}) copy-start(bf16[16,832]{1,0:T(8,128)(2,1)S(1)} %get-tuple-element.55.ad) | copy-start | bytes 79876
  86.2 23.8 %all-to-all-start.3 = ((bf16[16,8,320]{2,1,0:T(8,128)(2,1)}), bf16[16,8,320]{2,1,0:T(8,128)(2,1)}, u32[]{:S(2)}, u32[]{:S(2)}) async-start(bf16[16,8,320]{2,1,0:T(8,128)(2,1)} %broadcast_in_dim.22), calls=%async_computation.3 | async-start | bytes 196608 | tf_op jit(solution)/shard_map/all_to_all | solution.py:33
  95.3 15.6 %copy-start.12 = (bf16[2,320,64]{1,2,0:T(8,128)(2,1)S(1)}, bf16[2,320,64]{1,2,0:T(8,128)(2,1)}, u32[]{:S(2)}) copy-start(bf16[2,320,64]{1,2,0:T(8,128)(2,1)} %param.27) | copy-start | bytes 245764
  95.4 15.6 %copy-start.27 = (s32[2]{0:T(128)S(1)}, s32[2]{0:T(128)}, u32[]{:S(2)}) copy-start(s32[2]{0:T(128)} %ids.1) | copy-start | bytes 28
  96.8 62.9 %collective-permute-start.4 = (bf16[2048,384]{1,0:T(8,128)(2,1)}, bf16[2048,384]{1,0:T(8,128)(2,1)}, u32[]{:S(2)}, u32[]{:S(2)}) collective-permute-start(bf16[2048,384]{1,0:T(8,128)(2,1)} %partner_rows.1), channel_id=1, source_target_pairs={{0,1},{1,0},{2,3},{3,2},{4,5},{5,4},{6,7},{7,6},{8,9},{9,8},{10,11... | collective-permute-start | bytes 4718600 | tf_op jit(solution)/shard_map/ppermute | solution.py:288
  111.0 18.4 %copy-start.8 = (f32[8,8,320]{2,1,0:T(8,128)}, f32[8,8,320]{2,1,0:T(8,128)S(1)}, u32[]{:S(2)}) copy-start(f32[8,8,320]{2,1,0:T(8,128)S(1)} %convert_reduce_fusion.low) | copy-start | bytes 245764
  112.5 16.9 %all-to-all-start.4 = ((bf16[8,16,896]{2,1,0:T(8,128)(2,1)}), bf16[8,16,896]{2,1,0:T(8,128)(2,1)}, u32[]{:S(2)}, u32[]{:S(2)}) async-start(bf16[8,16,896]{2,1,0:T(8,128)(2,1)} %adapter_grads.1), calls=%async_computation.4 | async-start | bytes 458752 | tf_op jit(solution)/shard_map/all_to_all | solution.py:33
  119.5 40.2 %collective-permute-start.3 = (bf16[2,2,320,256]{3,2,1,0:T(8,128)(2,1)}, bf16[2,2,320,256]{3,2,1,0:T(8,128)(2,1)}, u32[]{:S(2)}, u32[]{:S(2)}) collective-permute-start(bf16[2,2,320,256]{3,2,1,0:T(8,128)(2,1)} %pad_maximum_fusion.refs_0_), channel_id=1, source_target_pairs={{0,6},{2,0},{4,2},{6,4},{1,7},{3,1},{5,3},{7,5},{8,14},{10,8},{12,... | collective-permute-start | bytes 1966088 | tf_op jit(solution)/shard_map/ppermute | solution.py:302
  122.5 37.2 %collective-permute-start.2 = (bf16[2,2,320,256]{3,2,1,0:T(8,128)(2,1)}, bf16[2,2,320,256]{3,2,1,0:T(8,128)(2,1)}, u32[]{:S(2)}, u32[]{:S(2)}) collective-permute-start(bf16[2,2,320,256]{3,2,1,0:T(8,128)(2,1)} %pad_maximum_fusion.refs_0_), channel_id=1, source_target_pairs={{0,4},{2,6},{4,0},{6,2},{1,5},{3,7},{5,1},{7,3},{8,12},{10,14},{12... | collective-permute-start | bytes 1966088 | tf_op jit(solution)/shard_map/ppermute | solution.py:302
  125.4 34.3 %collective-permute-start.1 = (bf16[2,2,320,256]{3,2,1,0:T(8,128)(2,1)}, bf16[2,2,320,256]{3,2,1,0:T(8,128)(2,1)}, u32[]{:S(2)}, u32[]{:S(2)}) collective-permute-start(bf16[2,2,320,256]{3,2,1,0:T(8,128)(2,1)} %pad_maximum_fusion.refs_0_), channel_id=1, source_target_pairs={{0,2},{2,4},{4,6},{6,0},{1,3},{3,5},{5,7},{7,1},{8,10},{10,12},{12... | collective-permute-start | bytes 1966088 | tf_op jit(solution)/shard_map/ppermute | solution.py:302
  142.4 0.9 copy-start.7
  144.4 0.7 copy-start.13
  145.0 24.9 %all-to-all-start.5 = ((f32[16,8,128]{2,1,0:T(8,128)}), f32[16,8,128]{2,1,0:T(8,128)}, u32[]{:S(2)}, u32[]{:S(2)}) async-start(f32[16,8,128]{2,1,0:T(8,128)} %copy-done.13), calls=%async_computation.5 | async-start | bytes 131072 | tf_op jit(solution)/shard_map/all_to_all | solution.py:33
  155.2 1.0 copy-start.4
  156.2 0.9 copy-start.19
  159.6 8.4 %copy-start.9 = (f32[8,8,320]{2,1,0:T(8,128)S(1)}, f32[8,8,320]{2,1,0:T(8,128)}, u32[]{:S(2)}) copy-start(f32[8,8,320]{2,1,0:T(8,128)} %copy-done.8) | copy-start | bytes 245764
  159.6 8.4 %copy-start.21 = (bf16[16,832]{1,0:T(8,128)(2,1)S(1)}, bf16[16,832]{1,0:T(8,128)(2,1)}, u32[]{:S(2)}) copy-start(bf16[16,832]{1,0:T(8,128)(2,1)} %copy-done.20) | copy-start | bytes 79876
  165.4 4.5 %copy-start.17 = (bf16[64,1024]{1,0:T(8,128)(2,1)S(1)}, bf16[64,1024]{1,0:T(8,128)(2,1)}, u32[]{:S(2)}) copy-start(bf16[64,1024]{1,0:T(8,128)(2,1)} %copy-done.16) | copy-start | bytes 393220
  165.4 4.5 %copy-start.23 = (f32[16,64]{1,0:T(8,128)S(1)}, f32[16,64]{1,0:T(8,128)}, u32[]{:S(2)}) copy-start(f32[16,64]{1,0:T(8,128)} %copy-done.22) | copy-start | bytes 12292
  (5 other events, 3.2 us)

commit v5 on v4

--- a/solution.py
+++ b/solution.py
@@ -52,11 +52,12 @@
     )(*args)
 
 
-def tables_kernel(ny, nz, place, task_embed, w_in, module, lat_line, lat_own, sg_own):
+def tables_kernel(task_embed, w_in, module, lat_line, lat_own, sg_own):
+    ny, nz = lax.axis_size("y"), lax.axis_size("zl")
     latents = w_in.shape[1]
     rows = latents // (ny * nz)
     rank = lat_own.shape[2] // rows
-    y, z = place[0], place[1]
+    y, z = lax.axis_index("y"), lax.axis_index("zl")
     pre = mm(task_embed[...], w_in[...])
     q = iota((latents, lat_line.shape[2]), 1)
     line = iota((latents, lat_line.shape[2]), 0) == (
@@ -106,7 +107,14 @@
         low[s, 1] = back * row_weight(lengths, s, hidden.shape[1])
 
 
+def sum_halves(low, rank):
+    both = low[...].astype(f32)
+    rows = both.shape[0] // 2
+    return (both[:rows] + both[rows:]).reshape(rows // rank, rank, both.shape[1])
+
+
 def adapter_grad_kernel(wq, wv, rank, lengths, ids, low, hidden, grad_q, grad_vt, out, rows):
+    low = sum_halves(low, rank)
     for s in range(hidden.shape[0]):
         at = slice(s * rank, (s + 1) * rank)
         weight = row_weight(lengths, s, hidden.shape[1])
@@ -166,27 +174,34 @@
     hi = both.astype(bf16)
     lo = (both - hi.astype(f32)).astype(bf16)
     g_in[...] = mm(hi, embeds[...]) + mm(lo, embeds[...])
-    g_mod[...] = jnp.sum(d_pre, axis=1, keepdims=True)
-
-
-def give_kernel(core, base_q, base_vt, out):
+    ones = jnp.ones((1, batches), f32)
+    for m in range(2):
+        g_mod[m : m + 1, :] = mm_nt(ones, d_pre[m * rows // 2 : (m + 1) * rows // 2], exact)
+
+
+def give_kernel(base_q, base_vt, out):
+    partner = 1 - lax.axis_index("c")
     wq, wv = base_q.shape[1], base_vt.shape[0]
     out[...] = jnp.zeros_like(out)
     for n in range(out.shape[0] // wq):
-        at = pl.ds(pl.multiple_of((2 * n + core[0]) * wq, wq), wq)
+        at = pl.ds(pl.multiple_of((2 * n + partner) * wq, wq), wq)
         to = slice(n * wq, (n + 1) * wq)
         out[to, :wq] = base_q[at, :]
         out[to, wq : wq + wv] = base_vt[:, at].astype(f32).T.astype(bf16)
 
 
-def base_kernel(order, *refs):
+def base_kernel(*refs):
     near = refs[:4]
     base_q, base_vt, theirs, acc_q, acc_v, out = refs[4:]
     halves, seqs, length, wq = near[0].shape
-    for n in range(halves * len(near)):
+    zh, x, c = (lax.axis_index(a) for a in ("zh", "x", "c"))
+    nx, nc = len(near), lax.axis_size("c")
+    for n in range(halves * nx):
+        k, half = n // halves, n % halves
+        block = lax.rem(zh + half, halves) * nx + lax.rem(x - k + nx, nx)
         h = near[n // halves][n % halves].reshape(seqs * length, wq)
-        at = pl.ds(pl.multiple_of(order[2 * n] * wq, wq), wq)
-        far = pl.ds(pl.multiple_of(order[2 * n + 1] * wq, wq), wq)
+        at = pl.ds(pl.multiple_of((block * nc + c) * wq, wq), wq)
+        far = pl.ds(pl.multiple_of(block * wq, wq), wq)
         adds = mm(h, base_q[at, :]), mm_nt(h, base_vt[:, at])
         partner = mm(h, theirs[far, :])
         if n == 0:
@@ -199,7 +214,9 @@
     out[...] = both[:, : out.shape[1]].astype(bf16)
 
 
-def out_kernel(rank, core, acc_q, acc_v, got, low, ad, q_out, vt_out):
+def out_kernel(rank, acc_q, acc_v, got, low, ad, q_out, vt_out):
+    low = sum_halves(low, rank)
+    partner = 1 - lax.axis_index("c")
     seqs, length, wq = q_out.shape
     both = ad[...].astype(f32)
     first = ((0,), (0,))
@@ -208,7 +225,7 @@
         b = both[s * rank : (s + 1) * rank, :].astype(bf16)
         low_q = mm(low[4 * s].astype(bf16), b[:, wq : 2 * wq], first)
         low_v = mm(b[:, 3 * wq :], low[4 * s + 1].astype(bf16), first)
-        theirs = got[core[0], own, :].astype(f32)
+        theirs = got[partner, own, :].astype(f32)
         got_q, got_v = theirs[:, :wq], theirs[:, wq:]
         q_out[s] = (acc_q[own, :] + got_q + scale * low_q).astype(bf16)
         vt_out[s] = ((acc_v[own, :] + got_v).T + scale * low_v).astype(bf16)
@@ -231,7 +248,6 @@
     grad_v,
 ):
     ny, nz, nh, nx, nc = (lax.axis_size(a) for a in ("y", "zl", "zh", "x", "c"))
-    y, zl, zh, x, c = (lax.axis_index(a) for a in ("y", "zl", "zh", "x", "c"))
     xc, head = ("x", "c"), ("zh", "x", "c")
     seqs, length, wq = hidden_in.shape
     rows, rank, _ = wa_q.shape
@@ -243,14 +259,13 @@
 
     packed = jnp.concatenate([wa_q, wb_q, wa_v, wb_v], axis=2).reshape(rows * rank, width)
     w_line = lax.all_gather(packed, "y", axis=0, tiled=True)
-    ids, w_line = lax.optimization_barrier((task_ids, w_line))
-    ids_rows = jnp.broadcast_to(ids[:, None, None], (seqs, rank, 128)).reshape(seqs * rank, 128)
-    ids_line = spread(ids_rows, "zl", nz)
+    ids_rows = jnp.broadcast_to(task_ids[None, :, None, None], (nz, seqs, rank, 128))
+    ids_rows, w_line = lax.optimization_barrier((ids_rows.reshape(nz, seqs * rank, 128), w_line))
+    ids_line = swap(ids_rows, "zl")
     lat_line, lat_own, sg_own = local(
-        functools.partial(tables_kernel, ny, nz),
+        tables_kernel,
         [((2, tasks, ny * rows * rank), bf16), ((2, tasks, rows * rank), bf16), ((2 * rows, tasks), f32)],
-        (jnp.stack([y, zl]).astype(jnp.int32), task_embed, w_in, module_embed),
-        scalars=1,
+        (task_embed, w_in, module_embed),
         name="tables",
     )
     other = lax.ppermute(hidden_in, "zh", [(0, 1), (1, 0)])
@@ -281,12 +296,11 @@
     (theirs,) = local(
         give_kernel,
         [((blocks * wq, wq + 128), bf16)],
-        (jnp.reshape(1 - c, (1,)).astype(jnp.int32), base_q, base_vt),
-        scalars=1,
+        (base_q, base_vt),
         name="partner_rows",
     )
     theirs = lax.ppermute(theirs, "c", pair)
-    low = jnp.sum(low.reshape(nh, 4 * seqs, rank, length).astype(f32), axis=0)
+    low = low.reshape(nh * 4 * seqs * rank, length)
     (d_own,) = local(
         functools.partial(adapter_grad_kernel, wq, wv, rank),
         [((nz, seqs * rank, width + 64), bf16)],
@@ -300,24 +314,16 @@
 
     both_z = jnp.stack([hidden_in, other])
     turned = [both_z] + [lax.ppermute(both_z, "x", [(i, (i + k) % nx) for i in range(nx)]) for k in range(1, nx)]
-    order = []
-    for k in range(nx):
-        for half in range(nh):
-            block = (zh ^ half) * nx + lax.rem(x - k + nx, nx)
-            order += [block * nc + c, block]
-    order = jnp.stack(order).astype(jnp.int32)
-    d_all, order = lax.optimization_barrier((d_all, order))
+    d_all, theirs = lax.optimization_barrier((d_all, theirs))
     acc_q, acc_v, given = local(
         base_kernel,
         [((seqs * length, wq), f32), ((seqs * length, wv), f32), ((seqs * length, wq + wv), bf16)],
         (
-            order,
             *turned,
             base_q,
             base_vt,
             theirs,
         ),
-        scalars=1,
         mib=20,
         name="base_product",
     )
@@ -339,13 +345,12 @@
     q_out, vt_out = local(
         functools.partial(out_kernel, rank),
         [((seqs, length, wq), bf16), ((seqs, wv, length), bf16)],
-        (jnp.reshape(1 - c, (1,)).astype(jnp.int32), acc_q, acc_v, lax.all_gather(given, "c"), low, adapters),
-        scalars=1,
+        (acc_q, acc_v, lax.all_gather(given, "c"), low, adapters),
         name="outputs",
     )
-    d_lat, sg_all, embeds, g_aq, q_out = lax.optimization_barrier((d_lat, sg_all, embeds, g_aq, q_out))
+    d_lat, g_aq, q_out = lax.optimization_barrier((d_lat, g_aq, q_out))
     g_in, g_mod = local(
-        trunk_kernel, [((rows, emb), f32), ((2 * rows, 1), f32)], (d_lat, sg_all, embeds), name="trunk_grads"
+        trunk_kernel, [((rows, emb), f32), ((2, rows), f32)], (d_lat, sg_all, embeds), name="trunk_grads"
     )
 
     def cube(g):
@@ -359,7 +364,7 @@
         cube(g_av),
         cube(g_bv),
         g_in.T,
-        g_mod.reshape(2, rows),
+        g_mod,
     )
 
 

time: 174 us -> 173 us (level)
  blocking collectives: 59.5 us -> 64.3 us
  waiting for transfers between devices: 20.6 us -> 17.8 us
  local copies, waits for them, and re-layouts: 16.4 us -> 14.1 us
    all_to_all x2, blocking collectives: 32 us -> 36.9 us  [swap(): return lax.all_to_all(blocks, axes, 0, 0, tiled=True)]
    all_to_all x4, waiting for transfers between devices: 20.6 us -> 17.8 us  [swap(): return lax.all_to_all(blocks, axes, 0, 0, tiled=True)]
    unnamed x56 -> x54, local copies, waits for them, and re-layouts: 13 us -> 12.6 us
  transfers between devices with their start and end apart: 9 -> 9, of which waited for: 4 -> 4; matrix products, arithmetic and copies ran while one was open for 3% -> 2% of each run, Pallas kernels for 7% -> 8%
where the time goes in v5:
time: 173 us; the launch traced here: 171 us
  blocking collectives  64.3 us (37%)
  starting transfers between devices  56.3 us (33%)
  waiting for transfers between devices  17.8 us (10%)
  Pallas kernels  15.4 us (9%)
  local copies, waits for them, and re-layouts  14.1 us (8%)
  other arithmetic  2.7 us (2%)
    all_to_all x2, blocking collectives, swap(): return lax.all_to_all(blocks, axes, 0, 0, tiled=True)  36.9 us
    all_to_all x4, starting transfers between devices, swap(): return lax.all_to_all(blocks, axes, 0, 0, tiled=True)  28.1 us
    all_to_all x4, waiting for transfers between devices, swap(): return lax.all_to_all(blocks, axes, 0, 0, tiled=True)  17.8 us
    ppermute x1, starting transfers between devices, on_device(): other = lax.ppermute(hidden_in, 'zh', [(0, 1), (1, 0)])  16.3 us
    pallas_call x10, Pallas kernels, local(): pl.pallas_call(body, out_shape=tuple((jax.ShapeDtypeStruct(s, d) for s, d...  15.4 us
    all_gather x1, blocking collectives, on_device(): d_all = lax.all_gather(d_line, 'y', axis=0, tiled=True)  12.9 us
    unnamed x54, local copies, waits for them, and re-layouts  12.6 us
    all_gather x1, blocking collectives, on_device(): w_line = lax.all_gather(packed, 'y', axis=0, tiled=True)  11.9 us
  transfers between devices with their start and end apart: 9, of which 4 were waited for; matrix products, arithmetic and copies ran while one was open for 2% of the time, Pallas kernels for 8%

profile of v5, /device:TPU:1, one launch (start us, length us, event | category | flops | bytes accessed | tf_op | source)
XLA Modules:
  0.0 171.5 jit_solution(13316184750462151713)
XLA Ops:
  0.6 16.3 %collective-permute-start = (bf16[2,320,256]{2,1,0:T(8,128)(2,1)}, bf16[2,320,256]{2,1,0:T(8,128)(2,1)}, u32[]{:S(2)}, u32[]{:S(2)}) collective-permute-start(bf16[2,320,256]{2,1,0:T(8,128)(2,1)} %hidden.3), channel_id=1, source_target_pairs={{0,8},{8,0},{1,9},{9,1},{2,10},{10,2},{3,11},{11,3},{4,12},{12,4},... | collective-permute-start | bytes 983048 | tf_op jit(solution)/shard_map/ppermute | solution.py:271
  18.6 11.9 %all_gather.12.w_line = bf16[256,832]{1,0:T(8,128)(2,1)S(1)} all-gather(bf16[64,832]{1,0:T(8,128)(2,1)S(1)} %maximum_bitcast_fusion.weights), channel_id=1, replica_groups=mesh['y'=4,'zl'=8,'zh'=2,'x'=4,'c'=2] {'y'}, dimensions={0}, use_global_device_ids=true | all-gather | bytes 532480 | tf_op jit(solution)/shard_map/all_gather | solution.py:261
  31.2 5.0 %all-to-all-start = ((s32[8,16,128]{2,1,0:T(8,128)}), s32[8,16,128]{2,1,0:T(8,128)S(1)}, u32[]{:S(2)}, u32[]{:S(2)}) async-start(s32[8,16,128]{2,1,0:T(8,128)} %broadcast_in_dim.18), calls=%async_computation | async-start | bytes 131072 | tf_op jit(solution)/shard_map/all_to_all | solution.py:33
  36.2 1.0 copy-done.3
  37.2 1.0 copy-done.11
  38.9 0.9 tables.1
  40.5 8.5 %all-to-all-done.ids = s32[8,16,128]{2,1,0:T(8,128)S(1)} async-done(((s32[8,16,128]{2,1,0:T(8,128)}), s32[8,16,128]{2,1,0:T(8,128)S(1)}, u32[]{:S(2)}, u32[]{:S(2)}) %all-to-all-start) | async-done | bytes 65568 | tf_op jit(solution)/shard_map/all_to_all | solution.py:33
  50.2 7.7 %all-to-all-start.1 = ((bf16[8,16,832]{2,1,0:T(8,128)(2,1)}), bf16[8,16,832]{2,1,0:T(8,128)(2,1)S(1)}, u32[]{:S(2)}, u32[]{:S(2)}) async-start(bf16[8,16,832]{2,1,0:T(8,128)(2,1)} %bitcast.21), calls=%async_computation.1 | async-start | bytes 458752 | tf_op jit(solution)/shard_map/all_to_all | solution.py:33
  58.0 1.4 partner_rows.1
  59.4 3.1 %collective-permute-start.1 = (bf16[2048,384]{1,0:T(8,128)(2,1)}, bf16[2048,384]{1,0:T(8,128)(2,1)}, u32[]{:S(2)}, u32[]{:S(2)}) collective-permute-start(bf16[2048,384]{1,0:T(8,128)(2,1)} %partner_rows.1), channel_id=1, source_target_pairs={{0,1},{1,0},{2,3},{3,2},{4,5},{5,4},{6,7},{7,6},{8,9},{9,8},{10,11... | collective-permute-start | bytes 4718600 | tf_op jit(solution)/shard_map/ppermute | solution.py:302
  62.5 6.9 %all-to-all-done.1.got = bf16[8,16,832]{2,1,0:T(8,128)(2,1)S(1)} async-done(((bf16[8,16,832]{2,1,0:T(8,128)(2,1)}), bf16[8,16,832]{2,1,0:T(8,128)(2,1)S(1)}, u32[]{:S(2)}, u32[]{:S(2)}) %all-to-all-start.1) | async-done | bytes 213024 | tf_op jit(solution)/shard_map/all_to_all | solution.py:33
  71.8 13.4 %all_to_all.30 = f32[8,8,320]{2,1,0:T(8,128)S(1)} all-to-all(f32[8,8,320]{2,1,0:T(8,128)S(1)} %bitcast.26), channel_id=1, replica_groups=mesh['y'=4,'zl'=8,'zh'=2,'x'=4,'c'=2] {'x','c'}, dimensions={0} | all-to-all | bytes 163840 | tf_op jit(solution)/shard_map/all_to_all | solution.py:33
  85.2 23.5 %all_to_all.31 = bf16[16,8,320]{2,1,0:T(8,128)(2,1)S(1)} all-to-all(bf16[16,8,320]{2,1,0:T(8,128)(2,1)S(1)} %broadcast_in_dim.19), channel_id=1, replica_groups=mesh['y'=4,'zl'=8,'zh'=2,'x'=4,'c'=2] {'zh','x','c'}, dimensions={0} | all-to-all | bytes 163840 | tf_op jit(solution)/shard_map/all_to_all | solution.py:33
  109.6 1.5 adapter_grads.1
  111.7 5.1 %all-to-all-start.4 = ((bf16[8,16,896]{2,1,0:T(8,128)(2,1)}), bf16[8,16,896]{2,1,0:T(8,128)(2,1)S(1)}, u32[]{:S(2)}, u32[]{:S(2)}) async-start(bf16[8,16,896]{2,1,0:T(8,128)(2,1)} %adapter_grads.1), calls=%async_computation.4 | async-start | bytes 458752 | tf_op jit(solution)/shard_map/all_to_all | solution.py:33
  116.9 1.9 %pad_maximum_fusion.refs_0_ = bf16[2,2,320,256]{3,2,1,0:T(8,128)(2,1)} fusion(bf16[1,2,320,256]{3,2,1,0:T(8,128)(2,1)} %bitcast.8, bf16[1,2,320,256]{3,2,1,0:T(8,128)(2,1)S(1)} %bitcast.18), kind=kLoop, calls=%fused_computation | loop fusion | flops 327680 | bytes 1310720 | tf_op jit(solution)/shard_map/stack | solution.py:315
  118.7 2.2 %collective-permute-start.2 = (bf16[2,2,320,256]{3,2,1,0:T(8,128)(2,1)}, bf16[2,2,320,256]{3,2,1,0:T(8,128)(2,1)}, u32[]{:S(2)}, u32[]{:S(2)}) collective-permute-start(bf16[2,2,320,256]{3,2,1,0:T(8,128)(2,1)} %pad_maximum_fusion.refs_0_), channel_id=1, source_target_pairs={{0,2},{2,4},{4,6},{6,0},{1,3},{3,5},{5,7},{7,1},{8,10},{10,12},{12... | collective-permute-start | bytes 1966088 | tf_op jit(solution)/shard_map/ppermute | solution.py:316
  120.9 3.9 %collective-permute-start.3 = (bf16[2,2,320,256]{3,2,1,0:T(8,128)(2,1)}, bf16[2,2,320,256]{3,2,1,0:T(8,128)(2,1)}, u32[]{:S(2)}, u32[]{:S(2)}) collective-permute-start(bf16[2,2,320,256]{3,2,1,0:T(8,128)(2,1)} %pad_maximum_fusion.refs_0_), channel_id=1, source_target_pairs={{0,4},{2,6},{4,0},{6,2},{1,5},{3,7},{5,1},{7,3},{8,12},{10,14},{12... | collective-permute-start | bytes 1966088 | tf_op jit(solution)/shard_map/ppermute | solution.py:316
  124.8 2.7 %collective-permute-start.4 = (bf16[2,2,320,256]{3,2,1,0:T(8,128)(2,1)}, bf16[2,2,320,256]{3,2,1,0:T(8,128)(2,1)}, u32[]{:S(2)}, u32[]{:S(2)}) collective-permute-start(bf16[2,2,320,256]{3,2,1,0:T(8,128)(2,1)} %pad_maximum_fusion.refs_0_), channel_id=1, source_target_pairs={{0,6},{2,0},{4,2},{6,4},{1,7},{3,1},{5,3},{7,5},{8,14},{10,8},{12,... | collective-permute-start | bytes 1966088 | tf_op jit(solution)/shard_map/ppermute | solution.py:316
  127.5 1.1 all-to-all-done.4
  129.2 12.9 %all_gather.13.d_all = bf16[512,896]{1,0:T(8,128)(2,1)S(1)} all-gather(bf16[128,896]{1,0:T(8,128)(2,1)} %bitcast.27), channel_id=1, replica_groups=mesh['y'=4,'zl'=8,'zh'=2,'x'=4,'c'=2] {'y'}, dimensions={0}, use_global_device_ids=true | all-gather | bytes 1146880 | tf_op jit(solution)/shard_map/all_gather | solution.py:313
  142.1 0.9 copy-done.7
  143.0 1.1 latent_grads.1
  144.8 10.3 %all-to-all-start.5 = ((f32[16,8,128]{2,1,0:T(8,128)}), f32[16,8,128]{2,1,0:T(8,128)}, u32[]{:S(2)}, u32[]{:S(2)}) async-start(f32[16,8,128]{2,1,0:T(8,128)} %copy-done.14), calls=%async_computation.5 | async-start | bytes 131072 | tf_op jit(solution)/shard_map/all_to_all | solution.py:33
  155.1 1.0 copy-done.4
  156.1 0.9 copy-done.18
  157.0 1.3 head_grads.1
  159.5 5.1 %base_product.1 = (f32[640,256]{1,0:T(8,128)S(1)}, f32[640,64]{1,0:T(8,128)S(1)}, bf16[640,320]{1,0:T(8,128)(2,1)S(1)}) custom-call(bf16[2,2,320,256]{3,2,1,0:T(8,128)(2,1)} %pad_maximum_fusion.refs_0_, bf16[2,2,320,256]{3,2,1,0:T(8,128)(2,1)} %collective-permute-done.2.refs_1_, bf16[2,2,320,256]{3,2,1,0:T(8,128)(2,1)} %collective-permute-done.3.refs_2_, ...), custom_call_target="tpu_custom_call" | custom-call | flops 1000000 | bytes 100000 | tf_op jit(solution)/shard_map/base_product/pallas_call | solution.py:43
  164.7 2.6 %all-gather = bf16[1280,320]{1,0:T(8,128)(2,1)S(1)} all-gather(bf16[640,320]{1,0:T(8,128)(2,1)S(1)} %get-tuple-element.50), channel_id=2, replica_groups=mesh['y'=4,'zl'=8,'zh'=2,'x'=4,'c'=2] {'c'}, dimensions={0}, use_global_device_ids=true | all-gather | bytes 1228800 | tf_op jit(solution)/shard_map/all_gather | solution.py:348
  167.3 1.1 outputs.1
  168.4 1.4 all-to-all-done.5.got
  169.8 1.7 trunk_grads.1
  (62 shorter events, 11.4 us)
Async XLA Ops:
  0.6 48.4 %collective-permute-start = (bf16[2,320,256]{2,1,0:T(8,128)(2,1)}, bf16[2,320,256]{2,1,0:T(8,128)(2,1)}, u32[]{:S(2)}, u32[]{:S(2)}) collective-permute-start(bf16[2,320,256]{2,1,0:T(8,128)(2,1)} %hidden.3), channel_id=1, source_target_pairs={{0,8},{8,0},{1,9},{9,1},{2,10},{10,2},{3,11},{11,3},{4,12},{12,4},... | collective-permute-start | bytes 983048 | tf_op jit(solution)/shard_map/ppermute | solution.py:271
  18.5 31.7 %copy-start.6 = (bf16[64,832]{1,0:T(8,128)(2,1)}, bf16[64,832]{1,0:T(8,128)(2,1)S(1)}, u32[]{:S(2)}) copy-start(bf16[64,832]{1,0:T(8,128)(2,1)S(1)} %maximum_bitcast_fusion.weights) | copy-start | bytes 319492
  18.6 39.4 %copy-start = (bf16[4096,256]{1,0:T(8,128)(2,1)S(1)}, bf16[4096,256]{1,0:T(8,128)(2,1)}, u32[]{:S(2)}) copy-start(bf16[4096,256]{1,0:T(8,128)(2,1)} %refs_4_.1) | copy-start | bytes 6291460
  18.6 39.4 %copy-start.2 = (bf16[4096,64]{0,1:T(8,128)(2,1)S(1)}, bf16[4096,64]{0,1:T(8,128)(2,1)}, u32[]{:S(2)}) copy-start(bf16[4096,64]{0,1:T(8,128)(2,1)} %param.24) | copy-start | bytes 1572868
  31.2 17.8 %all-to-all-start = ((s32[8,16,128]{2,1,0:T(8,128)}), s32[8,16,128]{2,1,0:T(8,128)S(1)}, u32[]{:S(2)}, u32[]{:S(2)}) async-start(s32[8,16,128]{2,1,0:T(8,128)} %broadcast_in_dim.18), calls=%async_computation | async-start | bytes 131072 | tf_op jit(solution)/shard_map/all_to_all | solution.py:33
  36.2 1.0 copy-start.3
  37.2 1.0 copy-start.11
  38.2 0.7 copy-start.24
  39.9 0.7 copy-start.17
  49.5 0.7 copy-start.8
  50.2 19.2 %all-to-all-start.1 = ((bf16[8,16,832]{2,1,0:T(8,128)(2,1)}), bf16[8,16,832]{2,1,0:T(8,128)(2,1)S(1)}, u32[]{:S(2)}, u32[]{:S(2)}) async-start(bf16[8,16,832]{2,1,0:T(8,128)(2,1)} %bitcast.21), calls=%async_computation.1 | async-start | bytes 458752 | tf_op jit(solution)/shard_map/all_to_all | solution.py:33
  57.9 11.5 %copy-start.1 = (bf16[2,320,256]{2,1,0:T(8,128)(2,1)S(1)}, bf16[2,320,256]{2,1,0:T(8,128)(2,1)}, u32[]{:S(2)}) copy-start(bf16[2,320,256]{2,1,0:T(8,128)(2,1)} %hidden.3) | copy-start | bytes 983044
  57.9 11.5 %copy-start.5 = (bf16[2,320,256]{2,1,0:T(8,128)(2,1)S(1)}, bf16[2,320,256]{2,1,0:T(8,128)(2,1)}, u32[]{:S(2)}) copy-start(bf16[2,320,256]{2,1,0:T(8,128)(2,1)} %grad_q.3) | copy-start | bytes 983044
  58.0 11.5 %copy-start.23 = (s32[2]{0:T(128)S(1)}, s32[2]{0:T(128)}, u32[]{:S(2)}) copy-start(s32[2]{0:T(128)} %lengths.3) | copy-start | bytes 28
  59.4 49.3 %copy-start.25 = (s32[2]{0:T(128)S(1)}, s32[2]{0:T(128)}, u32[]{:S(2)}) copy-start(s32[2]{0:T(128)} %ids.1) | copy-start | bytes 28
  59.4 82.7 %collective-permute-start.1 = (bf16[2048,384]{1,0:T(8,128)(2,1)}, bf16[2048,384]{1,0:T(8,128)(2,1)}, u32[]{:S(2)}, u32[]{:S(2)}) collective-permute-start(bf16[2048,384]{1,0:T(8,128)(2,1)} %partner_rows.1), channel_id=1, source_target_pairs={{0,1},{1,0},{2,3},{3,2},{4,5},{5,4},{6,7},{7,6},{8,9},{9,8},{10,11... | collective-permute-start | bytes 4718600 | tf_op jit(solution)/shard_map/ppermute | solution.py:302
  69.4 0.9 copy-start.12
  108.7 0.9 copy-start.13
  111.7 16.8 %all-to-all-start.4 = ((bf16[8,16,896]{2,1,0:T(8,128)(2,1)}), bf16[8,16,896]{2,1,0:T(8,128)(2,1)S(1)}, u32[]{:S(2)}, u32[]{:S(2)}) async-start(bf16[8,16,896]{2,1,0:T(8,128)(2,1)} %adapter_grads.1), calls=%async_computation.4 | async-start | bytes 458752 | tf_op jit(solution)/shard_map/all_to_all | solution.py:33
  118.7 40.8 %collective-permute-start.2 = (bf16[2,2,320,256]{3,2,1,0:T(8,128)(2,1)}, bf16[2,2,320,256]{3,2,1,0:T(8,128)(2,1)}, u32[]{:S(2)}, u32[]{:S(2)}) collective-permute-start(bf16[2,2,320,256]{3,2,1,0:T(8,128)(2,1)} %pad_maximum_fusion.refs_0_), channel_id=1, source_target_pairs={{0,2},{2,4},{4,6},{6,0},{1,3},{3,5},{5,7},{7,1},{8,10},{10,12},{12... | collective-permute-start | bytes 1966088 | tf_op jit(solution)/shard_map/ppermute | solution.py:316
  120.9 38.6 %collective-permute-start.3 = (bf16[2,2,320,256]{3,2,1,0:T(8,128)(2,1)}, bf16[2,2,320,256]{3,2,1,0:T(8,128)(2,1)}, u32[]{:S(2)}, u32[]{:S(2)}) collective-permute-start(bf16[2,2,320,256]{3,2,1,0:T(8,128)(2,1)} %pad_maximum_fusion.refs_0_), channel_id=1, source_target_pairs={{0,4},{2,6},{4,0},{6,2},{1,5},{3,7},{5,1},{7,3},{8,12},{10,14},{12... | collective-permute-start | bytes 1966088 | tf_op jit(solution)/shard_map/ppermute | solution.py:316
  124.8 34.7 %collective-permute-start.4 = (bf16[2,2,320,256]{3,2,1,0:T(8,128)(2,1)}, bf16[2,2,320,256]{3,2,1,0:T(8,128)(2,1)}, u32[]{:S(2)}, u32[]{:S(2)}) collective-permute-start(bf16[2,2,320,256]{3,2,1,0:T(8,128)(2,1)} %pad_maximum_fusion.refs_0_), channel_id=1, source_target_pairs={{0,6},{2,0},{4,2},{6,4},{1,7},{3,1},{5,3},{7,5},{8,14},{10,8},{12,... | collective-permute-start | bytes 1966088 | tf_op jit(solution)/shard_map/ppermute | solution.py:316
  128.6 0.7 copy-start.26
  142.1 0.9 copy-start.7
  144.8 25.0 %all-to-all-start.5 = ((f32[16,8,128]{2,1,0:T(8,128)}), f32[16,8,128]{2,1,0:T(8,128)}, u32[]{:S(2)}, u32[]{:S(2)}) async-start(f32[16,8,128]{2,1,0:T(8,128)} %copy-done.14), calls=%async_computation.5 | async-start | bytes 131072 | tf_op jit(solution)/shard_map/all_to_all | solution.py:33
  155.0 1.0 copy-start.4
  156.1 0.9 copy-start.18
  158.3 0.7 copy-start.15
  159.5 7.8 %copy-start.10 = (bf16[16,8,320]{2,1,0:T(8,128)(2,1)S(1)}, bf16[16,8,320]{2,1,0:T(8,128)(2,1)}, u32[]{:S(2)}) copy-start(bf16[16,8,320]{2,1,0:T(8,128)(2,1)} %copy-done.9) | copy-start | bytes 245764
  159.5 7.8 %copy-start.20 = (bf16[16,832]{1,0:T(8,128)(2,1)S(1)}, bf16[16,832]{1,0:T(8,128)(2,1)}, u32[]{:S(2)}) copy-start(bf16[16,832]{1,0:T(8,128)(2,1)} %copy-done.19) | copy-start | bytes 79876
  164.7 5.1 %copy-start.16 = (bf16[64,1024]{1,0:T(8,128)(2,1)S(1)}, bf16[64,1024]{1,0:T(8,128)(2,1)}, u32[]{:S(2)}) copy-start(bf16[64,1024]{1,0:T(8,128)(2,1)} %copy-done.15) | copy-start | bytes 393220
  164.7 5.1 %copy-start.22 = (f32[16,64]{1,0:T(8,128)S(1)}, f32[16,64]{1,0:T(8,128)}, u32[]{:S(2)}) copy-start(f32[16,64]{1,0:T(8,128)} %copy-done.21) | copy-start | bytes 12292
  (4 other events, 2.5 us)

commit v6 on v5

--- a/solution.py
+++ b/solution.py
@@ -76,13 +76,42 @@
         sg_own[m * rows : (m + 1) * rows, :] = mm_nt(mine, silu_grad(p), exact)
 
 
+def pick_tasks(ids, tasks):
+    at = ids[...].reshape(ids.shape[0] * ids.shape[1], ids.shape[2])[:, :1]
+    return (iota((at.shape[0], tasks), 1) == at).astype(f32).astype(bf16)
+
+
+def batch_kernel(rank, ids, lat_own, sg_own, task_embed, lat_rows, sg_all, embeds):
+    of_all = pick_tasks(ids, lat_own.shape[1])
+    ny, nz = lax.axis_size("y"), lax.axis_size("zl")
+    batches = of_all.shape[0]
+    seqs = batches // (ny * nz)
+
+    def ordered(repeat):
+        i, j = iota((batches * repeat, batches), 0) // repeat, iota((batches * repeat, batches), 1)
+        hit = (i // (nz * seqs) == (j // seqs) % ny) & ((i // seqs) % nz == j // (seqs * ny)) & (i % seqs == j % seqs)
+        return mm(hit.astype(f32).astype(bf16), of_all)
+
+    n, k = lat_rows.shape[1:]
+    pick = ordered(rank).astype(bf16)
+    same = iota((n, k), 0) % rank == iota((n, k), 1) % rank
+    for m in range(2):
+        lat_rows[m] = jnp.where(same, mm(pick, lat_own[m]), 0.0).astype(bf16)
+    one = ordered(1)
+    sg_all[...] = mm_nt(sg_own[...], one, exact)
+    embeds[...] = mm(one.astype(bf16), task_embed[...]).astype(bf16)
+
+
 def part_kernel(split, rank, ids, lat_line, w_line, part):
     n, k = part.shape[0], w_line.shape[0]
-    tasks = lat_line.shape[1]
-    at = ids[...].reshape(n, ids.shape[2])[:, :1]
-    pick = (iota((n, tasks), 1) == at).astype(f32).astype(bf16)
+    of_all = pick_tasks(ids, lat_line.shape[1])
+    i, j = iota((n, of_all.shape[0]), 0), iota((n, of_all.shape[0]), 1)
+    ny, y = lax.axis_size("y"), lax.axis_index("y")
+    seqs = ids.shape[1] // ny
+    mine = (i // (seqs * rank) == j // (seqs * ny)) & ((i // rank) % seqs == j % seqs) & ((j // seqs) % ny == y)
+    pick = mm(mine.astype(f32).astype(bf16), of_all).astype(bf16)
     same = iota((n, k), 0) % rank == iota((n, k), 1) % rank
-    for m, cols in enumerate((slice(0, split), slice(split, None))):
+    for m, cols in enumerate((slice(0, split), slice(split, part.shape[1]))):
         spread_lat = jnp.where(same, mm(pick, lat_line[m]), 0.0).astype(bf16)
         part[:, cols] = mm(spread_lat, w_line[:, cols]).astype(bf16)
 
@@ -145,22 +174,12 @@
         out[i] = both
 
 
-def head_grad_kernel(wq, wv, rank, d_all, lat_own, sg_own, task_embed, g_aq, g_bq, g_av, g_bv, sg_all, embeds):
-    n, k = d_all.shape[0], lat_own.shape[2]
-    tasks = lat_own.shape[1]
+def head_grad_kernel(wq, wv, d_all, lat_rows, g_aq, g_bq, g_av, g_bv):
     width = 3 * wq + wv
-    tail = d_all[:, 3 * wq :].astype(f32)
-    pick = (iota((n, tasks), 1).astype(f32) == tail[:, wv : wv + 1]).astype(f32)
-    same = iota((n, k), 0) % rank == iota((n, k), 1) % rank
-    lat = [jnp.where(same, mm(pick.astype(bf16), lat_own[m]), 0.0).astype(bf16) for m in range(2)]
-    g_q = mm(lat[0], d_all[:, : 2 * wq], ((0,), (0,)))
+    g_q = mm(lat_rows[0], d_all[:, : 2 * wq], ((0,), (0,)))
     g_aq[...], g_bq[...] = g_q[:, :wq], g_q[:, wq:]
-    g_v = mm(lat[1], d_all[:, 2 * wq : width], ((0,), (0,)))
+    g_v = mm(lat_rows[1], d_all[:, 2 * wq : width], ((0,), (0,)))
     g_av[...], g_bv[...] = g_v[:, :wq], g_v[:, wq:]
-    one = jnp.where(iota((n, tasks), 0) % rank == 0, pick, 0.0)
-    one = jnp.sum(one.reshape(n // rank, rank, tasks), axis=1)
-    sg_all[...] = mm_nt(sg_own[...], one, exact)
-    embeds[...] = mm(one.astype(bf16), task_embed[...]).astype(bf16)
 
 
 def trunk_kernel(got, sg_all, embeds, g_in, g_mod):
@@ -196,20 +215,24 @@
     halves, seqs, length, wq = near[0].shape
     zh, x, c = (lax.axis_index(a) for a in ("zh", "x", "c"))
     nx, nc = len(near), lax.axis_size("c")
-    for n in range(halves * nx):
-        k, half = n // halves, n % halves
-        block = lax.rem(zh + half, halves) * nx + lax.rem(x - k + nx, nx)
-        h = near[n // halves][n % halves].reshape(seqs * length, wq)
-        at = pl.ds(pl.multiple_of((block * nc + c) * wq, wq), wq)
-        far = pl.ds(pl.multiple_of(block * wq, wq), wq)
-        adds = mm(h, base_q[at, :]), mm_nt(h, base_vt[:, at])
-        partner = mm(h, theirs[far, :])
-        if n == 0:
-            acc_q[...], acc_v[...] = adds
+    for pair in range(0, nx, 2):
+        hs, at, far = [], [], []
+        for k in (pair, pair + 1):
+            for half in range(halves):
+                block = lax.rem(zh + half, halves) * nx + lax.rem(x - k + nx, nx)
+                hs.append(near[k][half].reshape(seqs * length, wq))
+                at.append(pl.ds(pl.multiple_of((block * nc + c) * wq, wq), wq))
+                far.append(pl.ds(pl.multiple_of(block * wq, wq), wq))
+        h = jnp.concatenate(hs, axis=1)
+        add_q = mm(h, jnp.concatenate([base_q[i, :] for i in at], axis=0))
+        add_v = mm_nt(h, jnp.concatenate([base_vt[:, i] for i in at], axis=1))
+        partner = mm(h, jnp.concatenate([theirs[i, :] for i in far], axis=0))
+        if pair == 0:
+            acc_q[...], acc_v[...] = add_q, add_v
             both = partner
         else:
-            acc_q[...] += adds[0]
-            acc_v[...] += adds[1]
+            acc_q[...] += add_q
+            acc_v[...] += add_v
             both += partner
     out[...] = both[:, : out.shape[1]].astype(bf16)
 
@@ -257,10 +280,12 @@
     batches = seqs * ny * nz
     grad_vt = grad_v.swapaxes(1, 2)
 
-    packed = jnp.concatenate([wa_q, wb_q, wa_v, wb_v], axis=2).reshape(rows * rank, width)
+    each = rows * rank // seqs
+    id_cols = jnp.broadcast_to(task_ids.astype(bf16)[:, None, None], (seqs, each, 64)).reshape(rows, rank, 64)
+    packed = jnp.concatenate([wa_q, wb_q, wa_v, wb_v, id_cols], axis=2).reshape(rows * rank, width + 64)
     w_line = lax.all_gather(packed, "y", axis=0, tiled=True)
-    ids_rows = jnp.broadcast_to(task_ids[None, :, None, None], (nz, seqs, rank, 128))
-    ids_rows, w_line = lax.optimization_barrier((ids_rows.reshape(nz, seqs * rank, 128), w_line))
+    ids_rows = w_line.reshape(ny * seqs, each, width + 64)[:, 0, width].astype(jnp.int32)
+    ids_rows = jnp.broadcast_to(ids_rows[None, :, None], (nz, ny * seqs, 128))
     ids_line = swap(ids_rows, "zl")
     lat_line, lat_own, sg_own = local(
         tables_kernel,
@@ -277,7 +302,14 @@
         (ids_line, lat_line, w_line),
         name="adapter_parts",
     )
+    lat_rows, sg_all, embeds = local(
+        functools.partial(batch_kernel, rank),
+        [((2, batches * rank, rows * rank), bf16), ((2 * rows, batches), f32), ((batches, emb), bf16)],
+        (ids_line, lat_own, sg_own, task_embed),
+        name="batch_tables",
+    )
     got = swap(part.reshape(nz, seqs * rank, width), "zl")
+    got, lat_rows, sg_all, embeds = lax.optimization_barrier((got, lat_rows, sg_all, embeds))
     adapters, low = local(
         functools.partial(low_kernel, wq, wv, rank),
         [((seqs * rank, width), bf16), ((seqs, 2, 2 * rank, length), f32)],
@@ -334,14 +366,12 @@
         name="latent_grads",
     )
     d_lat = swap(d_lat, head)
-    g_aq, g_bq, g_av, g_bv, sg_all, embeds = local(
-        functools.partial(head_grad_kernel, wq, wv, rank),
-        [((rows * rank, wq), f32)] * 3
-        + [((rows * rank, wv), f32), ((2 * rows, batches), f32), ((batches, emb), bf16)],
-        (d_all, lat_own, sg_own, task_embed),
+    g_aq, g_bq, g_av, g_bv = local(
+        functools.partial(head_grad_kernel, wq, wv),
+        [((rows * rank, wq), f32)] * 3 + [((rows * rank, wv), f32)],
+        (d_all, lat_rows),
         name="head_grads",
     )
-
     q_out, vt_out = local(
         functools.partial(out_kernel, rank),
         [((seqs, length, wq), bf16), ((seqs, wv, length), bf16)],

time: 173 us -> 171 us (0.988)
    unnamed x54 -> x57, local copies, waits for them, and re-layouts: 12.6 us -> 10.6 us
    pallas_call x10 -> x11, Pallas kernels: 15.4 us -> 16 us  [local(): pl.pallas_call(body, out_shape=tuple((jax.ShapeDtypeStruct(s, d) for s, d...]
  transfers between devices with their start and end apart: 9 -> 9, of which waited for: 4 -> 4; matrix products, arithmetic and copies ran while one was open for 2% -> 3% of each run, Pallas kernels for 8% -> 8%
where the time goes in v6:
time: 171 us; the launch traced here: 170 us
  blocking collectives  64.3 us (38%)
  starting transfers between devices  56.4 us (33%)
  waiting for transfers between devices  17.1 us (10%)
  Pallas kernels  16 us (9%)
  local copies, waits for them, and re-layouts  12.6 us (7%)
  other arithmetic  2.55 us (1%)
    all_to_all x2, blocking collectives, swap(): return lax.all_to_all(blocks, axes, 0, 0, tiled=True)  36.8 us
    all_to_all x4, starting transfers between devices, swap(): return lax.all_to_all(blocks, axes, 0, 0, tiled=True)  28.6 us
    all_to_all x4, waiting for transfers between devices, swap(): return lax.all_to_all(blocks, axes, 0, 0, tiled=True)  17.1 us
    ppermute x1, starting transfers between devices, on_device(): other = lax.ppermute(hidden_in, 'zh', [(0, 1), (1, 0)])  16.3 us
    pallas_call x11, Pallas kernels, local(): pl.pallas_call(body, out_shape=tuple((jax.ShapeDtypeStruct(s, d) for s, d...  16 us
    all_gather x1, blocking collectives, on_device(): d_all = lax.all_gather(d_line, 'y', axis=0, tiled=True)  13 us
    all_gather x1, blocking collectives, on_device(): w_line = lax.all_gather(packed, 'y', axis=0, tiled=True)  11.9 us
    unnamed x57, local copies, waits for them, and re-layouts  10.6 us
  transfers between devices with their start and end apart: 9, of which 4 were waited for; matrix products, arithmetic and copies ran while one was open for 3% of the time, Pallas kernels for 8%

profile of v6, /device:TPU:1, one launch (start us, length us, event | category | flops | bytes accessed | tf_op | source)
XLA Modules:
  0.0 169.9 jit_solution(16019705467457856687)
XLA Ops:
  0.6 16.3 %collective-permute-start = (bf16[2,320,256]{2,1,0:T(8,128)(2,1)}, bf16[2,320,256]{2,1,0:T(8,128)(2,1)}, u32[]{:S(2)}, u32[]{:S(2)}) collective-permute-start(bf16[2,320,256]{2,1,0:T(8,128)(2,1)} %hidden.3), channel_id=1, source_target_pairs={{0,8},{8,0},{1,9},{9,1},{2,10},{10,2},{3,11},{11,3},{4,12},{12,4},... | collective-permute-start | bytes 983048 | tf_op jit(solution)/shard_map/ppermute | solution.py:296
  18.0 0.9 concatenate.16.weights
  18.9 11.9 %all_gather.12.w_line = bf16[256,896]{1,0:T(8,128)(2,1)S(1)} all-gather(bf16[64,896]{1,0:T(8,128)(2,1)S(1)} %concatenate.16.weights), channel_id=1, replica_groups=mesh['y'=4,'zl'=8,'zh'=2,'x'=4,'c'=2] {'y'}, dimensions={0}, use_global_device_ids=true | all-gather | bytes 573440 | tf_op jit(solution)/shard_map/all_gather | solution.py:286
  31.7 5.0 %all-to-all-start = ((s32[8,8,128]{2,1,0:T(8,128)}), s32[8,8,128]{2,1,0:T(8,128)S(1)}, u32[]{:S(2)}, u32[]{:S(2)}) async-start(s32[8,8,128]{2,1,0:T(8,128)} %broadcast_in_dim.31), calls=%async_computation | async-start | bytes 65536 | tf_op jit(solution)/shard_map/all_to_all | solution.py:33
  36.7 1.0 copy-done.3
  37.7 1.0 copy-done.11
  39.4 0.9 tables.1
  41.0 6.9 %all-to-all-done.ids = s32[8,8,128]{2,1,0:T(8,128)S(1)} async-done(((s32[8,8,128]{2,1,0:T(8,128)}), s32[8,8,128]{2,1,0:T(8,128)S(1)}, u32[]{:S(2)}, u32[]{:S(2)}) %all-to-all-start) | async-done | bytes 32800 | tf_op jit(solution)/shard_map/all_to_all | solution.py:33
  49.2 7.5 %all-to-all-start.1 = ((bf16[8,16,832]{2,1,0:T(8,128)(2,1)}), bf16[8,16,832]{2,1,0:T(8,128)(2,1)S(1)}, u32[]{:S(2)}, u32[]{:S(2)}) async-start(bf16[8,16,832]{2,1,0:T(8,128)(2,1)} %bitcast.28), calls=%async_computation.1 | async-start | bytes 458752 | tf_op jit(solution)/shard_map/all_to_all | solution.py:33
  56.8 1.4 partner_rows.1
  58.3 3.0 %collective-permute-start.1 = (bf16[2048,384]{1,0:T(8,128)(2,1)}, bf16[2048,384]{1,0:T(8,128)(2,1)}, u32[]{:S(2)}, u32[]{:S(2)}) collective-permute-start(bf16[2048,384]{1,0:T(8,128)(2,1)} %partner_rows.1), channel_id=1, source_target_pairs={{0,1},{1,0},{2,3},{3,2},{4,5},{5,4},{6,7},{7,6},{8,9},{9,8},{10,11... | collective-permute-start | bytes 4718600 | tf_op jit(solution)/shard_map/ppermute | solution.py:334
  63.5 4.8 %all-to-all-done.1.got = bf16[8,16,832]{2,1,0:T(8,128)(2,1)S(1)} async-done(((bf16[8,16,832]{2,1,0:T(8,128)(2,1)}), bf16[8,16,832]{2,1,0:T(8,128)(2,1)S(1)}, u32[]{:S(2)}, u32[]{:S(2)}) %all-to-all-start.1) | async-done | bytes 213024 | tf_op jit(solution)/shard_map/all_to_all | solution.py:33
  70.0 13.3 %all_to_all.30 = f32[8,8,320]{2,1,0:T(8,128)S(1)} all-to-all(f32[8,8,320]{2,1,0:T(8,128)S(1)} %bitcast.33), channel_id=1, replica_groups=mesh['y'=4,'zl'=8,'zh'=2,'x'=4,'c'=2] {'x','c'}, dimensions={0} | all-to-all | bytes 163840 | tf_op jit(solution)/shard_map/all_to_all | solution.py:33
  83.4 23.4 %all_to_all.31 = bf16[16,8,320]{2,1,0:T(8,128)(2,1)S(1)} all-to-all(bf16[16,8,320]{2,1,0:T(8,128)(2,1)S(1)} %broadcast_in_dim.32), channel_id=1, replica_groups=mesh['y'=4,'zl'=8,'zh'=2,'x'=4,'c'=2] {'zh','x','c'}, dimensions={0} | all-to-all | bytes 163840 | tf_op jit(solution)/shard_map/all_to_all | solution.py:33
  107.7 1.5 adapter_grads.1
  109.8 5.7 %all-to-all-start.4 = ((bf16[8,16,896]{2,1,0:T(8,128)(2,1)}), bf16[8,16,896]{2,1,0:T(8,128)(2,1)}, u32[]{:S(2)}, u32[]{:S(2)}) async-start(bf16[8,16,896]{2,1,0:T(8,128)(2,1)} %adapter_grads.1), calls=%async_computation.4 | async-start | bytes 458752 | tf_op jit(solution)/shard_map/all_to_all | solution.py:33
  115.5 1.9 %pad_maximum_fusion.refs_0_ = bf16[2,2,320,256]{3,2,1,0:T(8,128)(2,1)} fusion(bf16[1,2,320,256]{3,2,1,0:T(8,128)(2,1)} %bitcast.13, bf16[1,2,320,256]{3,2,1,0:T(8,128)(2,1)S(1)} %bitcast.24), kind=kLoop, calls=%fused_computation | loop fusion | flops 327680 | bytes 1310720 | tf_op jit(solution)/shard_map/stack | solution.py:347
  117.4 1.9 %collective-permute-start.2 = (bf16[2,2,320,256]{3,2,1,0:T(8,128)(2,1)}, bf16[2,2,320,256]{3,2,1,0:T(8,128)(2,1)}, u32[]{:S(2)}, u32[]{:S(2)}) collective-permute-start(bf16[2,2,320,256]{3,2,1,0:T(8,128)(2,1)} %pad_maximum_fusion.refs_0_), channel_id=1, source_target_pairs={{0,2},{2,4},{4,6},{6,0},{1,3},{3,5},{5,7},{7,1},{8,10},{10,12},{12... | collective-permute-start | bytes 1966088 | tf_op jit(solution)/shard_map/ppermute | solution.py:348
  119.3 4.3 %collective-permute-start.3 = (bf16[2,2,320,256]{3,2,1,0:T(8,128)(2,1)}, bf16[2,2,320,256]{3,2,1,0:T(8,128)(2,1)}, u32[]{:S(2)}, u32[]{:S(2)}) collective-permute-start(bf16[2,2,320,256]{3,2,1,0:T(8,128)(2,1)} %pad_maximum_fusion.refs_0_), channel_id=1, source_target_pairs={{0,4},{2,6},{4,0},{6,2},{1,5},{3,7},{5,1},{7,3},{8,12},{10,14},{12... | collective-permute-start | bytes 1966088 | tf_op jit(solution)/shard_map/ppermute | solution.py:348
  123.6 2.3 %collective-permute-start.4 = (bf16[2,2,320,256]{3,2,1,0:T(8,128)(2,1)}, bf16[2,2,320,256]{3,2,1,0:T(8,128)(2,1)}, u32[]{:S(2)}, u32[]{:S(2)}) collective-permute-start(bf16[2,2,320,256]{3,2,1,0:T(8,128)(2,1)} %pad_maximum_fusion.refs_0_), channel_id=1, source_target_pairs={{0,6},{2,0},{4,2},{6,4},{1,7},{3,1},{5,3},{7,5},{8,14},{10,8},{12,... | collective-permute-start | bytes 1966088 | tf_op jit(solution)/shard_map/ppermute | solution.py:348
  125.9 1.4 all-to-all-done.4
  127.3 13.0 %all_gather.13.d_all = bf16[512,896]{1,0:T(8,128)(2,1)S(1)} all-gather(bf16[128,896]{1,0:T(8,128)(2,1)} %bitcast.10), channel_id=1, replica_groups=mesh['y'=4,'zl'=8,'zh'=2,'x'=4,'c'=2] {'y'}, dimensions={0}, use_global_device_ids=true | all-gather | bytes 1146880 | tf_op jit(solution)/shard_map/all_gather | solution.py:345
  140.4 0.9 copy-done.7
  141.3 1.1 latent_grads.1
  143.0 10.5 %all-to-all-start.5 = ((f32[16,8,128]{2,1,0:T(8,128)}), f32[16,8,128]{2,1,0:T(8,128)}, u32[]{:S(2)}, u32[]{:S(2)}) async-start(f32[16,8,128]{2,1,0:T(8,128)} %copy-done.14), calls=%async_computation.5 | async-start | bytes 131072 | tf_op jit(solution)/shard_map/all_to_all | solution.py:33
  153.5 0.9 copy-done.16
  154.4 0.9 head_grads.1
  155.4 5.1 %base_product.1 = (f32[640,256]{1,0:T(8,128)S(1)}, f32[640,64]{1,0:T(8,128)S(1)}, bf16[640,320]{1,0:T(8,128)(2,1)S(1)}) custom-call(bf16[2,2,320,256]{3,2,1,0:T(8,128)(2,1)} %pad_maximum_fusion.refs_0_, bf16[2,2,320,256]{3,2,1,0:T(8,128)(2,1)} %collective-permute-done.2.refs_1_, bf16[2,2,320,256]{3,2,1,0:T(8,128)(2,1)} %collective-permute-done.3.refs_2_, ...), custom_call_target="tpu_custom_call" | custom-call | flops 1000000 | bytes 100000 | tf_op jit(solution)/shard_map/base_product/pallas_call | solution.py:43
  160.5 2.6 %all-gather = bf16[1280,320]{1,0:T(8,128)(2,1)S(1)} all-gather(bf16[640,320]{1,0:T(8,128)(2,1)S(1)} %get-tuple-element.56), channel_id=2, replica_groups=mesh['y'=4,'zl'=8,'zh'=2,'x'=4,'c'=2] {'c'}, dimensions={0}, use_global_device_ids=true | all-gather | bytes 1228800 | tf_op jit(solution)/shard_map/all_gather | solution.py:378
  163.2 1.1 outputs.1
  164.2 4.0 %all-to-all-done.5.got = f32[16,8,128]{2,1,0:T(8,128)} async-done(((f32[16,8,128]{2,1,0:T(8,128)}), f32[16,8,128]{2,1,0:T(8,128)}, u32[]{:S(2)}, u32[]{:S(2)}) %all-to-all-start.5) | async-done | bytes 65568 | tf_op jit(solution)/shard_map/all_to_all | solution.py:33
  168.2 1.7 trunk_grads.1
  (72 shorter events, 10.8 us)
Async XLA Ops:
  0.6 47.3 %collective-permute-start = (bf16[2,320,256]{2,1,0:T(8,128)(2,1)}, bf16[2,320,256]{2,1,0:T(8,128)(2,1)}, u32[]{:S(2)}, u32[]{:S(2)}) collective-permute-start(bf16[2,320,256]{2,1,0:T(8,128)(2,1)} %hidden.3), channel_id=1, source_target_pairs={{0,8},{8,0},{1,9},{9,1},{2,10},{10,2},{3,11},{11,3},{4,12},{12,4},... | collective-permute-start | bytes 983048 | tf_op jit(solution)/shard_map/ppermute | solution.py:296
  18.9 37.8 %copy-start.6 = (bf16[64,896]{1,0:T(8,128)(2,1)}, bf16[64,896]{1,0:T(8,128)(2,1)S(1)}, u32[]{:S(2)}) copy-start(bf16[64,896]{1,0:T(8,128)(2,1)S(1)} %concatenate.16.weights) | copy-start | bytes 344068
  18.9 37.8 %copy-start = (bf16[4096,256]{1,0:T(8,128)(2,1)S(1)}, bf16[4096,256]{1,0:T(8,128)(2,1)}, u32[]{:S(2)}) copy-start(bf16[4096,256]{1,0:T(8,128)(2,1)} %refs_4_.1) | copy-start | bytes 6291460
  18.9 37.8 %copy-start.2 = (bf16[4096,64]{0,1:T(8,128)(2,1)S(1)}, bf16[4096,64]{0,1:T(8,128)(2,1)}, u32[]{:S(2)}) copy-start(bf16[4096,64]{0,1:T(8,128)(2,1)} %param.24) | copy-start | bytes 1572868
  31.7 16.2 %all-to-all-start = ((s32[8,8,128]{2,1,0:T(8,128)}), s32[8,8,128]{2,1,0:T(8,128)S(1)}, u32[]{:S(2)}, u32[]{:S(2)}) async-start(s32[8,8,128]{2,1,0:T(8,128)} %broadcast_in_dim.31), calls=%async_computation | async-start | bytes 65536 | tf_op jit(solution)/shard_map/all_to_all | solution.py:33
  36.7 1.0 copy-start.3
  37.7 1.0 copy-start.11
  41.0 15.7 %copy-start.23 = (f32[16,240]{1,0:T(8,128)}, f32[16,240]{1,0:T(8,128)S(1)}, u32[]{:S(2)}) copy-start(f32[16,240]{1,0:T(8,128)S(1)} %get-tuple-element.43.sg_own) | copy-start | bytes 46084
  48.5 0.7 copy-start.8
  49.2 19.0 %all-to-all-start.1 = ((bf16[8,16,832]{2,1,0:T(8,128)(2,1)}), bf16[8,16,832]{2,1,0:T(8,128)(2,1)S(1)}, u32[]{:S(2)}, u32[]{:S(2)}) async-start(bf16[8,16,832]{2,1,0:T(8,128)(2,1)} %bitcast.28), calls=%async_computation.1 | async-start | bytes 458752 | tf_op jit(solution)/shard_map/all_to_all | solution.py:33
  56.7 4.6 %copy-start.4 = (bf16[240,1024]{1,0:T(8,128)(2,1)S(1)}, bf16[240,1024]{1,0:T(8,128)(2,1)}, u32[]{:S(2)}) copy-start(bf16[240,1024]{1,0:T(8,128)(2,1)} %task_embed.3) | copy-start | bytes 1474564
  56.8 4.6 %copy-start.20 = (bf16[2,240,64]{2,1,0:T(8,128)(2,1)S(1)}, bf16[2,240,64]{2,1,0:T(8,128)(2,1)}, u32[]{:S(2)}) copy-start(bf16[2,240,64]{2,1,0:T(8,128)(2,1)} %copy-done.19) | copy-start | bytes 184324
  56.8 4.5 %copy-start.24 = (f32[16,240]{1,0:T(8,128)S(1)}, f32[16,240]{1,0:T(8,128)}, u32[]{:S(2)}) copy-start(f32[16,240]{1,0:T(8,128)} %copy-done.23) | copy-start | bytes 46084
  56.8 11.5 %copy-start.1 = (bf16[2,320,256]{2,1,0:T(8,128)(2,1)S(1)}, bf16[2,320,256]{2,1,0:T(8,128)(2,1)}, u32[]{:S(2)}) copy-start(bf16[2,320,256]{2,1,0:T(8,128)(2,1)} %hidden.3) | copy-start | bytes 983044
  56.8 11.5 %copy-start.5 = (bf16[2,320,256]{2,1,0:T(8,128)(2,1)S(1)}, bf16[2,320,256]{2,1,0:T(8,128)(2,1)}, u32[]{:S(2)}) copy-start(bf16[2,320,256]{2,1,0:T(8,128)(2,1)} %grad_q.3) | copy-start | bytes 983044
  56.8 11.5 %copy-start.25 = (s32[2]{0:T(128)S(1)}, s32[2]{0:T(128)}, u32[]{:S(2)}) copy-start(s32[2]{0:T(128)} %lengths.3) | copy-start | bytes 28
  58.3 48.6 %copy-start.27 = (s32[2]{0:T(128)S(1)}, s32[2]{0:T(128)}, u32[]{:S(2)}) copy-start(s32[2]{0:T(128)} %ids.1) | copy-start | bytes 28
  58.3 82.1 %collective-permute-start.1 = (bf16[2048,384]{1,0:T(8,128)(2,1)}, bf16[2048,384]{1,0:T(8,128)(2,1)}, u32[]{:S(2)}, u32[]{:S(2)}) collective-permute-start(bf16[2048,384]{1,0:T(8,128)(2,1)} %partner_rows.1), channel_id=1, source_target_pairs={{0,1},{1,0},{2,3},{3,2},{4,5},{5,4},{6,7},{7,6},{8,9},{9,8},{10,11... | collective-permute-start | bytes 4718600 | tf_op jit(solution)/shard_map/ppermute | solution.py:334
  62.1 0.7 copy-start.15
  68.3 0.9 copy-start.12
  70.0 47.4 %copy-start.21 = (bf16[16,832]{1,0:T(8,128)(2,1)}, bf16[16,832]{1,0:T(8,128)(2,1)S(1)}, u32[]{:S(2)}) copy-start(bf16[16,832]{1,0:T(8,128)(2,1)S(1)} %get-tuple-element.57.ad) | copy-start | bytes 79876
  106.8 0.9 copy-start.13
  109.8 17.5 %all-to-all-start.4 = ((bf16[8,16,896]{2,1,0:T(8,128)(2,1)}), bf16[8,16,896]{2,1,0:T(8,128)(2,1)}, u32[]{:S(2)}, u32[]{:S(2)}) async-start(bf16[8,16,896]{2,1,0:T(8,128)(2,1)} %adapter_grads.1), calls=%async_computation.4 | async-start | bytes 458752 | tf_op jit(solution)/shard_map/all_to_all | solution.py:33
  117.4 38.0 %collective-permute-start.2 = (bf16[2,2,320,256]{3,2,1,0:T(8,128)(2,1)}, bf16[2,2,320,256]{3,2,1,0:T(8,128)(2,1)}, u32[]{:S(2)}, u32[]{:S(2)}) collective-permute-start(bf16[2,2,320,256]{3,2,1,0:T(8,128)(2,1)} %pad_maximum_fusion.refs_0_), channel_id=1, source_target_pairs={{0,2},{2,4},{4,6},{6,0},{1,3},{3,5},{5,7},{7,1},{8,10},{10,12},{12... | collective-permute-start | bytes 1966088 | tf_op jit(solution)/shard_map/ppermute | solution.py:348
  119.3 36.1 %collective-permute-start.3 = (bf16[2,2,320,256]{3,2,1,0:T(8,128)(2,1)}, bf16[2,2,320,256]{3,2,1,0:T(8,128)(2,1)}, u32[]{:S(2)}, u32[]{:S(2)}) collective-permute-start(bf16[2,2,320,256]{3,2,1,0:T(8,128)(2,1)} %pad_maximum_fusion.refs_0_), channel_id=1, source_target_pairs={{0,4},{2,6},{4,0},{6,2},{1,5},{3,7},{5,1},{7,3},{8,12},{10,14},{12... | collective-permute-start | bytes 1966088 | tf_op jit(solution)/shard_map/ppermute | solution.py:348
  123.6 31.8 %collective-permute-start.4 = (bf16[2,2,320,256]{3,2,1,0:T(8,128)(2,1)}, bf16[2,2,320,256]{3,2,1,0:T(8,128)(2,1)}, u32[]{:S(2)}, u32[]{:S(2)}) collective-permute-start(bf16[2,2,320,256]{3,2,1,0:T(8,128)(2,1)} %pad_maximum_fusion.refs_0_), channel_id=1, source_target_pairs={{0,6},{2,0},{4,2},{6,4},{1,7},{3,1},{5,3},{7,5},{8,14},{10,8},{12,... | collective-permute-start | bytes 1966088 | tf_op jit(solution)/shard_map/ppermute | solution.py:348
  140.3 0.9 copy-start.7
  143.0 25.2 %all-to-all-start.5 = ((f32[16,8,128]{2,1,0:T(8,128)}), f32[16,8,128]{2,1,0:T(8,128)}, u32[]{:S(2)}, u32[]{:S(2)}) async-start(f32[16,8,128]{2,1,0:T(8,128)} %copy-done.14), calls=%async_computation.5 | async-start | bytes 131072 | tf_op jit(solution)/shard_map/all_to_all | solution.py:33
  153.5 0.9 copy-start.16
  155.4 7.8 %copy-start.10 = (bf16[16,8,320]{2,1,0:T(8,128)(2,1)S(1)}, bf16[16,8,320]{2,1,0:T(8,128)(2,1)}, u32[]{:S(2)}) copy-start(bf16[16,8,320]{2,1,0:T(8,128)(2,1)} %copy-done.9) | copy-start | bytes 245764
  155.4 7.8 %copy-start.22 = (bf16[16,832]{1,0:T(8,128)(2,1)S(1)}, bf16[16,832]{1,0:T(8,128)(2,1)}, u32[]{:S(2)}) copy-start(bf16[16,832]{1,0:T(8,128)(2,1)} %copy-done.21) | copy-start | bytes 79876
  160.5 7.7 %copy-start.18 = (bf16[64,1024]{1,0:T(8,128)(2,1)S(1)}, bf16[64,1024]{1,0:T(8,128)(2,1)}, u32[]{:S(2)}) copy-start(bf16[64,1024]{1,0:T(8,128)(2,1)} %copy-done.17) | copy-start | bytes 393220
  (5 other events, 3.3 us)

commit v7 on v6

--- a/solution.py
+++ b/solution.py
@@ -131,9 +131,9 @@
         own = total[s * rank : (s + 1) * rank, :]
         a = jnp.concatenate([own[:, :wq], own[:, 2 * wq : 3 * wq]], axis=0).astype(bf16)
         b_q, b_v = own[:, wq : 2 * wq].astype(bf16), own[:, 3 * wq :].astype(bf16)
-        low[s, 0] = mm_nt(a, hidden[s])
+        low[s, 0] = mm_nt(a, hidden[s]).astype(low.dtype)
         back = jnp.concatenate([mm_nt(b_q, grad_q[s]), mm(b_v, grad_vt[s])], axis=0)
-        low[s, 1] = back * row_weight(lengths, s, hidden.shape[1])
+        low[s, 1] = (back * row_weight(lengths, s, hidden.shape[1])).astype(low.dtype)
 
 
 def sum_halves(low, rank):
@@ -169,7 +169,7 @@
         full = jnp.where(same, mm_nt(d_all[:, cols], weights[:, cols]), 0.0)
         by_batch = jnp.sum(full.reshape(n // rank, rank, k), axis=1)
         parts.append(mm_nt(fold, by_batch, exact))
-    both = jnp.concatenate(parts, axis=1)
+    both = jnp.concatenate(parts, axis=1).astype(out.dtype)
     for i in range(out.shape[0]):
         out[i] = both
 
@@ -183,9 +183,9 @@
 
 
 def trunk_kernel(got, sg_all, embeds, g_in, g_mod):
-    total = got[0]
+    total = got[0].astype(f32)
     for i in range(1, got.shape[0]):
-        total += got[i]
+        total += got[i].astype(f32)
     rows, batches = sg_all.shape
     total = jnp.concatenate([total[:, :batches], total[:, batches:]], axis=0)
     d_pre = total * sg_all[...]
@@ -312,14 +312,14 @@
     got, lat_rows, sg_all, embeds = lax.optimization_barrier((got, lat_rows, sg_all, embeds))
     adapters, low = local(
         functools.partial(low_kernel, wq, wv, rank),
-        [((seqs * rank, width), bf16), ((seqs, 2, 2 * rank, length), f32)],
+        [((seqs * rank, width), bf16), ((seqs, 2, 2 * rank, length), bf16)],
         (seq_lengths, got, hidden_in, grad_q, grad_vt),
         scalars=1,
         name="low_rank",
     )
 
     low = swap(low.reshape(nx * nc, seqs * 4 * rank // (nx * nc), length), xc)
-    low = jnp.sum(low, axis=0).astype(bf16)
+    low = jnp.sum(low.astype(f32), axis=0).astype(bf16)
     low = spread(low, head, nh * nx * nc)
 
     blocks = nh * nx
@@ -361,7 +361,7 @@
     )
     (d_lat,) = local(
         functools.partial(latent_grad_kernel, split, width, rank),
-        [((nh * nx * nc, rows, 2 * batches), f32)],
+        [((nh * nx * nc, rows, 2 * batches), bf16)],
         (d_all, packed),
         name="latent_grads",
     )

time: 171 us -> 171 us (level)
  no operation moved by 1% of the time
where the time goes in v7:
time: 171 us; the launch traced here: 169 us
  blocking collectives  64.1 us (37%)
  starting transfers between devices  56.4 us (33%)
  waiting for transfers between devices  17 us (10%)
  Pallas kernels  15.9 us (9%)
  local copies, waits for them, and re-layouts  12.6 us (7%)
  other arithmetic  2.55 us (1%)
    all_to_all x2, blocking collectives, swap(): return lax.all_to_all(blocks, axes, 0, 0, tiled=True)  36.5 us
    all_to_all x4, starting transfers between devices, swap(): return lax.all_to_all(blocks, axes, 0, 0, tiled=True)  28.6 us
    all_to_all x4, waiting for transfers between devices, swap(): return lax.all_to_all(blocks, axes, 0, 0, tiled=True)  17 us
    ppermute x1, starting transfers between devices, on_device(): other = lax.ppermute(hidden_in, 'zh', [(0, 1), (1, 0)])  16.3 us
    pallas_call x11, Pallas kernels, local(): pl.pallas_call(body, out_shape=tuple((jax.ShapeDtypeStruct(s, d) for s, d...  15.9 us
    all_gather x1, blocking collectives, on_device(): d_all = lax.all_gather(d_line, 'y', axis=0, tiled=True)  13 us
    all_gather x1, blocking collectives, on_device(): w_line = lax.all_gather(packed, 'y', axis=0, tiled=True)  11.9 us
    unnamed x57, local copies, waits for them, and re-layouts  10.6 us
  transfers between devices with their start and end apart: 9, of which 4 were waited for; matrix products, arithmetic and copies ran while one was open for 3% of the time, Pallas kernels for 8%

profile of v7, /device:TPU:1, one launch (start us, length us, event | category | flops | bytes accessed | tf_op | source)
XLA Modules:
  0.0 169.5 jit_solution(8153460386370187292)
XLA Ops:
  0.6 16.3 %collective-permute-start = (bf16[2,320,256]{2,1,0:T(8,128)(2,1)}, bf16[2,320,256]{2,1,0:T(8,128)(2,1)}, u32[]{:S(2)}, u32[]{:S(2)}) collective-permute-start(bf16[2,320,256]{2,1,0:T(8,128)(2,1)} %hidden.3), channel_id=1, source_target_pairs={{0,8},{8,0},{1,9},{9,1},{2,10},{10,2},{3,11},{11,3},{4,12},{12,4},... | collective-permute-start | bytes 983048 | tf_op jit(solution)/shard_map/ppermute | solution.py:296
  18.0 0.9 concatenate.16.weights
  18.9 11.9 %all_gather.12.w_line = bf16[256,896]{1,0:T(8,128)(2,1)S(1)} all-gather(bf16[64,896]{1,0:T(8,128)(2,1)S(1)} %concatenate.16.weights), channel_id=1, replica_groups=mesh['y'=4,'zl'=8,'zh'=2,'x'=4,'c'=2] {'y'}, dimensions={0}, use_global_device_ids=true | all-gather | bytes 573440 | tf_op jit(solution)/shard_map/all_gather | solution.py:286
  31.7 5.0 %all-to-all-start = ((s32[8,8,128]{2,1,0:T(8,128)}), s32[8,8,128]{2,1,0:T(8,128)S(1)}, u32[]{:S(2)}, u32[]{:S(2)}) async-start(s32[8,8,128]{2,1,0:T(8,128)} %broadcast_in_dim.31), calls=%async_computation | async-start | bytes 65536 | tf_op jit(solution)/shard_map/all_to_all | solution.py:33
  36.7 1.0 copy-done.3
  37.7 1.0 copy-done.11
  39.4 0.9 tables.1
  41.0 6.9 %all-to-all-done.ids = s32[8,8,128]{2,1,0:T(8,128)S(1)} async-done(((s32[8,8,128]{2,1,0:T(8,128)}), s32[8,8,128]{2,1,0:T(8,128)S(1)}, u32[]{:S(2)}, u32[]{:S(2)}) %all-to-all-start) | async-done | bytes 32800 | tf_op jit(solution)/shard_map/all_to_all | solution.py:33
  49.2 7.5 %all-to-all-start.1 = ((bf16[8,16,832]{2,1,0:T(8,128)(2,1)}), bf16[8,16,832]{2,1,0:T(8,128)(2,1)S(1)}, u32[]{:S(2)}, u32[]{:S(2)}) async-start(bf16[8,16,832]{2,1,0:T(8,128)(2,1)} %bitcast.28), calls=%async_computation.1 | async-start | bytes 458752 | tf_op jit(solution)/shard_map/all_to_all | solution.py:33
  56.8 1.4 partner_rows.1
  58.3 3.0 %collective-permute-start.1 = (bf16[2048,384]{1,0:T(8,128)(2,1)}, bf16[2048,384]{1,0:T(8,128)(2,1)}, u32[]{:S(2)}, u32[]{:S(2)}) collective-permute-start(bf16[2048,384]{1,0:T(8,128)(2,1)} %partner_rows.1), channel_id=1, source_target_pairs={{0,1},{1,0},{2,3},{3,2},{4,5},{5,4},{6,7},{7,6},{8,9},{9,8},{10,11... | collective-permute-start | bytes 4718600 | tf_op jit(solution)/shard_map/ppermute | solution.py:334
  63.5 4.8 %all-to-all-done.1.got = bf16[8,16,832]{2,1,0:T(8,128)(2,1)S(1)} async-done(((bf16[8,16,832]{2,1,0:T(8,128)(2,1)}), bf16[8,16,832]{2,1,0:T(8,128)(2,1)S(1)}, u32[]{:S(2)}, u32[]{:S(2)}) %all-to-all-start.1) | async-done | bytes 213024 | tf_op jit(solution)/shard_map/all_to_all | solution.py:33
  70.0 13.1 %all_to_all.30 = bf16[8,8,320]{2,1,0:T(8,128)(2,1)S(1)} all-to-all(bf16[8,8,320]{2,1,0:T(8,128)(2,1)S(1)} %bitcast.33), channel_id=1, replica_groups=mesh['y'=4,'zl'=8,'zh'=2,'x'=4,'c'=2] {'x','c'}, dimensions={0} | all-to-all | bytes 81920 | tf_op jit(solution)/shard_map/all_to_all | solution.py:33
  83.2 23.4 %all_to_all.31 = bf16[16,8,320]{2,1,0:T(8,128)(2,1)S(1)} all-to-all(bf16[16,8,320]{2,1,0:T(8,128)(2,1)S(1)} %broadcast_in_dim.32), channel_id=1, replica_groups=mesh['y'=4,'zl'=8,'zh'=2,'x'=4,'c'=2] {'zh','x','c'}, dimensions={0} | all-to-all | bytes 163840 | tf_op jit(solution)/shard_map/all_to_all | solution.py:33
  107.5 1.5 adapter_grads.1
  109.6 5.7 %all-to-all-start.4 = ((bf16[8,16,896]{2,1,0:T(8,128)(2,1)}), bf16[8,16,896]{2,1,0:T(8,128)(2,1)}, u32[]{:S(2)}, u32[]{:S(2)}) async-start(bf16[8,16,896]{2,1,0:T(8,128)(2,1)} %adapter_grads.1), calls=%async_computation.4 | async-start | bytes 458752 | tf_op jit(solution)/shard_map/all_to_all | solution.py:33
  115.3 1.9 %pad_maximum_fusion.refs_0_ = bf16[2,2,320,256]{3,2,1,0:T(8,128)(2,1)} fusion(bf16[1,2,320,256]{3,2,1,0:T(8,128)(2,1)} %bitcast.13, bf16[1,2,320,256]{3,2,1,0:T(8,128)(2,1)S(1)} %bitcast.24), kind=kLoop, calls=%fused_computation | loop fusion | flops 327680 | bytes 1310720 | tf_op jit(solution)/shard_map/stack | solution.py:347
  117.1 1.9 %collective-permute-start.2 = (bf16[2,2,320,256]{3,2,1,0:T(8,128)(2,1)}, bf16[2,2,320,256]{3,2,1,0:T(8,128)(2,1)}, u32[]{:S(2)}, u32[]{:S(2)}) collective-permute-start(bf16[2,2,320,256]{3,2,1,0:T(8,128)(2,1)} %pad_maximum_fusion.refs_0_), channel_id=1, source_target_pairs={{0,2},{2,4},{4,6},{6,0},{1,3},{3,5},{5,7},{7,1},{8,10},{10,12},{12... | collective-permute-start | bytes 1966088 | tf_op jit(solution)/shard_map/ppermute | solution.py:348
  119.0 4.3 %collective-permute-start.3 = (bf16[2,2,320,256]{3,2,1,0:T(8,128)(2,1)}, bf16[2,2,320,256]{3,2,1,0:T(8,128)(2,1)}, u32[]{:S(2)}, u32[]{:S(2)}) collective-permute-start(bf16[2,2,320,256]{3,2,1,0:T(8,128)(2,1)} %pad_maximum_fusion.refs_0_), channel_id=1, source_target_pairs={{0,4},{2,6},{4,0},{6,2},{1,5},{3,7},{5,1},{7,3},{8,12},{10,14},{12... | collective-permute-start | bytes 1966088 | tf_op jit(solution)/shard_map/ppermute | solution.py:348
  123.3 2.3 %collective-permute-start.4 = (bf16[2,2,320,256]{3,2,1,0:T(8,128)(2,1)}, bf16[2,2,320,256]{3,2,1,0:T(8,128)(2,1)}, u32[]{:S(2)}, u32[]{:S(2)}) collective-permute-start(bf16[2,2,320,256]{3,2,1,0:T(8,128)(2,1)} %pad_maximum_fusion.refs_0_), channel_id=1, source_target_pairs={{0,6},{2,0},{4,2},{6,4},{1,7},{3,1},{5,3},{7,5},{8,14},{10,8},{12,... | collective-permute-start | bytes 1966088 | tf_op jit(solution)/shard_map/ppermute | solution.py:348
  125.7 1.4 all-to-all-done.4
  127.1 13.0 %all_gather.13.d_all = bf16[512,896]{1,0:T(8,128)(2,1)S(1)} all-gather(bf16[128,896]{1,0:T(8,128)(2,1)} %bitcast.10), channel_id=1, replica_groups=mesh['y'=4,'zl'=8,'zh'=2,'x'=4,'c'=2] {'y'}, dimensions={0}, use_global_device_ids=true | all-gather | bytes 1146880 | tf_op jit(solution)/shard_map/all_gather | solution.py:345
  140.1 0.9 copy-done.7
  141.0 1.1 latent_grads.1
  142.7 10.5 %all-to-all-start.5 = ((bf16[16,8,128]{2,1,0:T(8,128)(2,1)}), bf16[16,8,128]{2,1,0:T(8,128)(2,1)}, u32[]{:S(2)}, u32[]{:S(2)}) async-start(bf16[16,8,128]{2,1,0:T(8,128)(2,1)} %copy-done.16), calls=%async_computation.5 | async-start | bytes 65536 | tf_op jit(solution)/shard_map/all_to_all | solution.py:33
  153.2 0.9 copy-done.15
  154.1 0.9 head_grads.1
  155.1 5.1 %base_product.1 = (f32[640,256]{1,0:T(8,128)S(1)}, f32[640,64]{1,0:T(8,128)S(1)}, bf16[640,320]{1,0:T(8,128)(2,1)S(1)}) custom-call(bf16[2,2,320,256]{3,2,1,0:T(8,128)(2,1)} %pad_maximum_fusion.refs_0_, bf16[2,2,320,256]{3,2,1,0:T(8,128)(2,1)} %collective-permute-done.2.refs_1_, bf16[2,2,320,256]{3,2,1,0:T(8,128)(2,1)} %collective-permute-done.3.refs_2_, ...), custom_call_target="tpu_custom_call" | custom-call | flops 1000000 | bytes 100000 | tf_op jit(solution)/shard_map/base_product/pallas_call | solution.py:43
  160.2 2.6 %all-gather = bf16[1280,320]{1,0:T(8,128)(2,1)S(1)} all-gather(bf16[640,320]{1,0:T(8,128)(2,1)S(1)} %get-tuple-element.56), channel_id=2, replica_groups=mesh['y'=4,'zl'=8,'zh'=2,'x'=4,'c'=2] {'c'}, dimensions={0}, use_global_device_ids=true | all-gather | bytes 1228800 | tf_op jit(solution)/shard_map/all_gather | solution.py:378
  162.9 1.1 outputs.1
  163.9 3.9 %all-to-all-done.5.got = bf16[16,8,128]{2,1,0:T(8,128)(2,1)} async-done(((bf16[16,8,128]{2,1,0:T(8,128)(2,1)}), bf16[16,8,128]{2,1,0:T(8,128)(2,1)}, u32[]{:S(2)}, u32[]{:S(2)}) %all-to-all-start.5) | async-done | bytes 32800 | tf_op jit(solution)/shard_map/all_to_all | solution.py:33
  167.9 1.6 trunk_grads.1
  (72 shorter events, 10.8 us)
Async XLA Ops:
  0.6 47.3 %collective-permute-start = (bf16[2,320,256]{2,1,0:T(8,128)(2,1)}, bf16[2,320,256]{2,1,0:T(8,128)(2,1)}, u32[]{:S(2)}, u32[]{:S(2)}) collective-permute-start(bf16[2,320,256]{2,1,0:T(8,128)(2,1)} %hidden.3), channel_id=1, source_target_pairs={{0,8},{8,0},{1,9},{9,1},{2,10},{10,2},{3,11},{11,3},{4,12},{12,4},... | collective-permute-start | bytes 983048 | tf_op jit(solution)/shard_map/ppermute | solution.py:296
  18.9 37.8 %copy-start.6 = (bf16[64,896]{1,0:T(8,128)(2,1)}, bf16[64,896]{1,0:T(8,128)(2,1)S(1)}, u32[]{:S(2)}) copy-start(bf16[64,896]{1,0:T(8,128)(2,1)S(1)} %concatenate.16.weights) | copy-start | bytes 344068
  18.9 37.8 %copy-start = (bf16[4096,256]{1,0:T(8,128)(2,1)S(1)}, bf16[4096,256]{1,0:T(8,128)(2,1)}, u32[]{:S(2)}) copy-start(bf16[4096,256]{1,0:T(8,128)(2,1)} %refs_4_.1) | copy-start | bytes 6291460
  18.9 37.8 %copy-start.2 = (bf16[4096,64]{0,1:T(8,128)(2,1)S(1)}, bf16[4096,64]{0,1:T(8,128)(2,1)}, u32[]{:S(2)}) copy-start(bf16[4096,64]{0,1:T(8,128)(2,1)} %param.24) | copy-start | bytes 1572868
  31.7 16.2 %all-to-all-start = ((s32[8,8,128]{2,1,0:T(8,128)}), s32[8,8,128]{2,1,0:T(8,128)S(1)}, u32[]{:S(2)}, u32[]{:S(2)}) async-start(s32[8,8,128]{2,1,0:T(8,128)} %broadcast_in_dim.31), calls=%async_computation | async-start | bytes 65536 | tf_op jit(solution)/shard_map/all_to_all | solution.py:33
  36.7 1.0 copy-start.3
  37.7 1.0 copy-start.11
  41.0 15.7 %copy-start.23 = (f32[16,240]{1,0:T(8,128)}, f32[16,240]{1,0:T(8,128)S(1)}, u32[]{:S(2)}) copy-start(f32[16,240]{1,0:T(8,128)S(1)} %get-tuple-element.43.sg_own) | copy-start | bytes 46084
  48.5 0.7 copy-start.8
  49.2 19.0 %all-to-all-start.1 = ((bf16[8,16,832]{2,1,0:T(8,128)(2,1)}), bf16[8,16,832]{2,1,0:T(8,128)(2,1)S(1)}, u32[]{:S(2)}, u32[]{:S(2)}) async-start(bf16[8,16,832]{2,1,0:T(8,128)(2,1)} %bitcast.28), calls=%async_computation.1 | async-start | bytes 458752 | tf_op jit(solution)/shard_map/all_to_all | solution.py:33
  56.7 4.6 %copy-start.4 = (bf16[240,1024]{1,0:T(8,128)(2,1)S(1)}, bf16[240,1024]{1,0:T(8,128)(2,1)}, u32[]{:S(2)}) copy-start(bf16[240,1024]{1,0:T(8,128)(2,1)} %task_embed.3) | copy-start | bytes 1474564
  56.8 4.6 %copy-start.20 = (bf16[2,240,64]{2,1,0:T(8,128)(2,1)S(1)}, bf16[2,240,64]{2,1,0:T(8,128)(2,1)}, u32[]{:S(2)}) copy-start(bf16[2,240,64]{2,1,0:T(8,128)(2,1)} %copy-done.19) | copy-start | bytes 184324
  56.8 4.5 %copy-start.24 = (f32[16,240]{1,0:T(8,128)S(1)}, f32[16,240]{1,0:T(8,128)}, u32[]{:S(2)}) copy-start(f32[16,240]{1,0:T(8,128)} %copy-done.23) | copy-start | bytes 46084
  56.8 11.5 %copy-start.1 = (bf16[2,320,256]{2,1,0:T(8,128)(2,1)S(1)}, bf16[2,320,256]{2,1,0:T(8,128)(2,1)}, u32[]{:S(2)}) copy-start(bf16[2,320,256]{2,1,0:T(8,128)(2,1)} %hidden.3) | copy-start | bytes 983044
  56.8 11.5 %copy-start.5 = (bf16[2,320,256]{2,1,0:T(8,128)(2,1)S(1)}, bf16[2,320,256]{2,1,0:T(8,128)(2,1)}, u32[]{:S(2)}) copy-start(bf16[2,320,256]{2,1,0:T(8,128)(2,1)} %grad_q.3) | copy-start | bytes 983044
  56.8 11.5 %copy-start.25 = (s32[2]{0:T(128)S(1)}, s32[2]{0:T(128)}, u32[]{:S(2)}) copy-start(s32[2]{0:T(128)} %lengths.3) | copy-start | bytes 28
  58.3 48.3 %copy-start.27 = (s32[2]{0:T(128)S(1)}, s32[2]{0:T(128)}, u32[]{:S(2)}) copy-start(s32[2]{0:T(128)} %ids.1) | copy-start | bytes 28
  58.3 81.8 %collective-permute-start.1 = (bf16[2048,384]{1,0:T(8,128)(2,1)}, bf16[2048,384]{1,0:T(8,128)(2,1)}, u32[]{:S(2)}, u32[]{:S(2)}) collective-permute-start(bf16[2048,384]{1,0:T(8,128)(2,1)} %partner_rows.1), channel_id=1, source_target_pairs={{0,1},{1,0},{2,3},{3,2},{4,5},{5,4},{6,7},{7,6},{8,9},{9,8},{10,11... | collective-permute-start | bytes 4718600 | tf_op jit(solution)/shard_map/ppermute | solution.py:334
  62.1 0.7 copy-start.14
  68.3 0.9 copy-start.12
  70.0 47.1 %copy-start.21 = (bf16[16,832]{1,0:T(8,128)(2,1)}, bf16[16,832]{1,0:T(8,128)(2,1)S(1)}, u32[]{:S(2)}) copy-start(bf16[16,832]{1,0:T(8,128)(2,1)S(1)} %get-tuple-element.57.ad) | copy-start | bytes 79876
  106.6 0.9 copy-start.13
  109.6 17.5 %all-to-all-start.4 = ((bf16[8,16,896]{2,1,0:T(8,128)(2,1)}), bf16[8,16,896]{2,1,0:T(8,128)(2,1)}, u32[]{:S(2)}, u32[]{:S(2)}) async-start(bf16[8,16,896]{2,1,0:T(8,128)(2,1)} %adapter_grads.1), calls=%async_computation.4 | async-start | bytes 458752 | tf_op jit(solution)/shard_map/all_to_all | solution.py:33
  117.1 38.0 %collective-permute-start.2 = (bf16[2,2,320,256]{3,2,1,0:T(8,128)(2,1)}, bf16[2,2,320,256]{3,2,1,0:T(8,128)(2,1)}, u32[]{:S(2)}, u32[]{:S(2)}) collective-permute-start(bf16[2,2,320,256]{3,2,1,0:T(8,128)(2,1)} %pad_maximum_fusion.refs_0_), channel_id=1, source_target_pairs={{0,2},{2,4},{4,6},{6,0},{1,3},{3,5},{5,7},{7,1},{8,10},{10,12},{12... | collective-permute-start | bytes 1966088 | tf_op jit(solution)/shard_map/ppermute | solution.py:348
  119.0 36.1 %collective-permute-start.3 = (bf16[2,2,320,256]{3,2,1,0:T(8,128)(2,1)}, bf16[2,2,320,256]{3,2,1,0:T(8,128)(2,1)}, u32[]{:S(2)}, u32[]{:S(2)}) collective-permute-start(bf16[2,2,320,256]{3,2,1,0:T(8,128)(2,1)} %pad_maximum_fusion.refs_0_), channel_id=1, source_target_pairs={{0,4},{2,6},{4,0},{6,2},{1,5},{3,7},{5,1},{7,3},{8,12},{10,14},{12... | collective-permute-start | bytes 1966088 | tf_op jit(solution)/shard_map/ppermute | solution.py:348
  123.3 31.8 %collective-permute-start.4 = (bf16[2,2,320,256]{3,2,1,0:T(8,128)(2,1)}, bf16[2,2,320,256]{3,2,1,0:T(8,128)(2,1)}, u32[]{:S(2)}, u32[]{:S(2)}) collective-permute-start(bf16[2,2,320,256]{3,2,1,0:T(8,128)(2,1)} %pad_maximum_fusion.refs_0_), channel_id=1, source_target_pairs={{0,6},{2,0},{4,2},{6,4},{1,7},{3,1},{5,3},{7,5},{8,14},{10,8},{12,... | collective-permute-start | bytes 1966088 | tf_op jit(solution)/shard_map/ppermute | solution.py:348
  140.1 0.9 copy-start.7
  142.7 25.2 %all-to-all-start.5 = ((bf16[16,8,128]{2,1,0:T(8,128)(2,1)}), bf16[16,8,128]{2,1,0:T(8,128)(2,1)}, u32[]{:S(2)}, u32[]{:S(2)}) async-start(bf16[16,8,128]{2,1,0:T(8,128)(2,1)} %copy-done.16), calls=%async_computation.5 | async-start | bytes 65536 | tf_op jit(solution)/shard_map/all_to_all | solution.py:33
  153.2 0.9 copy-start.15
  155.1 7.8 %copy-start.10 = (bf16[16,8,320]{2,1,0:T(8,128)(2,1)S(1)}, bf16[16,8,320]{2,1,0:T(8,128)(2,1)}, u32[]{:S(2)}) copy-start(bf16[16,8,320]{2,1,0:T(8,128)(2,1)} %copy-done.9) | copy-start | bytes 245764
  155.1 7.8 %copy-start.22 = (bf16[16,832]{1,0:T(8,128)(2,1)S(1)}, bf16[16,832]{1,0:T(8,128)(2,1)}, u32[]{:S(2)}) copy-start(bf16[16,832]{1,0:T(8,128)(2,1)} %copy-done.21) | copy-start | bytes 79876
  160.2 7.7 %copy-start.18 = (bf16[64,1024]{1,0:T(8,128)(2,1)S(1)}, bf16[64,1024]{1,0:T(8,128)(2,1)}, u32[]{:S(2)}) copy-start(bf16[64,1024]{1,0:T(8,128)(2,1)} %copy-done.17) | copy-start | bytes 393220
  (5 other events, 3.3 us)
